TPU v7x, 256 devices: a whole 4x4x8 slice. The times are simulated.
256 devices in a mesh: dp: 64 (over x, z_lo, y, core), tensor: 4 (over z_hi).
Axes of the slice: x: 4, y: 4, z: 8 (z_hi: 4, z_lo: 2; z = z_hi * 2 + z_lo), core: 2. Of those that a mesh axis runs over, the one named last changes fastest.
Arguments:
- picture_embeds: bfloat16 [131072, 1152], P('dp', 'tensor'), may hold values from -6 to 6
- caption_embeds: bfloat16 [131072, 1152], P(('dp', 'tensor')), may hold values from -6 to 6
- starting_caption_slab: int32 [], replicated, may hold values from 0 to 63
- score_multiplier: float32 [], replicated, may hold values from 5 to 20
- score_offset: float32 [], replicated, may hold values from -4 to -2
Outputs:
- image_grad: bfloat16 [131072, 1152], P('dp', 'tensor')
- text_grad: float32 [2, 4, 512, 1152], P(None, 'tensor', 'dp')
All inputs are finite; a program needn't handle non-finite values.
Results may differ from a plain program's by a relative error of at most 0.0058.
Values may be sent and summed in bfloat16 or wider, within the bound.
No kernel may reach another device: no remote copies, remote signals or barrier semaphores. Data moves between devices by JAX's collectives and lax.ppermute only.
A program may use at most 64 MiB of HBM per device.

v0:
```python
import jax
import jax.numpy as jnp
from jax import lax
from jax.sharding import PartitionSpec as P

STEPS = 2


epsilon = 1e-06


def from_root(shard, axis, root):
    mine = lax.axis_index(axis) == root
    return lax.psum(jnp.where(mine, shard, jnp.zeros_like(shard)), axis)


def unit_rows(values):
    widened = values.astype(jnp.float32)
    return widened * lax.rsqrt(jnp.sum(widened * widened, axis=-1, keepdims=True) + epsilon)


def per_device(
    picture_embeds, caption_embeds, starting_caption_slab, score_multiplier, score_offset
):
    row_layout = lax.all_to_all(picture_embeds, "tensor", split_axis=0, concat_axis=1, tiled=True)
    images = unit_rows(row_layout).astype(jnp.bfloat16)
    captions = unit_rows(caption_embeds).astype(jnp.bfloat16)
    dp_place = lax.axis_index("dp")
    dp_count = lax.axis_size("dp")
    row_count = images.shape[0]
    identity = jnp.eye(row_count, dtype=jnp.float32)
    image_sum = jnp.zeros(images.shape, jnp.float32)
    partials = []
    for step_index in range(STEPS):
        holder_index = (starting_caption_slab + step_index) % dp_count
        present_caption_slab = from_root(captions, "dp", holder_index)
        similarity_scores = (
            score_multiplier
            * lax.dot_general(
                images,
                present_caption_slab,
                (((1,), (1,)), ((), ())),
                preferred_element_type=jnp.float32,
            )
            + score_offset
        )
        matching_labels = (
            jnp.where(dp_place == holder_index, 1.0, 0.0).astype(jnp.float32) * identity
        )
        parameters_halfwidth = (
            (jax.nn.sigmoid(similarity_scores) - matching_labels) * score_multiplier
        ).astype(jnp.bfloat16)
        image_sum = image_sum + jnp.dot(
            parameters_halfwidth, present_caption_slab, preferred_element_type=jnp.float32
        )
        text_part = lax.dot_general(
            parameters_halfwidth,
            images,
            (((0,), (0,)), ((), ())),
            preferred_element_type=jnp.float32,
        )
        partials.append(
            lax.psum_scatter(text_part[None, None], "dp", scatter_dimension=2, tiled=True)
        )
    text_grad = jnp.concatenate(partials, axis=0)
    image_grad = lax.all_to_all(
        image_sum.astype(jnp.bfloat16), "tensor", split_axis=1, concat_axis=0, tiled=True
    )
    return (image_grad, text_grad)


def solution(mesh):
    placed = (P("dp", "tensor"), P(("dp", "tensor"), None), P(), P(), P())
    return jax.shard_map(
        per_device,
        mesh=mesh,
        in_specs=placed,
        out_specs=(P("dp", "tensor"), P(None, "tensor", "dp", None)),
        check_vma=False,
    )
```

profile of v0, /device:TPU:1, one launch (start us, length us, event | category | flops | bytes accessed | tf_op | source)
XLA Modules:
  0.0 1162.1 jit_solution(13843225290107438485)
XLA Ops:
  7.2 2.4 copy.22
  9.6 9.1 all-to-all-start
  19.4 0.3 fusion.1
  19.7 1.9 broadcast_select_fusion
  21.6 0.0 all-reduce.7.cloned.1.call-start
  23.0 21.6 %all-to-all-done = bf16[4,512,288]{1,2,0:T(8,128)(2,1)S(1)} async-done(((bf16[4,512,288]{1,2,0:T(8,128)(2,1)}), bf16[4,512,288]{1,2,0:T(8,128)(2,1)S(1)}, u32[]{:S(2)}, u32[]{:S(2)}) %all-to-all-start) | async-done | bytes 1179680 | tf_op jit(solution)/shard_map/all_to_all | solution.py:25
  44.6 0.3 multiply_reduce_fusion
  44.9 0.2 fusion.3
  45.1 531.2 %all-reduce.9.cloned.1.call-done = (bf16[512,1152]{1,0:T(8,128)(2,1)}, bf16[512,1152]{1,0:T(8,128)(2,1)}) async-done(((bf16[512,1152]{1,0:T(8,128)(2,1)}, bf16[512,1152]{1,0:T(8,128)(2,1)}), (bf16[512,1152]{1,0:T(8,128)(2,1)}, bf16[512,1152]{1,0:T(8,128)(2,1)})) %all-reduce.9.cloned.1.call-update) | async-done | bytes 2359312 | tf_op jit(solution)/shard_map/psum | solution.py:14
  576.3 2.3 fusion.19
  578.6 2.3 convolution_bitcast_fusion
  580.9 1.1 fusion.18
  582.0 2.4 convolution_bitcast_fusion.1
  584.4 0.8 fusion.20
  585.2 0.4 copy-done.1
  585.7 0.9 fusion
  586.5 1.4 copy.13
  588.0 6.0 all-to-all-start.1
  593.9 0.6 dynamic-slice
  595.2 14.2 %all-to-all-done.1 = bf16[512,4,288]{0,2,1:T(8,128)(2,1)S(1)} async-done(((bf16[512,4,288]{0,2,1:T(8,128)(2,1)}), bf16[512,4,288]{0,2,1:T(8,128)(2,1)S(1)}, u32[]{:S(2)}, u32[]{:S(2)}) %all-to-all-start.1) | async-done | bytes 1179680 | tf_op jit(solution)/shard_map/all_to_all | solution.py:66
  609.4 1.2 copy.20
  610.6 543.2 %all-reduce.7.cloned.1.call-done = (f32[1,1,512,1152]{3,2,1,0:T(8,128)}, f32[1,1,512,1152]{3,2,1,0:T(8,128)}) async-done(((f32[1,1,512,1152]{3,2,1,0:T(8,128)}, f32[1,1,512,1152]{3,2,1,0:T(8,128)}), (f32[1,1,512,1152]{3,2,1,0:T(8,128)}, f32[1,1,512,1152]{3,2,1,0:T(8,128)})) %all-reduce.7.cloned.1.call-update) | async-done | bytes 4718608
  1153.8 0.8 constant_dynamic-slice_fusion
  1154.6 0.6 pad_maximum_fusion
  (12 shorter events, 0.1 us)
Async XLA Ops:
  9.6 9.8 copy-start
  9.6 35.0 %all-to-all-start = ((bf16[4,512,288]{1,2,0:T(8,128)(2,1)}), bf16[4,512,288]{1,2,0:T(8,128)(2,1)S(1)}, u32[]{:S(2)}, u32[]{:S(2)}) async-start(bf16[4,512,288]{1,2,0:T(8,128)(2,1)} %bitcast.34), calls=%async_computation | async-start | bytes 2359296 | tf_op jit(solution)/shard_map/all_to_all | solution.py:25
  18.7 557.6 %all-reduce.9.cloned.1.call-start = ((), (), s32[]{:S(2)}) async-start(), calls=%async_computation.3 | async-start | bytes 4718592 | tf_op jit(solution)/shard_map/psum | solution.py:14
  21.6 1132.2 %all-reduce.7.cloned.1.call-start = ((), (), s32[]{:S(2)}) async-start(), calls=%async_computation.2 | async-start | bytes 9437184
  578.6 2.3 copy-start.2
  584.4 1.3 copy-start.1
  588.0 6.0 copy-start.3
  588.0 21.4 %all-to-all-start.1 = ((bf16[512,4,288]{0,2,1:T(8,128)(2,1)}), bf16[512,4,288]{0,2,1:T(8,128)(2,1)S(1)}, u32[]{:S(2)}, u32[]{:S(2)}) async-start(bf16[512,4,288]{0,2,1:T(8,128)(2,1)} %bitcast.2), calls=%async_computation.1 | async-start | bytes 2359296 | tf_op jit(solution)/shard_map/all_to_all | solution.py:66
Sparse Core Ops, SparseCore 0:
  22.2 554.0 all-reduce.8
  584.5 569.2 all-reduce.6
where the time goes:
time: 1160 us
  waiting for transfers between devices  1110 us (96%)
  between operations  16.8 us (1%)
  starting transfers between devices  15.2 us (1%)
    unnamed x3, waiting for transfers between devices  543 us
    psum x1, waiting for transfers between devices, from_root(): return lax.psum(jnp.where(mine, shard, jnp.zeros_like(shard)), axis)  531 us
  transfers between devices with their start and end apart: 4, of which 4 were waited for; matrix products, arithmetic and copies ran while one was open for 1% of the time, Pallas kernels for 0%

commit v1 on v0

v1 whole, which is shorter than its diff:
```python
import jax
import jax.numpy as jnp
from jax import lax
from jax.sharding import Mesh
from jax.sharding import PartitionSpec as P

EPSILON = 1e-06
SIZES = (("x", 4), ("zl", 2), ("y", 4), ("c", 2), ("t", 4))
DP = ("x", "zl", "y", "c")


def shift(value, axis, by, size):
    return lax.ppermute(value, axis, [(i, (i + by) % size) for i in range(size)])


def unit(values, axis):
    widened = values.astype(jnp.float32)
    total = jnp.sum(widened * widened, axis=axis, keepdims=True)
    return (widened * lax.rsqrt(total + EPSILON)).astype(jnp.bfloat16)


def pick(parts, index):
    return lax.dynamic_index_in_dim(parts, index, 0, keepdims=False)


def exchange_width(parts):
    mine = lax.axis_index("t")
    got = [pick(parts, mine)]
    for by in (3, 2, 1):
        got.append(shift(pick(parts, (mine + by) % 4), "t", by, 4))
    ring = jnp.concatenate(got + got)
    start = (4 - mine) % 4
    size = parts.shape[1]
    return lax.dynamic_slice_in_dim(ring, start * size, 4 * size, 0)


def across(parts):
    return lax.all_to_all(parts, ("x", "y"), split_axis=0, concat_axis=0, tiled=True)


def per_device(pictures, captions, start, multiplier, offset):
    f32, bf16 = jnp.float32, jnp.bfloat16
    width = captions.shape[1]
    core, z_lo = lax.axis_index("c"), lax.axis_index("zl")
    place = lax.axis_index(DP)

    step_of = (start ^ core) & 1
    holders = [(start + step_of) % 64, (start + (1 - step_of)) % 64]
    chip = holders[0] >> 1
    root_y, root_z, root_x = chip & 3, (chip >> 2) & 1, chip >> 3

    text = captions.reshape(4, 2, 4, 16, width).transpose(0, 2, 1, 3, 4).reshape(16, 32, width)
    wide = pictures.reshape(4, 512, 288).transpose(0, 2, 1)
    images = unit(exchange_width(wide), 0)

    piece = pick(across(text), root_x * 4 + root_y)
    other = shift(piece, "zl", 1, 2)
    piece = unit(jnp.where(z_lo == root_z, piece, other), 1)
    own = across(jnp.broadcast_to(piece[None], (16, 32, width))).reshape(512, width)
    slabs = [own, shift(own, "c", 1, 2)]

    place_of = jnp.arange(512, dtype=jnp.int32)
    row = ((((place_of >> 7) * 2 + ((place_of >> 4) & 1)) * 4 + ((place_of >> 5) & 3)) << 4) + (place_of & 15)
    same = row[:, None] == jnp.arange(512, dtype=jnp.int32)[None, :]

    grad, terms = 0.0, []
    for slab, holder in zip(slabs, holders):
        logits = multiplier * jnp.dot(slab, images, preferred_element_type=f32) + offset
        positive = (same & (place == holder)).astype(f32)
        weights = ((jax.nn.sigmoid(logits) - positive) * multiplier).astype(bf16)
        grad = grad + lax.dot_general(slab, weights, (((0,), (0,)), ((), ())), preferred_element_type=f32)
        terms.append(lax.dot_general(weights, images, (((1,), (1,)), ((), ())), preferred_element_type=f32))

    back = exchange_width(grad.astype(bf16).reshape(4, 288, 512)).reshape(4, 288, 512)
    image_grad = back.transpose(0, 2, 1).reshape(2048, 288)

    total = terms[0] + shift(terms[1].astype(bf16), "c", 1, 2).astype(f32)
    total = jnp.sum(across(total.astype(bf16).reshape(16, 32, width)).astype(f32), axis=0)
    total = total.reshape(2, 16, width)
    total = pick(total, z_lo) + shift(pick(total, 1 - z_lo), "zl", 1, 2)
    total = total.reshape(2, 8, width)
    mine, theirs = pick(total, core), shift(pick(total, 1 - core), "c", 1, 2)
    first = step_of == 0
    text_grad = jnp.stack([jnp.where(first, mine, theirs), jnp.where(first, theirs, mine)])
    return image_grad, text_grad[:, None]


def solution(mesh):
    names, sizes = zip(*SIZES)
    grid = Mesh(mesh.devices.reshape(sizes), names)
    return jax.shard_map(
        per_device,
        mesh=grid,
        in_specs=(P(DP, "t"), P(names, None), P(), P(), P()),
        out_specs=(P(DP, "t"), P(None, "t", DP, None)),
        check_vma=False,
    )
```

time: 1160 us -> 143 us (0.12)
  waiting for transfers between devices: 1110 us -> 43.5 us
  starting transfers between devices: 15.2 us -> 59.3 us
  local copies, waits for them, and re-layouts: 6.79 us -> 23.8 us
  between operations: 16.8 us -> 2.99 us
    unnamed x3 -> x0, waiting for transfers between devices: 543 us -> none
    psum x1 -> x0, waiting for transfers between devices: 531 us -> none  [from_root(): return lax.psum(jnp.where(mine, shard, jnp.zeros_like(shard)), axis)]
    ppermute x0 -> x11, starting transfers between devices: none -> 40.9 us  [shift(): lax.ppermute(value, axis, [(i, (i + by) % size) for i in range(size)])]
    ppermute x0 -> x11, waiting for transfers between devices: none -> 27.5 us  [shift(): lax.ppermute(value, axis, [(i, (i + by) % size) for i in range(size)])]
    all_to_all x2 -> x3, waiting for transfers between devices: 35.8 us -> 16 us  [across(): lax.all_to_all(parts, ('x', 'y'), split_axis=0, concat_axis=0, tiled=True)]
  transfers between devices with their start and end apart: 4 -> 14, of which waited for: 4 -> 8; matrix products, arithmetic and copies ran while one was open for 1% -> 16% of each run, Pallas kernels for 0% -> 0%
where the time goes in v1:
time: 143 us
  starting transfers between devices  59.3 us (41%)
  waiting for transfers between devices  43.5 us (30%)
  local copies, waits for them, and re-layouts  23.8 us (17%)
  matrix products  10.5 us (7%)
  between operations  2.99 us (2%)
  other arithmetic  2.65 us (2%)
    ppermute x11, starting transfers between devices, shift(): lax.ppermute(value, axis, [(i, (i + by) % size) for i in range(size)])  40.9 us
    ppermute x11, waiting for transfers between devices, shift(): lax.ppermute(value, axis, [(i, (i + by) % size) for i in range(size)])  27.5 us
    all_to_all x3, starting transfers between devices, across(): lax.all_to_all(parts, ('x', 'y'), split_axis=0, concat_axis=0, tiled=True)  18.4 us
    all_to_all x3, waiting for transfers between devices, across(): lax.all_to_all(parts, ('x', 'y'), split_axis=0, concat_axis=0, tiled=True)  16 us
    unnamed x29, local copies, waits for them, and re-layouts  12.1 us
    dot_general x2, matrix products, per_device(): lax.dot_general(weights, images, (((1,), (1,)), ((), ())), preferred_elem...  5.18 us
    dot_general x2, matrix products, per_device(): jnp.dot(slab, images, preferred_element_type=f32)  3.68 us
  transfers between devices with their start and end apart: 14, of which 8 were waited for; matrix products, arithmetic and copies ran while one was open for 16% of the time, Pallas kernels for 0%

profile of v1, /device:TPU:1, one launch (start us, length us, event | category | flops | bytes accessed | tf_op | source)
XLA Modules:
  0.0 142.7 jit_solution(1090363253564438095)
XLA Ops:
  0.6 2.4 %copy.19 = bf16[4,4,2,16,1152]{4,3,2,1,0:T(8,128)(2,1)} copy(bf16[4,4,2,16,1152]{4,3,1,2,0:T(8,128)(2,1)} %bitcast.88) | data formatting | bytes 2359296 | tf_op jit(solution)/shard_map/transpose | solution.py:52
  3.0 7.6 %all-to-all-start = ((bf16[16,32,1152]{2,1,0:T(8,128)(2,1)}), bf16[16,32,1152]{2,1,0:T(8,128)(2,1)S(1)}, u32[]{:S(2)}, u32[]{:S(2)}) async-start(bf16[16,32,1152]{2,1,0:T(8,128)(2,1)} %bitcast.2), calls=%async_computation | async-start | bytes 2359296 | tf_op jit(solution)/shard_map/all_to_all | solution.py:38
  11.4 16.0 %all-to-all-done = bf16[16,32,1152]{2,1,0:T(8,128)(2,1)S(1)} async-done(((bf16[16,32,1152]{2,1,0:T(8,128)(2,1)}), bf16[16,32,1152]{2,1,0:T(8,128)(2,1)S(1)}, u32[]{:S(2)}, u32[]{:S(2)}) %all-to-all-start) | async-done | bytes 1179680 | tf_op jit(solution)/shard_map/all_to_all | solution.py:38
  29.1 1.7 %collective-permute-done = bf16[32,1152]{1,0:T(8,128)(2,1)S(1)} collective-permute-done((bf16[32,1152]{1,0:T(8,128)(2,1)S(1)}, bf16[32,1152]{1,0:T(8,128)(2,1)S(1)}, u32[]{:S(2)}, u32[]{:S(2)}) %collective-permute-start) | collective-permute-done | bytes 73760 | tf_op jit(solution)/shard_map/ppermute | solution.py:13
  32.1 4.2 %all-to-all-start.1 = ((bf16[16,32,1152]{2,1,0:T(8,128)(2,1)}), bf16[16,32,1152]{2,1,0:T(8,128)(2,1)S(1)}, u32[]{:S(2)}, u32[]{:S(2)}) async-start(bf16[16,32,1152]{2,1,0:T(8,128)(2,1)} %broadcast_in_dim.4), calls=%async_computation.1 | async-start | bytes 2359296 | tf_op jit(solution)/shard_map/all_to_all | solution.py:38
  37.3 2.4 %dynamic-slice_bitcast_fusion = (bf16[1,288,512]{2,0,1:T(2,128)(2,1)S(1)}, bf16[1,288,512]{2,0,1:T(2,128)(2,1)S(1)}, bf16[1,288,512]{2,0,1:T(2,128)(2,1)S(1)}, bf16[1,288,512]{2,0,1:T(2,128)(2,1)S(1)}) fusion(bf16[4,512,288]{1,0,2:T(4,128)(2,1)S(1)} %reshape.68, s32[]{:T(128)S(6)} %select_n.104, s32[]{:T(128)S(6)} %select_n.102, s32[]{:T(128)S(6)} %select_n.100, ...), kind=kLoop, calls=%fused_computation.30 | loop fusion | bytes 2359312 | tf_op jit(solution)/shard_map/jit(dynamic_index_in_dim)/dynamic_slice | solution.py:23
  39.8 5.9 %collective-permute-start.1 = (bf16[288,512]{1,0:T(8,128)(2,1)S(1)}, bf16[288,512]{1,0:T(8,128)(2,1)S(1)}, u32[]{:S(2)}, u32[]{:S(2)}) collective-permute-start(bf16[288,512]{1,0:T(8,128)(2,1)S(1)} %bitcast.92), channel_id=1, source_target_pairs={{0,3},{1,0},{2,1},{3,2},{4,7},{5,4},{6,5},{7,6},{8,11},{9,8},{10,9... | collective-permute-start | bytes 884744 | tf_op jit(solution)/shard_map/ppermute | solution.py:13
  46.8 2.4 %collective-permute-start.3 = (bf16[288,512]{1,0:T(8,128)(2,1)S(1)}, bf16[288,512]{1,0:T(8,128)(2,1)S(1)}, u32[]{:S(2)}, u32[]{:S(2)}) collective-permute-start(bf16[288,512]{1,0:T(8,128)(2,1)S(1)} %bitcast.94), channel_id=1, source_target_pairs={{0,1},{1,2},{2,3},{3,0},{4,5},{5,6},{6,7},{7,4},{8,9},{9,10},{10,1... | collective-permute-start | bytes 884744 | tf_op jit(solution)/shard_map/ppermute | solution.py:13
  51.3 5.0 %collective-permute-start.4 = (bf16[512,1152]{1,0:T(8,128)(2,1)S(1)}, bf16[512,1152]{1,0:T(8,128)(2,1)S(1)}, u32[]{:S(2)}, u32[]{:S(2)}) collective-permute-start(bf16[512,1152]{1,0:T(8,128)(2,1)S(1)} %bitcast.81), channel_id=1, source_target_pairs={{0,4},{4,0},{1,5},{5,1},{2,6},{6,2},{3,7},{7,3},{8,12},{12,8},{9,1... | collective-permute-start | bytes 3538952 | tf_op jit(solution)/shard_map/ppermute | solution.py:13
  57.1 4.5 %collective-permute-done.2 = bf16[288,512]{1,0:T(8,128)(2,1)S(1)} collective-permute-done((bf16[288,512]{1,0:T(8,128)(2,1)S(1)}, bf16[288,512]{1,0:T(8,128)(2,1)S(1)}, u32[]{:S(2)}, u32[]{:S(2)}) %collective-permute-start.2) | collective-permute-done | bytes 294944 | tf_op jit(solution)/shard_map/ppermute | solution.py:13
  62.3 4.7 %collective-permute-done.3 = bf16[288,512]{1,0:T(8,128)(2,1)S(1)} collective-permute-done((bf16[288,512]{1,0:T(8,128)(2,1)S(1)}, bf16[288,512]{1,0:T(8,128)(2,1)S(1)}, u32[]{:S(2)}, u32[]{:S(2)}) %collective-permute-start.3) | collective-permute-done | bytes 294944 | tf_op jit(solution)/shard_map/ppermute | solution.py:13
  73.3 2.5 %fusion.18 = bf16[512,512]{1,0:T(8,128)(2,1)S(1)} fusion(bf16[512,1152]{1,0:T(8,128)(2,1)S(1)} %collective-permute-done.4, s32[512]{0:T(512)S(1)} %fusion.42, f32[]{:T(128)S(6)} %copy.50, f32[]{:T(128)S(6)} %copy.49, pred[]{:T(512)S(6)} %eq.47, f32[512]{0:T(512)S(1)} %add_rsqrt_fusion, bf16[2304,512]{1,0:T(8,128)(2,1)} %constant_dynamic-update-slice_fusion, ...), kind=kOutput, calls=%fused_computation.26 | convolution fusion | flops 608632832 | bytes 2887693 | tf_op jit(solution)/shard_map/dot_general | solution.py:68
  75.9 2.0 %convolution_convert_fusion = bf16[512,1152]{1,0:T(8,128)(2,1)} fusion(bf16[512,512]{1,0:T(8,128)(2,1)S(1)} %fusion.18, f32[512]{0:T(512)S(1)} %add_rsqrt_fusion, bf16[2304,512]{1,0:T(8,128)(2,1)S(1)} %copy-done.3, s32[]{:T(128)S(6)} %select_n.106), kind=kOutput, calls=%fused_computation.2 | convolution fusion | flops 606339072 | bytes 2885636 | tf_op jit(solution)/shard_map/dot_general | solution.py:72
  77.9 6.4 %collective-permute-start.8 = (bf16[512,1152]{1,0:T(8,128)(2,1)}, bf16[512,1152]{1,0:T(8,128)(2,1)}, u32[]{:S(2)}, u32[]{:S(2)}) collective-permute-start(bf16[512,1152]{1,0:T(8,128)(2,1)} %convolution_convert_fusion), channel_id=1, source_target_pairs={{0,4},{4,0},{1,5},{5,1},{2,6},{6,2},{3,7},{7,3},{8,12},{12,8},{9,1... | collective-permute-start | bytes 3538952 | tf_op jit(solution)/shard_map/ppermute | solution.py:13
  87.7 3.2 %add_convert_fusion = bf16[512,1152]{1,0:T(8,128)(2,1)} fusion(bf16[512,1152]{1,0:T(8,128)(2,1)} %collective-permute-done.8, bf16[512,512]{1,0:T(8,128)(2,1)S(1)} %fusion.17, f32[512]{0:T(512)S(1)} %add_rsqrt_fusion, bf16[2304,512]{1,0:T(8,128)(2,1)S(1)} %copy-done.3, s32[]{:T(128)S(6)} %select_n.106), kind=kOutput, calls=%fused_computation.8 | convolution fusion | flops 607518720 | bytes 4065284 | tf_op jit(solution)/shard_map/dot_general | solution.py:72
  90.9 6.6 %all-to-all-start.2 = ((bf16[16,32,1152]{2,1,0:T(8,128)(2,1)}), bf16[16,32,1152]{2,1,0:T(8,128)(2,1)S(1)}, u32[]{:S(2)}, u32[]{:S(2)}) async-start(bf16[16,32,1152]{2,1,0:T(8,128)(2,1)} %bitcast.16), calls=%async_computation.2 | async-start | bytes 2359296 | tf_op jit(solution)/shard_map/all_to_all | solution.py:38
  98.4 4.3 %collective-permute-start.5 = (bf16[288,512]{1,0:T(8,128)(2,1)}, bf16[288,512]{1,0:T(8,128)(2,1)S(1)}, u32[]{:S(2)}, u32[]{:S(2)}) collective-permute-start(bf16[288,512]{1,0:T(8,128)(2,1)} %get-tuple-element.4), channel_id=1, source_target_pairs={{0,3},{1,0},{2,1},{3,2},{4,7},{5,4},{6,5},{7,6},{8,11},{9,8},{10,9... | collective-permute-start | bytes 884744 | tf_op jit(solution)/shard_map/ppermute | solution.py:13
  102.7 1.7 %collective-permute-start.6 = (bf16[288,512]{1,0:T(8,128)(2,1)}, bf16[288,512]{1,0:T(8,128)(2,1)S(1)}, u32[]{:S(2)}, u32[]{:S(2)}) collective-permute-start(bf16[288,512]{1,0:T(8,128)(2,1)} %get-tuple-element.3), channel_id=1, source_target_pairs={{0,2},{1,3},{2,0},{3,1},{4,6},{5,7},{6,4},{7,5},{8,10},{9,11},{10,... | collective-permute-start | bytes 884744 | tf_op jit(solution)/shard_map/ppermute | solution.py:13
  104.3 2.4 %collective-permute-start.7 = (bf16[288,512]{1,0:T(8,128)(2,1)S(1)}, bf16[288,512]{1,0:T(8,128)(2,1)S(1)}, u32[]{:S(2)}, u32[]{:S(2)}) collective-permute-start(bf16[288,512]{1,0:T(8,128)(2,1)S(1)} %get-tuple-element.2), channel_id=1, source_target_pairs={{0,1},{1,2},{2,3},{3,0},{4,5},{5,6},{6,7},{7,4},{8,9},{9,10},{10,1... | collective-permute-start | bytes 884744 | tf_op jit(solution)/shard_map/ppermute | solution.py:13
  107.4 4.1 %collective-permute-done.5 = bf16[288,512]{1,0:T(8,128)(2,1)S(1)} collective-permute-done((bf16[288,512]{1,0:T(8,128)(2,1)}, bf16[288,512]{1,0:T(8,128)(2,1)S(1)}, u32[]{:S(2)}, u32[]{:S(2)}) %collective-permute-start.5) | collective-permute-done | bytes 294944 | tf_op jit(solution)/shard_map/ppermute | solution.py:13
  112.3 8.4 %collective-permute-done.6 = bf16[288,512]{1,0:T(8,128)(2,1)S(1)} collective-permute-done((bf16[288,512]{1,0:T(8,128)(2,1)}, bf16[288,512]{1,0:T(8,128)(2,1)S(1)}, u32[]{:S(2)}, u32[]{:S(2)}) %collective-permute-start.6) | collective-permute-done | bytes 294944 | tf_op jit(solution)/shard_map/ppermute | solution.py:13
  121.4 3.0 %collective-permute-done.7 = bf16[288,512]{1,0:T(8,128)(2,1)S(1)} collective-permute-done((bf16[288,512]{1,0:T(8,128)(2,1)S(1)}, bf16[288,512]{1,0:T(8,128)(2,1)S(1)}, u32[]{:S(2)}, u32[]{:S(2)}) %collective-permute-start.7) | collective-permute-done | bytes 294944 | tf_op jit(solution)/shard_map/ppermute | solution.py:13
  127.6 8.1 %collective-permute-start.9 = (f32[16,1152]{1,0:T(8,128)S(1)}, f32[16,1152]{1,0:T(8,128)S(1)}, u32[]{:S(2)}, u32[]{:S(2)}) collective-permute-start(f32[16,1152]{1,0:T(8,128)S(1)} %dynamic-slice_bitcast_fusion.7), channel_id=1, source_target_pairs={{0,32},{32,0},{1,33},{33,1},{2,34},{34,2},{3,35},{35,3},{4,36},{36... | collective-permute-start | bytes 221192 | tf_op jit(solution)/shard_map/ppermute | solution.py:13
  137.5 2.0 %collective-permute-start.10 = (f32[8,1152]{1,0:T(8,128)S(1)}, f32[8,1152]{1,0:T(8,128)S(1)}, u32[]{:S(2)}, u32[]{:S(2)}) collective-permute-start(f32[8,1152]{1,0:T(8,128)S(1)} %dynamic-slice_bitcast_fusion.9), channel_id=1, source_target_pairs={{0,4},{4,0},{1,5},{5,1},{2,6},{6,2},{3,7},{7,3},{8,12},{12,8},{9,1... | collective-permute-start | bytes 110600 | tf_op jit(solution)/shard_map/ppermute | solution.py:13
  (61 shorter events, 28.1 us)
Async XLA Ops:
  3.0 24.4 %all-to-all-start = ((bf16[16,32,1152]{2,1,0:T(8,128)(2,1)}), bf16[16,32,1152]{2,1,0:T(8,128)(2,1)S(1)}, u32[]{:S(2)}, u32[]{:S(2)}) async-start(bf16[16,32,1152]{2,1,0:T(8,128)(2,1)} %bitcast.2), calls=%async_computation | async-start | bytes 2359296 | tf_op jit(solution)/shard_map/all_to_all | solution.py:38
  10.6 25.8 %copy-start.2 = (bf16[2048,288]{0,1:T(8,128)(2,1)S(1)}, bf16[2048,288]{0,1:T(8,128)(2,1)}, u32[]{:S(2)}) copy-start(bf16[2048,288]{0,1:T(8,128)(2,1)} %param.5) | copy-start | bytes 3538948
  27.4 3.4 %collective-permute-start = (bf16[32,1152]{1,0:T(8,128)(2,1)S(1)}, bf16[32,1152]{1,0:T(8,128)(2,1)S(1)}, u32[]{:S(2)}, u32[]{:S(2)}) collective-permute-start(bf16[32,1152]{1,0:T(8,128)(2,1)S(1)} %dynamic-slice_bitcast_fusion.8), channel_id=1, source_target_pairs={{0,32},{32,0},{1,33},{33,1},{2,34},{34,2},{3,35},{35,3},{4,36},{36... | collective-permute-start | bytes 221192 | tf_op jit(solution)/shard_map/ppermute | solution.py:13
  32.1 19.2 %all-to-all-start.1 = ((bf16[16,32,1152]{2,1,0:T(8,128)(2,1)}), bf16[16,32,1152]{2,1,0:T(8,128)(2,1)S(1)}, u32[]{:S(2)}, u32[]{:S(2)}) async-start(bf16[16,32,1152]{2,1,0:T(8,128)(2,1)} %broadcast_in_dim.4), calls=%async_computation.1 | async-start | bytes 2359296 | tf_op jit(solution)/shard_map/all_to_all | solution.py:38
  39.8 16.5 %collective-permute-start.1 = (bf16[288,512]{1,0:T(8,128)(2,1)S(1)}, bf16[288,512]{1,0:T(8,128)(2,1)S(1)}, u32[]{:S(2)}, u32[]{:S(2)}) collective-permute-start(bf16[288,512]{1,0:T(8,128)(2,1)S(1)} %bitcast.92), channel_id=1, source_target_pairs={{0,3},{1,0},{2,1},{3,2},{4,7},{5,4},{6,5},{7,6},{8,11},{9,8},{10,9... | collective-permute-start | bytes 884744 | tf_op jit(solution)/shard_map/ppermute | solution.py:13
  45.8 15.8 %collective-permute-start.2 = (bf16[288,512]{1,0:T(8,128)(2,1)S(1)}, bf16[288,512]{1,0:T(8,128)(2,1)S(1)}, u32[]{:S(2)}, u32[]{:S(2)}) collective-permute-start(bf16[288,512]{1,0:T(8,128)(2,1)S(1)} %bitcast.93), channel_id=1, source_target_pairs={{0,2},{1,3},{2,0},{3,1},{4,6},{5,7},{6,4},{7,5},{8,10},{9,11},{10,... | collective-permute-start | bytes 884744 | tf_op jit(solution)/shard_map/ppermute | solution.py:13
  46.8 20.2 %collective-permute-start.3 = (bf16[288,512]{1,0:T(8,128)(2,1)S(1)}, bf16[288,512]{1,0:T(8,128)(2,1)S(1)}, u32[]{:S(2)}, u32[]{:S(2)}) collective-permute-start(bf16[288,512]{1,0:T(8,128)(2,1)S(1)} %bitcast.94), channel_id=1, source_target_pairs={{0,1},{1,2},{2,3},{3,0},{4,5},{5,6},{6,7},{7,4},{8,9},{9,10},{10,1... | collective-permute-start | bytes 884744 | tf_op jit(solution)/shard_map/ppermute | solution.py:13
  51.3 21.0 %collective-permute-start.4 = (bf16[512,1152]{1,0:T(8,128)(2,1)S(1)}, bf16[512,1152]{1,0:T(8,128)(2,1)S(1)}, u32[]{:S(2)}, u32[]{:S(2)}) collective-permute-start(bf16[512,1152]{1,0:T(8,128)(2,1)S(1)} %bitcast.81), channel_id=1, source_target_pairs={{0,4},{4,0},{1,5},{5,1},{2,6},{6,2},{3,7},{7,3},{8,12},{12,8},{9,1... | collective-permute-start | bytes 3538952 | tf_op jit(solution)/shard_map/ppermute | solution.py:13
  72.3 3.6 %copy-start.3 = (bf16[2304,512]{1,0:T(8,128)(2,1)S(1)}, bf16[2304,512]{1,0:T(8,128)(2,1)}, u32[]{:S(2)}) copy-start(bf16[2304,512]{1,0:T(8,128)(2,1)} %constant_dynamic-update-slice_fusion) | copy-start | bytes 7077892
  72.3 1.0 copy-start
  75.9 2.0 %copy-start.4 = (bf16[512,512]{1,0:T(8,128)(2,1)}, bf16[512,512]{1,0:T(8,128)(2,1)S(1)}, u32[]{:S(2)}) copy-start(bf16[512,512]{1,0:T(8,128)(2,1)S(1)} %fusion.18) | copy-start | bytes 1572868
  77.9 9.8 %collective-permute-start.8 = (bf16[512,1152]{1,0:T(8,128)(2,1)}, bf16[512,1152]{1,0:T(8,128)(2,1)}, u32[]{:S(2)}, u32[]{:S(2)}) collective-permute-start(bf16[512,1152]{1,0:T(8,128)(2,1)} %convolution_convert_fusion), channel_id=1, source_target_pairs={{0,4},{4,0},{1,5},{5,1},{2,6},{6,2},{3,7},{7,3},{8,12},{12,8},{9,1... | collective-permute-start | bytes 3538952 | tf_op jit(solution)/shard_map/ppermute | solution.py:13
  85.5 1.3 copy-start.1
  85.5 1.4 copy-start.5
  90.9 36.5 %all-to-all-start.2 = ((bf16[16,32,1152]{2,1,0:T(8,128)(2,1)}), bf16[16,32,1152]{2,1,0:T(8,128)(2,1)S(1)}, u32[]{:S(2)}, u32[]{:S(2)}) async-start(bf16[16,32,1152]{2,1,0:T(8,128)(2,1)} %bitcast.16), calls=%async_computation.2 | async-start | bytes 2359296 | tf_op jit(solution)/shard_map/all_to_all | solution.py:38
  98.4 13.2 %collective-permute-start.5 = (bf16[288,512]{1,0:T(8,128)(2,1)}, bf16[288,512]{1,0:T(8,128)(2,1)S(1)}, u32[]{:S(2)}, u32[]{:S(2)}) collective-permute-start(bf16[288,512]{1,0:T(8,128)(2,1)} %get-tuple-element.4), channel_id=1, source_target_pairs={{0,3},{1,0},{2,1},{3,2},{4,7},{5,4},{6,5},{7,6},{8,11},{9,8},{10,9... | collective-permute-start | bytes 884744 | tf_op jit(solution)/shard_map/ppermute | solution.py:13
  102.7 18.0 %collective-permute-start.6 = (bf16[288,512]{1,0:T(8,128)(2,1)}, bf16[288,512]{1,0:T(8,128)(2,1)S(1)}, u32[]{:S(2)}, u32[]{:S(2)}) collective-permute-start(bf16[288,512]{1,0:T(8,128)(2,1)} %get-tuple-element.3), channel_id=1, source_target_pairs={{0,2},{1,3},{2,0},{3,1},{4,6},{5,7},{6,4},{7,5},{8,10},{9,11},{10,... | collective-permute-start | bytes 884744 | tf_op jit(solution)/shard_map/ppermute | solution.py:13
  104.3 20.1 %collective-permute-start.7 = (bf16[288,512]{1,0:T(8,128)(2,1)S(1)}, bf16[288,512]{1,0:T(8,128)(2,1)S(1)}, u32[]{:S(2)}, u32[]{:S(2)}) collective-permute-start(bf16[288,512]{1,0:T(8,128)(2,1)S(1)} %get-tuple-element.2), channel_id=1, source_target_pairs={{0,1},{1,2},{2,3},{3,0},{4,5},{5,6},{6,7},{7,4},{8,9},{9,10},{10,1... | collective-permute-start | bytes 884744 | tf_op jit(solution)/shard_map/ppermute | solution.py:13
  127.6 9.9 %collective-permute-start.9 = (f32[16,1152]{1,0:T(8,128)S(1)}, f32[16,1152]{1,0:T(8,128)S(1)}, u32[]{:S(2)}, u32[]{:S(2)}) collective-permute-start(f32[16,1152]{1,0:T(8,128)S(1)} %dynamic-slice_bitcast_fusion.7), channel_id=1, source_target_pairs={{0,32},{32,0},{1,33},{33,1},{2,34},{34,2},{3,35},{35,3},{4,36},{36... | collective-permute-start | bytes 221192 | tf_op jit(solution)/shard_map/ppermute | solution.py:13
  137.5 4.6 %collective-permute-start.10 = (f32[8,1152]{1,0:T(8,128)S(1)}, f32[8,1152]{1,0:T(8,128)S(1)}, u32[]{:S(2)}, u32[]{:S(2)}) collective-permute-start(f32[8,1152]{1,0:T(8,128)S(1)} %dynamic-slice_bitcast_fusion.9), channel_id=1, source_target_pairs={{0,4},{4,0},{1,5},{5,1},{2,6},{6,2},{3,7},{7,3},{8,12},{12,8},{9,1... | collective-permute-start | bytes 110600 | tf_op jit(solution)/shard_map/ppermute | solution.py:13

commit v2 on v1

v2 whole, which is shorter than its diff:
```python
import jax
import jax.numpy as jnp
from jax import lax
from jax.experimental import pallas as pl
from jax.experimental.pallas import tpu as pltpu
from jax.sharding import Mesh
from jax.sharding import PartitionSpec as P

EPSILON = 1e-06
SIZES = (("x", 4), ("zl", 2), ("y", 4), ("c", 2), ("t", 4))
DP = ("x", "zl", "y", "c")
D, ROWS, PART, PEERS = 1152, 512, 288, 4
F32, BF16 = jnp.float32, jnp.bfloat16
VMEM, SMEM = pl.BlockSpec(memory_space=pltpu.VMEM), pl.BlockSpec(memory_space=pltpu.SMEM)
PARAMS = pltpu.CompilerParams(vmem_limit_bytes=24 << 20)


def like(*shape, dtype=BF16):
    return jax.ShapeDtypeStruct(shape, dtype)


def shift(value, axis, by, size):
    return lax.ppermute(value, axis, [(i, (i + by) % size) for i in range(size)])


def pick(parts, index):
    return lax.dynamic_index_in_dim(parts, index, 0, keepdims=False)


def across(parts):
    return lax.all_to_all(parts, ("x", "y"), split_axis=0, concat_axis=0, tiled=True)


def exchange_width(pieces):
    return [pieces[0]] + [shift(pieces[d], "t", d, PEERS) for d in (1, 2, 3)]


def cut_kernel(pictures, *pieces):
    mine = lax.axis_index("t")
    for d, piece in enumerate(pieces):
        block = lax.rem(mine + d, PEERS)
        rows = pl.ds(pl.multiple_of(block * ROWS, ROWS), ROWS)
        piece[...] = pictures[rows, :].T


def cut(pictures):
    return pl.pallas_call(
        cut_kernel,
        out_shape=[like(PART, ROWS)] * PEERS,
        in_specs=[VMEM],
        out_specs=[VMEM] * PEERS,
        compiler_params=PARAMS,
        cost_estimate=pl.CostEstimate(flops=0, bytes_accessed=3 << 20, transcendentals=0),
    )(pictures)


def unit_kernel(*refs):
    pieces, out = refs[:PEERS], refs[PEERS]
    mine = lax.axis_index("t")
    total = jnp.zeros((1, ROWS), F32)
    for piece in pieces:
        wide = piece[...].astype(F32)
        total = total + jnp.sum(wide * wide, axis=0, keepdims=True)
    scale = lax.rsqrt(total + EPSILON)
    for d, piece in enumerate(pieces):
        source = lax.rem(mine + (PEERS - d), PEERS)
        rows = pl.ds(pl.multiple_of(source * PART, PART), PART)
        out[rows, :] = (piece[...].astype(F32) * scale).astype(BF16)


def unit_columns(pieces):
    return pl.pallas_call(
        unit_kernel,
        out_shape=like(D, ROWS),
        in_specs=[VMEM] * PEERS,
        out_specs=VMEM,
        compiler_params=PARAMS,
        cost_estimate=pl.CostEstimate(flops=3 << 20, bytes_accessed=3 << 20, transcendentals=0),
    )(*pieces)


def unit_rows(values):
    wide = values.astype(F32)
    total = jnp.sum(wide * wide, axis=1, keepdims=True)
    return (wide * lax.rsqrt(total + EPSILON)).astype(BF16)


def place():
    axis = lax.axis_index
    return ((axis("x") * 2 + axis("zl")) * 4 + axis("y")) * 2 + axis("c")


def slab_weights(other, start, multiplier, offset, text, images, weights):
    core = lax.axis_index("c")
    step = (start[0] + core + other) & 1
    holder = lax.rem(start[0] + step, 64)
    held = place() == holder
    times, plus = multiplier[0], offset[0]
    tile = 128
    for at in range(0, ROWS, tile):
        logits = times * jnp.dot(text[at : at + tile, :], images[...], preferred_element_type=F32) + plus
        spot = lax.broadcasted_iota(jnp.int32, (tile, ROWS), 0) + at
        row = ((((spot >> 7) * 2 + ((spot >> 4) & 1)) * 4 + ((spot >> 5) & 3)) << 4) + (spot & 15)
        same = row == lax.broadcasted_iota(jnp.int32, (tile, ROWS), 1)
        positive = jnp.where(same & held, 1.0, 0.0)
        weights[at : at + tile, :] = ((jax.nn.sigmoid(logits) - positive) * times).astype(BF16)


def own_kernel(start, multiplier, offset, text, images, grad, terms, weights):
    slab_weights(0, start, multiplier, offset, text, images, weights)
    terms[...] = lax.dot_general(weights[...], images[...], (((1,), (1,)), ((), ())), preferred_element_type=F32)
    grad[...] = lax.dot_general(text[...], weights[...], (((0,), (0,)), ((), ())), preferred_element_type=F32)


def other_kernel(start, multiplier, offset, text, images, before, terms, *refs):
    pieces, (weights, grad) = refs[:PEERS], refs[PEERS:]
    mine = lax.axis_index("t")
    slab_weights(1, start, multiplier, offset, text, images, weights)
    terms[...] = lax.dot_general(
        weights[...], images[...], (((1,), (1,)), ((), ())), preferred_element_type=F32
    ).astype(BF16)
    grad[...] = before[...] + lax.dot_general(
        text[...], weights[...], (((0,), (0,)), ((), ())), preferred_element_type=F32
    )
    for d, piece in enumerate(pieces):
        target = lax.rem(mine + d, PEERS)
        piece[...] = grad[pl.ds(pl.multiple_of(target * PART, PART), PART), :].astype(BF16)


COST = pl.CostEstimate(flops=6 * D * ROWS * ROWS, bytes_accessed=8 << 20, transcendentals=ROWS * ROWS)


def own_slab(scalars, text, images):
    return pl.pallas_call(
        own_kernel,
        out_shape=[like(D, ROWS, dtype=F32), like(ROWS, D, dtype=F32)],
        in_specs=[SMEM] * 3 + [VMEM] * 2,
        out_specs=[VMEM] * 2,
        scratch_shapes=[pltpu.VMEM((ROWS, ROWS), BF16)],
        compiler_params=PARAMS,
        cost_estimate=COST,
    )(*scalars, text, images)


def other_slab(scalars, text, images, before):
    return pl.pallas_call(
        other_kernel,
        out_shape=[like(ROWS, D)] + [like(PART, ROWS)] * PEERS,
        in_specs=[SMEM] * 3 + [VMEM] * 3,
        out_specs=[VMEM] * (1 + PEERS),
        scratch_shapes=[pltpu.VMEM((ROWS, ROWS), BF16), pltpu.VMEM((D, ROWS), F32)],
        compiler_params=PARAMS,
        cost_estimate=COST,
    )(*scalars, text, images, before)


def lay_kernel(*refs):
    pieces, out = refs[:PEERS], refs[PEERS]
    mine = lax.axis_index("t")
    for d, piece in enumerate(pieces):
        block = lax.rem(mine + (PEERS - d), PEERS)
        out[pl.ds(pl.multiple_of(block * ROWS, ROWS), ROWS), :] = piece[...].T


def lay(pieces):
    return pl.pallas_call(
        lay_kernel,
        out_shape=like(PEERS * ROWS, PART),
        in_specs=[VMEM] * PEERS,
        out_specs=VMEM,
        compiler_params=PARAMS,
        cost_estimate=pl.CostEstimate(flops=0, bytes_accessed=3 << 20, transcendentals=0),
    )(*pieces)


def per_device(pictures, captions, start, multiplier, offset):
    core, z_lo = lax.axis_index("c"), lax.axis_index("zl")

    step_of = (start ^ core) & 1
    chip = ((start + step_of) % 64) >> 1
    root_y, root_z, root_x = chip & 3, (chip >> 2) & 1, chip >> 3

    pieces = cut(pictures)
    captions, pieces = lax.optimization_barrier((captions, pieces))
    text = captions.reshape(4, 2, 4, 16, D).transpose(0, 2, 1, 3, 4).reshape(16, 32, D)
    arrived = exchange_width(pieces)

    piece = pick(across(text), root_x * 4 + root_y)
    other = shift(piece, "zl", 1, 2)
    piece = unit_rows(jnp.where(z_lo == root_z, piece, other))
    piece, arrived = lax.optimization_barrier((piece, arrived))
    own = across(jnp.broadcast_to(piece[None], (16, 32, D))).reshape(ROWS, D)
    images = unit_columns(arrived)

    scalars = [value.reshape(1) for value in (start, multiplier, offset)]
    grad, own_terms = own_slab(scalars, own, images)
    other_terms, *pieces = other_slab(scalars, shift(own, "c", 1, 2), images, grad)

    image_grad = lay(exchange_width(pieces))

    total = own_terms + shift(other_terms, "c", 1, 2).astype(F32)
    total = jnp.sum(across(total.astype(BF16).reshape(16, 32, D)).astype(F32), axis=0)
    total = total.reshape(2, 2, 8, D)
    near, far = pick(total, z_lo), pick(total, 1 - z_lo)

    def flip(value, z, c):
        pairs = [(i, i ^ (8 * z + c)) for i in range(16)]
        return lax.ppermute(value, ("zl", "y", "c"), pairs)

    mine = pick(near, core) + flip(pick(far, core), 1, 0)
    theirs = flip(pick(near, 1 - core), 0, 1) + flip(pick(far, 1 - core), 1, 1)
    first = step_of == 0
    text_grad = jnp.stack([jnp.where(first, mine, theirs), jnp.where(first, theirs, mine)])
    return image_grad, text_grad[:, None]


def solution(mesh):
    names, sizes = zip(*SIZES)
    grid = Mesh(mesh.devices.reshape(sizes), names)
    return jax.shard_map(
        per_device,
        mesh=grid,
        in_specs=(P(DP, "t"), P(names, None), P(), P(), P()),
        out_specs=(P(DP, "t"), P(None, "t", DP, None)),
        check_vma=False,
    )
```

time: 143 us -> 138 us (0.965)
  blocking collectives: 0 us -> 26.5 us
  starting transfers between devices: 59.3 us -> 36.5 us
  local copies, waits for them, and re-layouts: 23.8 us -> 5.34 us
  waiting for transfers between devices: 43.5 us -> 55.9 us
  matrix products: 10.5 us -> 0 us
  Pallas kernels: 0 us -> 7.2 us
    all_to_all x0 -> x1, blocking collectives: none -> 26.5 us  [across(): lax.all_to_all(parts, ('x', 'y'), split_axis=0, concat_axis=0, tiled=True)]
    ppermute x11 -> x9, starting transfers between devices: 40.9 us -> 21.7 us  [shift(): lax.ppermute(value, axis, [(i, (i + by) % size) for i in range(size)])]
    all_to_all x3 -> x2, waiting for transfers between devices: 16 us -> 27.6 us  [across(): lax.all_to_all(parts, ('x', 'y'), split_axis=0, concat_axis=0, tiled=True)]
    dot_general x6 -> x0, matrix products: 10.5 us -> none  [the longest x2 5.18 us: per_device(): lax.dot_general(weights, images, (((1,), (1,)), ((), ())), preferred_elem...]
    unnamed x29 -> x4, local copies, waits for them, and re-layouts: 12.1 us -> 4.11 us
    pallas_call x0 -> x5, Pallas kernels: none -> 7.2 us  [the longest x1 3.71 us: other_slab(): pl.pallas_call(other_kernel, out_shape=[like(ROWS, D)] + [like(PART, ROWS...]
    all_to_all x3 -> x2, starting transfers between devices: 18.4 us -> 12 us  [across(): lax.all_to_all(parts, ('x', 'y'), split_axis=0, concat_axis=0, tiled=True)]
    dynamic_slice x2 -> x0, local copies, waits for them, and re-layouts: 3.78 us -> none  [the longest x1 2.43 us: pick(): return lax.dynamic_index_in_dim(parts, index, 0, keepdims=False)]
  transfers between devices with their start and end apart: 14 -> 14, of which waited for: 8 -> 7; matrix products, arithmetic and copies ran while one was open for 16% -> 2% of each run, Pallas kernels for 0% -> 2%
where the time goes in v2:
time: 138 us
  waiting for transfers between devices  55.9 us (41%)
  starting transfers between devices  36.5 us (26%)
  blocking collectives  26.5 us (19%)
  Pallas kernels  7.2 us (5%)
  local copies, waits for them, and re-layouts  5.34 us (4%)
  other arithmetic  3.63 us (3%)
  between operations  2.75 us (2%)
    ppermute x9, waiting for transfers between devices, shift(): lax.ppermute(value, axis, [(i, (i + by) % size) for i in range(size)])  28.4 us
    all_to_all x2, waiting for transfers between devices, across(): lax.all_to_all(parts, ('x', 'y'), split_axis=0, concat_axis=0, tiled=True)  27.6 us
    all_to_all x1, blocking collectives, across(): lax.all_to_all(parts, ('x', 'y'), split_axis=0, concat_axis=0, tiled=True)  26.5 us
    ppermute x9, starting transfers between devices, shift(): lax.ppermute(value, axis, [(i, (i + by) % size) for i in range(size)])  21.7 us
    all_to_all x2, starting transfers between devices, across(): lax.all_to_all(parts, ('x', 'y'), split_axis=0, concat_axis=0, tiled=True)  12 us
    unnamed x4, local copies, waits for them, and re-layouts  4.11 us
    pallas_call x1, Pallas kernels, other_slab(): pl.pallas_call(other_kernel, out_shape=[like(ROWS, D)] + [like(PART, ROWS...  3.71 us
    ppermute x3, starting transfers between devices, flip(): return lax.ppermute(value, ('zl', 'y', 'c'), pairs)  2.79 us
  transfers between devices with their start and end apart: 14, of which 7 were waited for; matrix products, arithmetic and copies ran while one was open for 2% of the time, Pallas kernels for 2%

profile of v2, /device:TPU:1, one launch (start us, length us, event | category | flops | bytes accessed | tf_op | source)
XLA Modules:
  0.0 137.9 jit_solution(18269958026465569269)
XLA Ops:
  0.6 1.8 %copy.11.pictures = bf16[2048,288]{1,0:T(8,128)(2,1)S(1)} copy(bf16[2048,288]{0,1:T(8,128)(2,1)} %param.5) | data formatting | bytes 2359296 | tf_op args[0]
  4.8 7.6 %all-to-all-start = ((bf16[16,32,1152]{2,1,0:T(8,128)(2,1)}), bf16[16,32,1152]{2,1,0:T(8,128)(2,1)S(1)}, u32[]{:S(2)}, u32[]{:S(2)}) async-start(bf16[16,32,1152]{2,1,0:T(8,128)(2,1)} %bitcast.5), calls=%async_computation | async-start | bytes 2359296 | tf_op jit(solution)/shard_map/all_to_all | solution.py:31
  13.1 16.1 %all-to-all-done = bf16[16,32,1152]{2,1,0:T(8,128)(2,1)S(1)} async-done(((bf16[16,32,1152]{2,1,0:T(8,128)(2,1)}), bf16[16,32,1152]{2,1,0:T(8,128)(2,1)S(1)}, u32[]{:S(2)}, u32[]{:S(2)}) %all-to-all-start) | async-done | bytes 1179680 | tf_op jit(solution)/shard_map/all_to_all | solution.py:31
  29.3 1.6 %collective-permute-start = (bf16[32,1152]{1,0:T(8,128)(2,1)S(1)}, bf16[32,1152]{1,0:T(8,128)(2,1)S(1)}, u32[]{:S(2)}, u32[]{:S(2)}) collective-permute-start(bf16[32,1152]{1,0:T(8,128)(2,1)S(1)} %dynamic-slice_bitcast_fusion), channel_id=1, source_target_pairs={{0,32},{32,0},{1,33},{33,1},{2,34},{34,2},{3,35},{35,3},{4,36},{36... | collective-permute-start | bytes 221192 | tf_op jit(solution)/shard_map/ppermute | solution.py:23
  30.9 3.0 %collective-permute-start.1 = (bf16[288,512]{1,0:T(8,128)(2,1)S(1)}, bf16[288,512]{1,0:T(8,128)(2,1)S(1)}, u32[]{:S(2)}, u32[]{:S(2)}) collective-permute-start(bf16[288,512]{1,0:T(8,128)(2,1)S(1)} %get-tuple-element.29), channel_id=1, source_target_pairs={{0,1},{1,2},{2,3},{3,0},{4,5},{5,6},{6,7},{7,4},{8,9},{9,10},{10,1... | collective-permute-start | bytes 884744 | tf_op jit(solution)/shard_map/ppermute | solution.py:23
  33.9 4.2 %collective-permute-start.2 = (bf16[288,512]{1,0:T(8,128)(2,1)S(1)}, bf16[288,512]{1,0:T(8,128)(2,1)S(1)}, u32[]{:S(2)}, u32[]{:S(2)}) collective-permute-start(bf16[288,512]{1,0:T(8,128)(2,1)S(1)} %get-tuple-element.30), channel_id=1, source_target_pairs={{0,2},{1,3},{2,0},{3,1},{4,6},{5,7},{6,4},{7,5},{8,10},{9,11},{10,... | collective-permute-start | bytes 884744 | tf_op jit(solution)/shard_map/ppermute | solution.py:23
  38.1 2.4 %collective-permute-start.3 = (bf16[288,512]{1,0:T(8,128)(2,1)S(1)}, bf16[288,512]{1,0:T(8,128)(2,1)S(1)}, u32[]{:S(2)}, u32[]{:S(2)}) collective-permute-start(bf16[288,512]{1,0:T(8,128)(2,1)S(1)} %get-tuple-element.31), channel_id=1, source_target_pairs={{0,3},{1,0},{2,1},{3,2},{4,7},{5,4},{6,5},{7,6},{8,11},{9,8},{10,9... | collective-permute-start | bytes 884744 | tf_op jit(solution)/shard_map/ppermute | solution.py:23
  40.7 7.1 %collective-permute-done.1.refs_1_ = bf16[288,512]{1,0:T(8,128)(2,1)S(1)} collective-permute-done((bf16[288,512]{1,0:T(8,128)(2,1)S(1)}, bf16[288,512]{1,0:T(8,128)(2,1)S(1)}, u32[]{:S(2)}, u32[]{:S(2)}) %collective-permute-start.1) | collective-permute-done | bytes 294944 | tf_op jit(solution)/shard_map/ppermute | solution.py:23
  47.8 10.2 %collective-permute-done.2.refs_2_ = bf16[288,512]{1,0:T(8,128)(2,1)S(1)} collective-permute-done((bf16[288,512]{1,0:T(8,128)(2,1)S(1)}, bf16[288,512]{1,0:T(8,128)(2,1)S(1)}, u32[]{:S(2)}, u32[]{:S(2)}) %collective-permute-start.2) | collective-permute-done | bytes 294944 | tf_op jit(solution)/shard_map/ppermute | solution.py:23
  58.7 26.5 %all_to_all.15 = bf16[16,32,1152]{2,1,0:T(8,128)(2,1)S(1)} all-to-all(bf16[16,32,1152]{2,1,0:T(8,128)(2,1)S(1)} %broadcast_in_dim.4), channel_id=1, replica_groups=mesh['x'=4,'zl'=2,'y'=4,'c'=2,'t'=4] {'x','y'}, dimensions={0} | all-to-all | bytes 2359296 | tf_op jit(solution)/shard_map/all_to_all | solution.py:31
  85.2 2.6 %collective-permute-start.4 = (bf16[512,1152]{1,0:T(8,128)(2,1)S(1)}, bf16[512,1152]{1,0:T(8,128)(2,1)}, u32[]{:S(2)}, u32[]{:S(2)}) collective-permute-start(bf16[512,1152]{1,0:T(8,128)(2,1)S(1)} %bitcast.40), channel_id=1, source_target_pairs={{0,4},{4,0},{1,5},{5,1},{2,6},{6,2},{3,7},{7,3},{8,12},{12,8},{9,1... | collective-permute-start | bytes 3538952 | tf_op jit(solution)/shard_map/ppermute | solution.py:23
  89.4 2.2 %shard_map.70 = (f32[1152,512]{1,0:T(8,128)S(1)}, f32[512,1152]{1,0:T(8,128)S(1)}) custom-call(s32[1]{0:T(128)} %bitcast.34.start, f32[1]{0:T(128)} %bitcast.36.multiplier, f32[1]{0:T(128)} %bitcast.38.offset, bf16[512,1152]{1,0:T(8,128)(2,1)S(1)} %bitcast.41, bf16[1152,512]{1,0:T(8,128)(2,1)S(1)} %shard_map.69.images), custom_call_target="tpu_custom_call" | custom-call | flops 1811939328 | bytes 8388608 | tf_op jit(solution)/shard_map/pallas_call | solution.py:134
  91.7 3.7 %shard_map.71 = (bf16[512,1152]{1,0:T(8,128)(2,1)S(1)}, bf16[288,512]{1,0:T(8,128)(2,1)S(1)}, bf16[288,512]{1,0:T(8,128)(2,1)S(1)}, bf16[288,512]{1,0:T(8,128)(2,1)S(1)}, bf16[288,512]{1,0:T(8,128)(2,1)S(1)}) custom-call(s32[1]{0:T(128)} %bitcast.35.start, f32[1]{0:T(128)} %bitcast.37.multiplier, f32[1]{0:T(128)} %bitcast.39.offset, ...), custom_call_target="tpu_custom_call" | custom-call | flops 1811939328 | bytes 8388608 | tf_op jit(solution)/shard_map/pallas_call | solution.py:146
  95.5 2.8 %collective-permute-done.8 = bf16[512,1152]{1,0:T(8,128)(2,1)S(1)} collective-permute-done((bf16[512,1152]{1,0:T(8,128)(2,1)S(1)}, bf16[512,1152]{1,0:T(8,128)(2,1)S(1)}, u32[]{:S(2)}, u32[]{:S(2)}) %collective-permute-start.8) | collective-permute-done | bytes 1179680 | tf_op jit(solution)/shard_map/ppermute | solution.py:23
  99.6 4.4 %all-to-all-start.2 = ((bf16[16,32,1152]{2,1,0:T(8,128)(2,1)}), bf16[16,32,1152]{2,1,0:T(8,128)(2,1)}, u32[]{:S(2)}, u32[]{:S(2)}) async-start(bf16[16,32,1152]{2,1,0:T(8,128)(2,1)} %bitcast.8), calls=%async_computation.2 | async-start | bytes 2359296 | tf_op jit(solution)/shard_map/all_to_all | solution.py:31
  104.0 1.5 %collective-permute-start.5 = (bf16[288,512]{1,0:T(8,128)(2,1)S(1)}, bf16[288,512]{1,0:T(8,128)(2,1)S(1)}, u32[]{:S(2)}, u32[]{:S(2)}) collective-permute-start(bf16[288,512]{1,0:T(8,128)(2,1)S(1)} %get-tuple-element.39), channel_id=1, source_target_pairs={{0,1},{1,2},{2,3},{3,0},{4,5},{5,6},{6,7},{7,4},{8,9},{9,10},{10,1... | collective-permute-start | bytes 884744 | tf_op jit(solution)/shard_map/ppermute | solution.py:23
  105.5 4.0 %collective-permute-start.6 = (bf16[288,512]{1,0:T(8,128)(2,1)S(1)}, bf16[288,512]{1,0:T(8,128)(2,1)S(1)}, u32[]{:S(2)}, u32[]{:S(2)}) collective-permute-start(bf16[288,512]{1,0:T(8,128)(2,1)S(1)} %get-tuple-element.40), channel_id=1, source_target_pairs={{0,2},{1,3},{2,0},{3,1},{4,6},{5,7},{6,4},{7,5},{8,10},{9,11},{10,... | collective-permute-start | bytes 884744 | tf_op jit(solution)/shard_map/ppermute | solution.py:23
  109.5 2.3 %collective-permute-start.7 = (bf16[288,512]{1,0:T(8,128)(2,1)S(1)}, bf16[288,512]{1,0:T(8,128)(2,1)S(1)}, u32[]{:S(2)}, u32[]{:S(2)}) collective-permute-start(bf16[288,512]{1,0:T(8,128)(2,1)S(1)} %get-tuple-element.41), channel_id=1, source_target_pairs={{0,3},{1,0},{2,1},{3,2},{4,7},{5,4},{6,5},{7,6},{8,11},{9,8},{10,9... | collective-permute-start | bytes 884744 | tf_op jit(solution)/shard_map/ppermute | solution.py:23
  111.9 11.4 %all-to-all-done.2 = bf16[16,32,1152]{2,1,0:T(8,128)(2,1)} async-done(((bf16[16,32,1152]{2,1,0:T(8,128)(2,1)}), bf16[16,32,1152]{2,1,0:T(8,128)(2,1)}, u32[]{:S(2)}, u32[]{:S(2)}) %all-to-all-start.2) | async-done | bytes 1179680 | tf_op jit(solution)/shard_map/all_to_all | solution.py:31
  123.3 1.4 %convert_reduce_fusion = f32[32,1152]{1,0:T(8,128)S(1)} fusion(bf16[16,32,1152]{2,1,0:T(8,128)(2,1)} %all-to-all-done.2), kind=kLoop, calls=%fused_computation | loop fusion | flops 1142784 | bytes 1327104 | tf_op jit(solution)/shard_map/reduce_sum | solution.py:202
  124.8 1.3 collective-permute-start.10
  126.1 1.4 %collective-permute-start.9 = (f32[8,1152]{1,0:T(8,128)S(1)}, f32[8,1152]{1,0:T(8,128)S(1)}, u32[]{:S(2)}, u32[]{:S(2)}) collective-permute-start(f32[8,1152]{1,0:T(8,128)S(1)} %get-tuple-element.52), channel_id=1, source_target_pairs={{0,32},{4,36},{8,40},{12,44},{16,48},{20,52},{24,56},{28,60},{32,0... | collective-permute-start | bytes 110600 | tf_op jit(solution)/shard_map/ppermute | solution.py:208
  127.6 7.7 %collective-permute-done.6.refs_2_ = bf16[288,512]{1,0:T(8,128)(2,1)S(1)} collective-permute-done((bf16[288,512]{1,0:T(8,128)(2,1)S(1)}, bf16[288,512]{1,0:T(8,128)(2,1)S(1)}, u32[]{:S(2)}, u32[]{:S(2)}) %collective-permute-start.6) | collective-permute-done | bytes 294944 | tf_op jit(solution)/shard_map/ppermute | solution.py:23
  135.7 1.5 %copy.13 = bf16[2048,288]{0,1:T(8,128)(2,1)} copy(bf16[2048,288]{1,0:T(8,128)(2,1)S(1)} %shard_map.72) | data formatting | bytes 2359296
  (25 shorter events, 6.1 us)
Async XLA Ops:
  2.4 1.3 copy-start
  4.8 24.4 %all-to-all-start = ((bf16[16,32,1152]{2,1,0:T(8,128)(2,1)}), bf16[16,32,1152]{2,1,0:T(8,128)(2,1)S(1)}, u32[]{:S(2)}, u32[]{:S(2)}) async-start(bf16[16,32,1152]{2,1,0:T(8,128)(2,1)} %bitcast.5), calls=%async_computation | async-start | bytes 2359296 | tf_op jit(solution)/shard_map/all_to_all | solution.py:31
  29.3 11.2 %collective-permute-start = (bf16[32,1152]{1,0:T(8,128)(2,1)S(1)}, bf16[32,1152]{1,0:T(8,128)(2,1)S(1)}, u32[]{:S(2)}, u32[]{:S(2)}) collective-permute-start(bf16[32,1152]{1,0:T(8,128)(2,1)S(1)} %dynamic-slice_bitcast_fusion), channel_id=1, source_target_pairs={{0,32},{32,0},{1,33},{33,1},{2,34},{34,2},{3,35},{35,3},{4,36},{36... | collective-permute-start | bytes 221192 | tf_op jit(solution)/shard_map/ppermute | solution.py:23
  30.9 16.9 %collective-permute-start.1 = (bf16[288,512]{1,0:T(8,128)(2,1)S(1)}, bf16[288,512]{1,0:T(8,128)(2,1)S(1)}, u32[]{:S(2)}, u32[]{:S(2)}) collective-permute-start(bf16[288,512]{1,0:T(8,128)(2,1)S(1)} %get-tuple-element.29), channel_id=1, source_target_pairs={{0,1},{1,2},{2,3},{3,0},{4,5},{5,6},{6,7},{7,4},{8,9},{9,10},{10,1... | collective-permute-start | bytes 884744 | tf_op jit(solution)/shard_map/ppermute | solution.py:23
  33.9 24.1 %collective-permute-start.2 = (bf16[288,512]{1,0:T(8,128)(2,1)S(1)}, bf16[288,512]{1,0:T(8,128)(2,1)S(1)}, u32[]{:S(2)}, u32[]{:S(2)}) collective-permute-start(bf16[288,512]{1,0:T(8,128)(2,1)S(1)} %get-tuple-element.30), channel_id=1, source_target_pairs={{0,2},{1,3},{2,0},{3,1},{4,6},{5,7},{6,4},{7,5},{8,10},{9,11},{10,... | collective-permute-start | bytes 884744 | tf_op jit(solution)/shard_map/ppermute | solution.py:23
  38.1 20.5 %collective-permute-start.3 = (bf16[288,512]{1,0:T(8,128)(2,1)S(1)}, bf16[288,512]{1,0:T(8,128)(2,1)S(1)}, u32[]{:S(2)}, u32[]{:S(2)}) collective-permute-start(bf16[288,512]{1,0:T(8,128)(2,1)S(1)} %get-tuple-element.31), channel_id=1, source_target_pairs={{0,3},{1,0},{2,1},{3,2},{4,7},{5,4},{6,5},{7,6},{8,11},{9,8},{10,9... | collective-permute-start | bytes 884744 | tf_op jit(solution)/shard_map/ppermute | solution.py:23
  85.2 6.5 %collective-permute-start.4 = (bf16[512,1152]{1,0:T(8,128)(2,1)S(1)}, bf16[512,1152]{1,0:T(8,128)(2,1)}, u32[]{:S(2)}, u32[]{:S(2)}) collective-permute-start(bf16[512,1152]{1,0:T(8,128)(2,1)S(1)} %bitcast.40), channel_id=1, source_target_pairs={{0,4},{4,0},{1,5},{5,1},{2,6},{6,2},{3,7},{7,3},{8,12},{12,8},{9,1... | collective-permute-start | bytes 3538952 | tf_op jit(solution)/shard_map/ppermute | solution.py:23
  95.4 2.9 %collective-permute-start.8 = (bf16[512,1152]{1,0:T(8,128)(2,1)S(1)}, bf16[512,1152]{1,0:T(8,128)(2,1)S(1)}, u32[]{:S(2)}, u32[]{:S(2)}) collective-permute-start(bf16[512,1152]{1,0:T(8,128)(2,1)S(1)} %get-tuple-element.43), channel_id=1, source_target_pairs={{0,4},{4,0},{1,5},{5,1},{2,6},{6,2},{3,7},{7,3},{8,12},{12,8},{9,1... | collective-permute-start | bytes 3538952 | tf_op jit(solution)/shard_map/ppermute | solution.py:23
  99.6 23.7 %all-to-all-start.2 = ((bf16[16,32,1152]{2,1,0:T(8,128)(2,1)}), bf16[16,32,1152]{2,1,0:T(8,128)(2,1)}, u32[]{:S(2)}, u32[]{:S(2)}) async-start(bf16[16,32,1152]{2,1,0:T(8,128)(2,1)} %bitcast.8), calls=%async_computation.2 | async-start | bytes 2359296 | tf_op jit(solution)/shard_map/all_to_all | solution.py:31
  104.0 22.1 %collective-permute-start.5 = (bf16[288,512]{1,0:T(8,128)(2,1)S(1)}, bf16[288,512]{1,0:T(8,128)(2,1)S(1)}, u32[]{:S(2)}, u32[]{:S(2)}) collective-permute-start(bf16[288,512]{1,0:T(8,128)(2,1)S(1)} %get-tuple-element.39), channel_id=1, source_target_pairs={{0,1},{1,2},{2,3},{3,0},{4,5},{5,6},{6,7},{7,4},{8,9},{9,10},{10,1... | collective-permute-start | bytes 884744 | tf_op jit(solution)/shard_map/ppermute | solution.py:23
  105.5 29.7 %collective-permute-start.6 = (bf16[288,512]{1,0:T(8,128)(2,1)S(1)}, bf16[288,512]{1,0:T(8,128)(2,1)S(1)}, u32[]{:S(2)}, u32[]{:S(2)}) collective-permute-start(bf16[288,512]{1,0:T(8,128)(2,1)S(1)} %get-tuple-element.40), channel_id=1, source_target_pairs={{0,2},{1,3},{2,0},{3,1},{4,6},{5,7},{6,4},{7,5},{8,10},{9,11},{10,... | collective-permute-start | bytes 884744 | tf_op jit(solution)/shard_map/ppermute | solution.py:23
  109.5 25.7 %collective-permute-start.7 = (bf16[288,512]{1,0:T(8,128)(2,1)S(1)}, bf16[288,512]{1,0:T(8,128)(2,1)S(1)}, u32[]{:S(2)}, u32[]{:S(2)}) collective-permute-start(bf16[288,512]{1,0:T(8,128)(2,1)S(1)} %get-tuple-element.41), channel_id=1, source_target_pairs={{0,3},{1,0},{2,1},{3,2},{4,7},{5,4},{6,5},{7,6},{8,11},{9,8},{10,9... | collective-permute-start | bytes 884744 | tf_op jit(solution)/shard_map/ppermute | solution.py:23
  124.8 12.4 %collective-permute-start.10 = (f32[8,1152]{1,0:T(8,128)S(1)}, f32[8,1152]{1,0:T(8,128)S(1)}, u32[]{:S(2)}, u32[]{:S(2)}) collective-permute-start(f32[8,1152]{1,0:T(8,128)S(1)} %get-tuple-element.54), channel_id=1, source_target_pairs={{0,4},{4,0},{8,12},{12,8},{16,20},{20,16},{24,28},{28,24},{32,36},... | collective-permute-start | bytes 110600 | tf_op jit(solution)/shard_map/ppermute | solution.py:208
  126.1 11.1 %collective-permute-start.11 = (f32[8,1152]{1,0:T(8,128)S(1)}, f32[8,1152]{1,0:T(8,128)S(1)}, u32[]{:S(2)}, u32[]{:S(2)}) collective-permute-start(f32[8,1152]{1,0:T(8,128)S(1)} %get-tuple-element.53), channel_id=1, source_target_pairs={{0,36},{4,32},{8,44},{12,40},{16,52},{20,48},{24,60},{28,56},{32,4... | collective-permute-start | bytes 110600 | tf_op jit(solution)/shard_map/ppermute | solution.py:208
  126.1 11.1 %collective-permute-start.9 = (f32[8,1152]{1,0:T(8,128)S(1)}, f32[8,1152]{1,0:T(8,128)S(1)}, u32[]{:S(2)}, u32[]{:S(2)}) collective-permute-start(f32[8,1152]{1,0:T(8,128)S(1)} %get-tuple-element.52), channel_id=1, source_target_pairs={{0,32},{4,36},{8,40},{12,44},{16,48},{20,52},{24,56},{28,60},{32,0... | collective-permute-start | bytes 110600 | tf_op jit(solution)/shard_map/ppermute | solution.py:208

commit v3 on v2

v3 whole, which is shorter than its diff:
```python
import jax
import jax.numpy as jnp
from jax import lax
from jax.experimental import pallas as pl
from jax.experimental.pallas import tpu as pltpu
from jax.sharding import Mesh
from jax.sharding import PartitionSpec as P

EPSILON = 1e-06
SIZES = (("x", 4), ("zl", 2), ("y", 4), ("c", 2), ("t", 4))
DP = ("x", "zl", "y", "c")
D, ROWS, PART, PEERS = 1152, 512, 288, 4
F32, BF16 = jnp.float32, jnp.bfloat16
VMEM, SMEM, HBM = (pl.BlockSpec(memory_space=space) for space in (pltpu.VMEM, pltpu.SMEM, pltpu.HBM))
PARAMS = pltpu.CompilerParams(vmem_limit_bytes=24 << 20)


def like(*shape, dtype=BF16):
    return jax.ShapeDtypeStruct(shape, dtype)


def shift(value, axis, by, size):
    return lax.ppermute(value, axis, [(i, (i + by) % size) for i in range(size)])


def pick(parts, index):
    return lax.dynamic_index_in_dim(parts, index, 0, keepdims=False)


def across(parts):
    return lax.all_to_all(parts, ("x", "y"), split_axis=0, concat_axis=0, tiled=True)


def exchange_width(pieces):
    return [pieces[0]] + [shift(pieces[d], "t", d, PEERS) for d in (1, 2, 3)]


def cut_kernel(pictures, *refs):
    pieces, done = refs[:PEERS], refs[PEERS]
    mine = lax.axis_index("t")
    copies = []
    for d, piece in enumerate(pieces):
        block = lax.rem(mine + d, PEERS)
        rows = pl.ds(pl.multiple_of(block * ROWS, ROWS), ROWS)
        copies.append(pltpu.make_async_copy(pictures.at[:, rows], piece, done.at[d]))
        copies[-1].start()
    for copy in copies:
        copy.wait()


def cut(pictures):
    return pl.pallas_call(
        cut_kernel,
        out_shape=[like(PART, ROWS)] * PEERS,
        in_specs=[HBM],
        out_specs=[VMEM] * PEERS,
        scratch_shapes=[pltpu.SemaphoreType.DMA((PEERS,))],
        compiler_params=PARAMS,
        cost_estimate=pl.CostEstimate(flops=0, bytes_accessed=3 << 20, transcendentals=0),
    )(pictures)


def unit_kernel(*refs):
    pieces, out = refs[:PEERS], refs[PEERS]
    mine = lax.axis_index("t")
    total = jnp.zeros((1, ROWS), F32)
    for piece in pieces:
        wide = piece[...].astype(F32)
        total = total + jnp.sum(wide * wide, axis=0, keepdims=True)
    scale = lax.rsqrt(total + EPSILON)
    for d, piece in enumerate(pieces):
        source = lax.rem(mine + (PEERS - d), PEERS)
        rows = pl.ds(pl.multiple_of(source * PART, PART), PART)
        out[rows, :] = (piece[...].astype(F32) * scale).astype(BF16)


def unit_columns(pieces):
    return pl.pallas_call(
        unit_kernel,
        out_shape=like(D, ROWS),
        in_specs=[VMEM] * PEERS,
        out_specs=VMEM,
        compiler_params=PARAMS,
        cost_estimate=pl.CostEstimate(flops=3 << 20, bytes_accessed=3 << 20, transcendentals=0),
    )(*pieces)


def unit_rows(values):
    wide = values.astype(F32)
    total = jnp.sum(wide * wide, axis=1, keepdims=True)
    return (wide * lax.rsqrt(total + EPSILON)).astype(BF16)


def place():
    axis = lax.axis_index
    return ((axis("x") * 2 + axis("zl")) * 4 + axis("y")) * 2 + axis("c")


def slab_weights(other, start, multiplier, offset, text, images, weights):
    core = lax.axis_index("c")
    step = (start[0] + core + other) & 1
    holder = lax.rem(start[0] + step, 64)
    held = place() == holder
    times, plus = multiplier[0], offset[0]
    tile = 128
    for at in range(0, ROWS, tile):
        logits = times * jnp.dot(text[at : at + tile, :], images[...], preferred_element_type=F32) + plus
        row = lax.broadcasted_iota(jnp.int32, (tile, ROWS), 0) + at
        same = row == lax.broadcasted_iota(jnp.int32, (tile, ROWS), 1)
        positive = jnp.where(same & held, 1.0, 0.0)
        weights[at : at + tile, :] = ((jax.nn.sigmoid(logits) - positive) * times).astype(BF16)


def slab_terms(images, weights, by_owner, keep, send):
    core = lax.axis_index("c")
    tile = 128
    for at in range(0, ROWS, tile):
        terms = lax.dot_general(
            weights[at : at + tile, :], images[...], (((1,), (1,)), ((), ())), preferred_element_type=F32
        )
        for inner in range(tile // 8):
            group = at // 8 + inner
            x, z, y, c = group >> 4, (group >> 3) & 1, (group >> 1) & 3, group & 1
            by_owner[c, x * 4 + y, 8 * z : 8 * z + 8, :] = terms[8 * inner : 8 * inner + 8, :]
    keep[...] = by_owner[core]
    send[...] = by_owner[1 - core].astype(BF16)


def own_kernel(start, multiplier, offset, text, images, keep, send, grad, weights, by_owner):
    slab_weights(0, start, multiplier, offset, text, images, weights)
    slab_terms(images, weights, by_owner, keep, send)
    grad[...] = lax.dot_general(text[...], weights[...], (((0,), (0,)), ((), ())), preferred_element_type=F32)


def other_kernel(start, multiplier, offset, text, images, keep, send, weights, by_owner):
    slab_weights(1, start, multiplier, offset, text, images, weights)
    slab_terms(images, weights, by_owner, keep, send)


def pieces_kernel(text, weights, before, *refs):
    pieces, grad = refs[:PEERS], refs[PEERS]
    mine = lax.axis_index("t")
    grad[...] = before[...] + lax.dot_general(
        text[...], weights[...], (((0,), (0,)), ((), ())), preferred_element_type=F32
    )
    for d, piece in enumerate(pieces):
        target = lax.rem(mine + d, PEERS)
        piece[...] = grad[pl.ds(pl.multiple_of(target * PART, PART), PART), :].astype(BF16)


def cost(products, moved):
    return pl.CostEstimate(flops=2 * products * D * ROWS * ROWS, bytes_accessed=moved << 20, transcendentals=0)


OWNED = (16, 16, D)


def own_slab(scalars, text, images):
    return pl.pallas_call(
        own_kernel,
        out_shape=[like(*OWNED, dtype=F32), like(*OWNED), like(D, ROWS, dtype=F32)],
        in_specs=[SMEM] * 3 + [VMEM] * 2,
        out_specs=[VMEM] * 3,
        scratch_shapes=[pltpu.VMEM((ROWS, ROWS), BF16), pltpu.VMEM((2,) + OWNED, F32)],
        compiler_params=PARAMS,
        cost_estimate=cost(3, 8),
    )(*scalars, text, images)


def other_slab(scalars, text, images):
    return pl.pallas_call(
        other_kernel,
        out_shape=[like(*OWNED, dtype=F32), like(*OWNED), like(ROWS, ROWS)],
        in_specs=[SMEM] * 3 + [VMEM] * 2,
        out_specs=[VMEM] * 3,
        scratch_shapes=[pltpu.VMEM((2,) + OWNED, F32)],
        compiler_params=PARAMS,
        cost_estimate=cost(2, 5),
    )(*scalars, text, images)


def image_pieces(text, weights, before):
    return pl.pallas_call(
        pieces_kernel,
        out_shape=[like(PART, ROWS)] * PEERS,
        in_specs=[VMEM] * 3,
        out_specs=[VMEM] * PEERS,
        scratch_shapes=[pltpu.VMEM((D, ROWS), F32)],
        compiler_params=PARAMS,
        cost_estimate=cost(1, 5),
    )(text, weights, before)


def join_kernel(own, from_other, other, from_own, out):
    out[:, :16, :] = (own[...] + from_other[...].astype(F32)).astype(BF16)
    out[:, 16:, :] = (other[...] + from_own[...].astype(F32)).astype(BF16)


def join(own, from_other, other, from_own):
    return pl.pallas_call(
        join_kernel,
        out_shape=like(16, 32, D),
        in_specs=[VMEM] * 4,
        out_specs=VMEM,
        compiler_params=PARAMS,
        cost_estimate=cost(0, 4),
    )(own, from_other, other, from_own)


def sum_kernel(start, parts, keep, send, total):
    z_lo = lax.axis_index("zl")
    first = (start[0] + lax.axis_index("c")) & 1
    total[...] = jnp.sum(parts[...].astype(F32), axis=0)
    for slab, step in ((0, first), (1, 1 - first)):
        keep[step] = total[pl.ds(pl.multiple_of(16 * slab + 8 * z_lo, 8), 8), :]
        send[step] = total[pl.ds(pl.multiple_of(16 * slab + 8 * (1 - z_lo), 8), 8), :]


def sum_chips(start, parts):
    return pl.pallas_call(
        sum_kernel,
        out_shape=[like(2, 8, D, dtype=F32)] * 2,
        in_specs=[SMEM, VMEM],
        out_specs=[VMEM] * 2,
        scratch_shapes=[pltpu.VMEM((32, D), F32)],
        compiler_params=PARAMS,
        cost_estimate=cost(0, 1),
    )(start, parts)


def lay_kernel(*refs):
    pieces, out, done = refs[:PEERS], refs[PEERS], refs[PEERS + 1]
    mine = lax.axis_index("t")
    copies = []
    for d, piece in enumerate(pieces):
        block = lax.rem(mine + (PEERS - d), PEERS)
        rows = pl.ds(pl.multiple_of(block * ROWS, ROWS), ROWS)
        copies.append(pltpu.make_async_copy(piece, out.at[:, rows], done.at[d]))
        copies[-1].start()
    for copy in copies:
        copy.wait()


def lay(pieces):
    return pl.pallas_call(
        lay_kernel,
        out_shape=like(PART, PEERS * ROWS),
        in_specs=[VMEM] * PEERS,
        out_specs=HBM,
        scratch_shapes=[pltpu.SemaphoreType.DMA((PEERS,))],
        compiler_params=PARAMS,
        cost_estimate=cost(0, 3),
    )(*pieces)


def per_device(pictures, captions, start, multiplier, offset):
    core, z_lo = lax.axis_index("c"), lax.axis_index("zl")

    step_of = (start ^ core) & 1
    chip = ((start + step_of) % 64) >> 1
    root_y, root_z, root_x = chip & 3, (chip >> 2) & 1, chip >> 3

    arrived = exchange_width(cut(pictures.T))
    text = across(captions.reshape(16, 32, D))
    text, arrived[1], arrived[3] = lax.optimization_barrier((text, arrived[1], arrived[3]))

    piece = pick(text, root_x * 4 + root_y)
    other = shift(piece, "zl", 1, 2)
    piece = unit_rows(jnp.where(z_lo == root_z, piece, other))
    own = across(jnp.broadcast_to(piece[None], (16, 32, D))).reshape(ROWS, D)
    own, arrived[2] = lax.optimization_barrier((own, arrived[2]))
    images = unit_columns(arrived)

    scalars = [value.reshape(1) for value in (start, multiplier, offset)]
    keep_own, send_own, grad = own_slab(scalars, own, images)
    theirs = shift(own, "c", 1, 2)
    keep_other, send_other, weights = other_slab(scalars, theirs, images)
    image_grad = lay(exchange_width(image_pieces(theirs, weights, grad))).T

    parts = join(keep_own, shift(send_other, "c", 1, 2), keep_other, shift(send_own, "c", 1, 2))
    keep, send = sum_chips(scalars[0], across(parts))
    text_grad = keep + shift(send, "zl", 1, 2)
    return image_grad, text_grad[:, None]


def solution(mesh):
    names, sizes = zip(*SIZES)
    grid = Mesh(mesh.devices.reshape(sizes), names)
    return jax.shard_map(
        per_device,
        mesh=grid,
        in_specs=(P(DP, "t"), P(names, None), P(), P(), P()),
        out_specs=(P(DP, "t"), P(None, "t", DP, None)),
        check_vma=False,
    )
```

time: 138 us -> 121 us (0.88)
  blocking collectives: 26.5 us -> 0 us
  Pallas kernels: 7.2 us -> 13.3 us
  starting transfers between devices: 36.5 us -> 40.5 us
    all_to_all x1 -> x0, blocking collectives: 26.5 us -> none  [across(): lax.all_to_all(parts, ('x', 'y'), split_axis=0, concat_axis=0, tiled=True)]
    ppermute x9 -> x11, waiting for transfers between devices: 28.4 us -> 47.7 us  [shift(): lax.ppermute(value, axis, [(i, (i + by) % size) for i in range(size)])]
    all_to_all x2 -> x3, waiting for transfers between devices: 27.6 us -> 8.58 us  [across(): lax.all_to_all(parts, ('x', 'y'), split_axis=0, concat_axis=0, tiled=True)]
    pallas_call x3 -> x6, Pallas kernels: 6.42 us -> 12.8 us  [the longest x1 3.81 us: other_slab(): pl.pallas_call(other_kernel, out_shape=[like(*OWNED, dtype=F32), like(*OW...]
    all_to_all x2 -> x3, starting transfers between devices: 12 us -> 18.1 us  [across(): lax.all_to_all(parts, ('x', 'y'), split_axis=0, concat_axis=0, tiled=True)]
    ppermute x3 -> x0, starting transfers between devices: 2.79 us -> none  [flip(): return lax.ppermute(value, ('zl', 'y', 'c'), pairs)]
    unnamed x4 -> x10, local copies, waits for them, and re-layouts: 4.11 us -> 2.56 us
    reduce_sum x1 -> x0, other arithmetic: 1.45 us -> none  [per_device(): jnp.sum(across(total.astype(BF16).reshape(16, 32, D)).astype(F32), axis=0)]
  transfers between devices with their start and end apart: 14 -> 14, of which waited for: 7 -> 11; matrix products, arithmetic and copies ran while one was open for 2% -> 0% of each run, Pallas kernels for 2% -> 10%
where the time goes in v3:
time: 121 us; the launch traced here: 120 us
  waiting for transfers between devices  56.3 us (47%)
  starting transfers between devices  40.5 us (33%)
  Pallas kernels  13.3 us (11%)
  local copies, waits for them, and re-layouts  4.55 us (4%)
  between operations  2.74 us (2%)
  other arithmetic  2.64 us (2%)
    ppermute x11, waiting for transfers between devices, shift(): lax.ppermute(value, axis, [(i, (i + by) % size) for i in range(size)])  47.7 us
    ppermute x11, starting transfers between devices, shift(): lax.ppermute(value, axis, [(i, (i + by) % size) for i in range(size)])  22.4 us
    all_to_all x3, starting transfers between devices, across(): lax.all_to_all(parts, ('x', 'y'), split_axis=0, concat_axis=0, tiled=True)  18.1 us
    all_to_all x3, waiting for transfers between devices, across(): lax.all_to_all(parts, ('x', 'y'), split_axis=0, concat_axis=0, tiled=True)  8.58 us
    pallas_call x1, Pallas kernels, other_slab(): pl.pallas_call(other_kernel, out_shape=[like(*OWNED, dtype=F32), like(*OW...  3.81 us
    pallas_call x1, Pallas kernels, own_slab(): pl.pallas_call(own_kernel, out_shape=[like(*OWNED, dtype=F32), like(*OWNE...  3.36 us
    pallas_call x1, Pallas kernels, image_pieces(): pl.pallas_call(pieces_kernel, out_shape=[like(PART, ROWS)] * PEERS, in_sp...  3.17 us
    unnamed x10, local copies, waits for them, and re-layouts  2.56 us
  transfers between devices with their start and end apart: 14, of which 11 were waited for; matrix products, arithmetic and copies ran while one was open for 0% of the time, Pallas kernels for 10%

profile of v3, /device:TPU:1, one launch (start us, length us, event | category | flops | bytes accessed | tf_op | source)
XLA Modules:
  0.0 120.0 jit_solution(17729552526423443371)
XLA Ops:
  0.6 7.8 %all-to-all-start = ((bf16[16,32,1152]{2,1,0:T(8,128)(2,1)}), bf16[16,32,1152]{2,1,0:T(8,128)(2,1)}, u32[]{:S(2)}, u32[]{:S(2)}) async-start(bf16[16,32,1152]{2,1,0:T(8,128)(2,1)} %bitcast.27), calls=%async_computation | async-start | bytes 2359296 | tf_op jit(solution)/shard_map/all_to_all | solution.py:31
  8.6 3.1 %collective-permute-start = (bf16[288,512]{1,0:T(8,128)(2,1)S(1)}, bf16[288,512]{1,0:T(8,128)(2,1)S(1)}, u32[]{:S(2)}, u32[]{:S(2)}) collective-permute-start(bf16[288,512]{1,0:T(8,128)(2,1)S(1)} %get-tuple-element.23), channel_id=1, source_target_pairs={{0,1},{1,2},{2,3},{3,0},{4,5},{5,6},{6,7},{7,4},{8,9},{9,10},{10,1... | collective-permute-start | bytes 884744 | tf_op jit(solution)/shard_map/ppermute | solution.py:23
  11.7 3.1 %collective-permute-start.1 = (bf16[288,512]{1,0:T(8,128)(2,1)S(1)}, bf16[288,512]{1,0:T(8,128)(2,1)S(1)}, u32[]{:S(2)}, u32[]{:S(2)}) collective-permute-start(bf16[288,512]{1,0:T(8,128)(2,1)S(1)} %get-tuple-element.24), channel_id=1, source_target_pairs={{0,3},{1,0},{2,1},{3,2},{4,7},{5,4},{6,5},{7,6},{8,11},{9,8},{10,9... | collective-permute-start | bytes 884744 | tf_op jit(solution)/shard_map/ppermute | solution.py:23
  15.5 7.4 %collective-permute-done.refs_1_ = bf16[288,512]{1,0:T(8,128)(2,1)S(1)} collective-permute-done((bf16[288,512]{1,0:T(8,128)(2,1)S(1)}, bf16[288,512]{1,0:T(8,128)(2,1)S(1)}, u32[]{:S(2)}, u32[]{:S(2)}) %collective-permute-start) | collective-permute-done | bytes 294944 | tf_op jit(solution)/shard_map/ppermute | solution.py:23
  22.8 6.3 %collective-permute-done.1.refs_3_ = bf16[288,512]{1,0:T(8,128)(2,1)S(1)} collective-permute-done((bf16[288,512]{1,0:T(8,128)(2,1)S(1)}, bf16[288,512]{1,0:T(8,128)(2,1)S(1)}, u32[]{:S(2)}, u32[]{:S(2)}) %collective-permute-start.1) | collective-permute-done | bytes 294944 | tf_op jit(solution)/shard_map/ppermute | solution.py:23
  30.0 3.2 %collective-permute-done.2 = bf16[32,1152]{1,0:T(8,128)(2,1)S(1)} collective-permute-done((bf16[32,1152]{1,0:T(8,128)(2,1)S(1)}, bf16[32,1152]{1,0:T(8,128)(2,1)S(1)}, u32[]{:S(2)}, u32[]{:S(2)}) %collective-permute-start.2) | collective-permute-done | bytes 73760 | tf_op jit(solution)/shard_map/ppermute | solution.py:23
  35.2 1.1 broadcast_in_dim.4
  36.3 6.6 %all-to-all-start.1 = ((bf16[16,32,1152]{2,1,0:T(8,128)(2,1)}), bf16[16,32,1152]{2,1,0:T(8,128)(2,1)S(1)}, u32[]{:S(2)}, u32[]{:S(2)}) async-start(bf16[16,32,1152]{2,1,0:T(8,128)(2,1)} %broadcast_in_dim.4), calls=%async_computation.1 | async-start | bytes 2359296 | tf_op jit(solution)/shard_map/all_to_all | solution.py:31
  42.9 2.9 %collective-permute-start.3 = (bf16[288,512]{1,0:T(8,128)(2,1)S(1)}, bf16[288,512]{1,0:T(8,128)(2,1)S(1)}, u32[]{:S(2)}, u32[]{:S(2)}) collective-permute-start(bf16[288,512]{1,0:T(8,128)(2,1)S(1)} %get-tuple-element.26), channel_id=1, source_target_pairs={{0,2},{1,3},{2,0},{3,1},{4,6},{5,7},{6,4},{7,5},{8,10},{9,11},{10,... | collective-permute-start | bytes 884744 | tf_op jit(solution)/shard_map/ppermute | solution.py:23
  45.8 8.9 %collective-permute-done.3.refs_2_ = bf16[288,512]{1,0:T(8,128)(2,1)S(1)} collective-permute-done((bf16[288,512]{1,0:T(8,128)(2,1)S(1)}, bf16[288,512]{1,0:T(8,128)(2,1)S(1)}, u32[]{:S(2)}, u32[]{:S(2)}) %collective-permute-start.3) | collective-permute-done | bytes 294944 | tf_op jit(solution)/shard_map/ppermute | solution.py:23
  54.7 4.1 %all-to-all-done.1 = bf16[16,32,1152]{2,1,0:T(8,128)(2,1)S(1)} async-done(((bf16[16,32,1152]{2,1,0:T(8,128)(2,1)}), bf16[16,32,1152]{2,1,0:T(8,128)(2,1)S(1)}, u32[]{:S(2)}, u32[]{:S(2)}) %all-to-all-start.1) | async-done | bytes 1179680 | tf_op jit(solution)/shard_map/all_to_all | solution.py:31
  58.7 3.7 %collective-permute-start.4 = (bf16[512,1152]{1,0:T(8,128)(2,1)S(1)}, bf16[512,1152]{1,0:T(8,128)(2,1)}, u32[]{:S(2)}, u32[]{:S(2)}) collective-permute-start(bf16[512,1152]{1,0:T(8,128)(2,1)S(1)} %bitcast.25), channel_id=1, source_target_pairs={{0,4},{4,0},{1,5},{5,1},{2,6},{6,2},{3,7},{7,3},{8,12},{12,8},{9,1... | collective-permute-start | bytes 3538952 | tf_op jit(solution)/shard_map/ppermute | solution.py:23
  64.0 3.4 %shard_map.71 = (f32[16,16,1152]{2,1,0:T(8,128)S(1)}, bf16[16,16,1152]{2,1,0:T(8,128)(2,1)S(1)}, f32[1152,512]{1,0:T(8,128)S(1)}) custom-call(s32[1]{0:T(128)} %bitcast.18.start, f32[1]{0:T(128)} %bitcast.21.multiplier, f32[1]{0:T(128)} %bitcast.23.offset, bf16[512,1152]{1,0:T(8,128)(2,1)S(1)} %bitcast.26, bf16[1152,512]{1,0:T(8,128)(2,1)S(1)} %shard_map.69.images), custom_call_target="tpu_custom_call" | custom-call | flops 1811939328 | bytes 8388608 | tf_op jit(solution)/shard_map/pallas_call | solution.py:159
  67.5 3.8 %shard_map.70 = (f32[16,16,1152]{2,1,0:T(8,128)S(1)}, bf16[16,16,1152]{2,1,0:T(8,128)(2,1)S(1)}, bf16[512,512]{1,0:T(8,128)(2,1)S(1)}) custom-call(s32[1]{0:T(128)} %bitcast.17.start, f32[1]{0:T(128)} %bitcast.20.multiplier, f32[1]{0:T(128)} %bitcast.22.offset, bf16[512,1152]{1,0:T(8,128)(2,1)} %collective-permute-done.4.text, ...), custom_call_target="tpu_custom_call" | custom-call | flops 1207959552 | bytes 5242880 | tf_op jit(solution)/shard_map/pallas_call | solution.py:171
  72.6 1.6 %collective-permute-done.8.from_other = bf16[16,16,1152]{2,1,0:T(8,128)(2,1)S(1)} collective-permute-done((bf16[16,16,1152]{2,1,0:T(8,128)(2,1)S(1)}, bf16[16,16,1152]{2,1,0:T(8,128)(2,1)S(1)}, u32[]{:S(2)}, u32[]{:S(2)}) %collective-permute-start.8) | collective-permute-done | bytes 589856 | tf_op jit(solution)/shard_map/ppermute | solution.py:23
  74.3 1.2 %shard_map.74 = bf16[16,32,1152]{2,1,0:T(8,128)(2,1)} custom-call(f32[16,16,1152]{2,1,0:T(8,128)S(1)} %get-tuple-element.38.own, bf16[16,16,1152]{2,1,0:T(8,128)(2,1)S(1)} %collective-permute-done.8.from_other, f32[16,16,1152]{2,1,0:T(8,128)S(1)} %get-tuple-element.40.other, bf16[16,16,1152]{2,1,0:T(8,128)(2,1)S(1)} %collective-permute-done.9.from_own), custom_call_target="tpu_custom_call" | custom-call | bytes 4194304 | tf_op jit(solution)/shard_map/pallas_call | solution.py:200
  75.5 3.7 %all-to-all-start.2 = ((bf16[16,32,1152]{2,1,0:T(8,128)(2,1)}), bf16[16,32,1152]{2,1,0:T(8,128)(2,1)S(1)}, u32[]{:S(2)}, u32[]{:S(2)}) async-start(bf16[16,32,1152]{2,1,0:T(8,128)(2,1)} %shard_map.74), calls=%async_computation.2 | async-start | bytes 2359296 | tf_op jit(solution)/shard_map/all_to_all | solution.py:31
  80.2 3.2 %shard_map.72 = (bf16[288,512]{1,0:T(8,128)(2,1)S(1)}, bf16[288,512]{1,0:T(8,128)(2,1)}, bf16[288,512]{1,0:T(8,128)(2,1)}, bf16[288,512]{1,0:T(8,128)(2,1)}) custom-call(bf16[512,1152]{1,0:T(8,128)(2,1)} %collective-permute-done.4.text, bf16[512,512]{1,0:T(8,128)(2,1)S(1)} %copy-done.2, f32[1152,512]{1,0:T(8,128)S(1)} %get-tuple-element.33.before), custom_call_target="tpu_custom_call" | custom-call | flops 603979776 | bytes 5242880 | tf_op jit(solution)/shard_map/pallas_call | solution.py:183
  84.1 5.2 %collective-permute-start.5 = (bf16[288,512]{1,0:T(8,128)(2,1)}, bf16[288,512]{1,0:T(8,128)(2,1)S(1)}, u32[]{:S(2)}, u32[]{:S(2)}) collective-permute-start(bf16[288,512]{1,0:T(8,128)(2,1)} %get-tuple-element.35), channel_id=1, source_target_pairs={{0,1},{1,2},{2,3},{3,0},{4,5},{5,6},{6,7},{7,4},{8,9},{9,10},{10,1... | collective-permute-start | bytes 884744 | tf_op jit(solution)/shard_map/ppermute | solution.py:23
  89.3 2.0 %collective-permute-start.6 = (bf16[288,512]{1,0:T(8,128)(2,1)}, bf16[288,512]{1,0:T(8,128)(2,1)S(1)}, u32[]{:S(2)}, u32[]{:S(2)}) collective-permute-start(bf16[288,512]{1,0:T(8,128)(2,1)} %get-tuple-element.36), channel_id=1, source_target_pairs={{0,2},{1,3},{2,0},{3,1},{4,6},{5,7},{6,4},{7,5},{8,10},{9,11},{10,... | collective-permute-start | bytes 884744 | tf_op jit(solution)/shard_map/ppermute | solution.py:23
  91.3 1.3 %collective-permute-start.7 = (bf16[288,512]{1,0:T(8,128)(2,1)}, bf16[288,512]{1,0:T(8,128)(2,1)S(1)}, u32[]{:S(2)}, u32[]{:S(2)}) collective-permute-start(bf16[288,512]{1,0:T(8,128)(2,1)} %get-tuple-element.37), channel_id=1, source_target_pairs={{0,3},{1,0},{2,1},{3,2},{4,7},{5,4},{6,5},{7,6},{8,11},{9,8},{10,9... | collective-permute-start | bytes 884744 | tf_op jit(solution)/shard_map/ppermute | solution.py:23
  92.6 4.5 %all-to-all-done.2.parts = bf16[16,32,1152]{2,1,0:T(8,128)(2,1)S(1)} async-done(((bf16[16,32,1152]{2,1,0:T(8,128)(2,1)}), bf16[16,32,1152]{2,1,0:T(8,128)(2,1)S(1)}, u32[]{:S(2)}, u32[]{:S(2)}) %all-to-all-start.2) | async-done | bytes 1179680 | tf_op jit(solution)/shard_map/all_to_all | solution.py:31
  98.0 1.9 %collective-permute-done.5.refs_1_ = bf16[288,512]{1,0:T(8,128)(2,1)S(1)} collective-permute-done((bf16[288,512]{1,0:T(8,128)(2,1)}, bf16[288,512]{1,0:T(8,128)(2,1)S(1)}, u32[]{:S(2)}, u32[]{:S(2)}) %collective-permute-start.5) | collective-permute-done | bytes 294944 | tf_op jit(solution)/shard_map/ppermute | solution.py:23
  99.9 17.6 %collective-permute-done.6.refs_2_ = bf16[288,512]{1,0:T(8,128)(2,1)S(1)} collective-permute-done((bf16[288,512]{1,0:T(8,128)(2,1)}, bf16[288,512]{1,0:T(8,128)(2,1)S(1)}, u32[]{:S(2)}, u32[]{:S(2)}) %collective-permute-start.6) | collective-permute-done | bytes 294944 | tf_op jit(solution)/shard_map/ppermute | solution.py:23
  (28 shorter events, 9.8 us)
Async XLA Ops:
  0.6 7.8 %copy-start = (bf16[2048,288]{0,1:T(8,128)(2,1)S(1)}, bf16[2048,288]{0,1:T(8,128)(2,1)}, u32[]{:S(2)}) copy-start(bf16[2048,288]{0,1:T(8,128)(2,1)} %param.5) | copy-start | bytes 3538948
  0.6 28.5 %all-to-all-start = ((bf16[16,32,1152]{2,1,0:T(8,128)(2,1)}), bf16[16,32,1152]{2,1,0:T(8,128)(2,1)}, u32[]{:S(2)}, u32[]{:S(2)}) async-start(bf16[16,32,1152]{2,1,0:T(8,128)(2,1)} %bitcast.27), calls=%async_computation | async-start | bytes 2359296 | tf_op jit(solution)/shard_map/all_to_all | solution.py:31
  8.6 14.2 %collective-permute-start = (bf16[288,512]{1,0:T(8,128)(2,1)S(1)}, bf16[288,512]{1,0:T(8,128)(2,1)S(1)}, u32[]{:S(2)}, u32[]{:S(2)}) collective-permute-start(bf16[288,512]{1,0:T(8,128)(2,1)S(1)} %get-tuple-element.23), channel_id=1, source_target_pairs={{0,1},{1,2},{2,3},{3,0},{4,5},{5,6},{6,7},{7,4},{8,9},{9,10},{10,1... | collective-permute-start | bytes 884744 | tf_op jit(solution)/shard_map/ppermute | solution.py:23
  11.7 17.5 %collective-permute-start.1 = (bf16[288,512]{1,0:T(8,128)(2,1)S(1)}, bf16[288,512]{1,0:T(8,128)(2,1)S(1)}, u32[]{:S(2)}, u32[]{:S(2)}) collective-permute-start(bf16[288,512]{1,0:T(8,128)(2,1)S(1)} %get-tuple-element.24), channel_id=1, source_target_pairs={{0,3},{1,0},{2,1},{3,2},{4,7},{5,4},{6,5},{7,6},{8,11},{9,8},{10,9... | collective-permute-start | bytes 884744 | tf_op jit(solution)/shard_map/ppermute | solution.py:23
  30.0 3.2 %collective-permute-start.2 = (bf16[32,1152]{1,0:T(8,128)(2,1)S(1)}, bf16[32,1152]{1,0:T(8,128)(2,1)S(1)}, u32[]{:S(2)}, u32[]{:S(2)}) collective-permute-start(bf16[32,1152]{1,0:T(8,128)(2,1)S(1)} %dynamic-slice_bitcast_fusion), channel_id=1, source_target_pairs={{0,32},{32,0},{1,33},{33,1},{2,34},{34,2},{3,35},{35,3},{4,36},{36... | collective-permute-start | bytes 221192 | tf_op jit(solution)/shard_map/ppermute | solution.py:23
  36.3 22.4 %all-to-all-start.1 = ((bf16[16,32,1152]{2,1,0:T(8,128)(2,1)}), bf16[16,32,1152]{2,1,0:T(8,128)(2,1)S(1)}, u32[]{:S(2)}, u32[]{:S(2)}) async-start(bf16[16,32,1152]{2,1,0:T(8,128)(2,1)} %broadcast_in_dim.4), calls=%async_computation.1 | async-start | bytes 2359296 | tf_op jit(solution)/shard_map/all_to_all | solution.py:31
  42.9 11.7 %collective-permute-start.3 = (bf16[288,512]{1,0:T(8,128)(2,1)S(1)}, bf16[288,512]{1,0:T(8,128)(2,1)S(1)}, u32[]{:S(2)}, u32[]{:S(2)}) collective-permute-start(bf16[288,512]{1,0:T(8,128)(2,1)S(1)} %get-tuple-element.26), channel_id=1, source_target_pairs={{0,2},{1,3},{2,0},{3,1},{4,6},{5,7},{6,4},{7,5},{8,10},{9,11},{10,... | collective-permute-start | bytes 884744 | tf_op jit(solution)/shard_map/ppermute | solution.py:23
  58.7 8.8 %collective-permute-start.4 = (bf16[512,1152]{1,0:T(8,128)(2,1)S(1)}, bf16[512,1152]{1,0:T(8,128)(2,1)}, u32[]{:S(2)}, u32[]{:S(2)}) collective-permute-start(bf16[512,1152]{1,0:T(8,128)(2,1)S(1)} %bitcast.25), channel_id=1, source_target_pairs={{0,4},{4,0},{1,5},{5,1},{2,6},{6,2},{3,7},{7,3},{8,12},{12,8},{9,1... | collective-permute-start | bytes 3538952 | tf_op jit(solution)/shard_map/ppermute | solution.py:23
  67.4 5.2 %collective-permute-start.9 = (bf16[16,16,1152]{2,1,0:T(8,128)(2,1)S(1)}, bf16[16,16,1152]{2,1,0:T(8,128)(2,1)S(1)}, u32[]{:S(2)}, u32[]{:S(2)}) collective-permute-start(bf16[16,16,1152]{2,1,0:T(8,128)(2,1)S(1)} %get-tuple-element.41), channel_id=1, source_target_pairs={{0,4},{4,0},{1,5},{5,1},{2,6},{6,2},{3,7},{7,3},{8,12},{12,8},{9,1... | collective-permute-start | bytes 1769480 | tf_op jit(solution)/shard_map/ppermute | solution.py:23
  71.3 0.8 copy-start.1
  72.1 2.1 %collective-permute-start.8 = (bf16[16,16,1152]{2,1,0:T(8,128)(2,1)S(1)}, bf16[16,16,1152]{2,1,0:T(8,128)(2,1)S(1)}, u32[]{:S(2)}, u32[]{:S(2)}) collective-permute-start(bf16[16,16,1152]{2,1,0:T(8,128)(2,1)S(1)} %get-tuple-element.39), channel_id=1, source_target_pairs={{0,4},{4,0},{1,5},{5,1},{2,6},{6,2},{3,7},{7,3},{8,12},{12,8},{9,1... | collective-permute-start | bytes 1769480 | tf_op jit(solution)/shard_map/ppermute | solution.py:23
  75.5 21.6 %all-to-all-start.2 = ((bf16[16,32,1152]{2,1,0:T(8,128)(2,1)}), bf16[16,32,1152]{2,1,0:T(8,128)(2,1)S(1)}, u32[]{:S(2)}, u32[]{:S(2)}) async-start(bf16[16,32,1152]{2,1,0:T(8,128)(2,1)} %shard_map.74), calls=%async_computation.2 | async-start | bytes 2359296 | tf_op jit(solution)/shard_map/all_to_all | solution.py:31
  79.2 1.0 copy-start.2
  83.4 0.7 copy-start.3
  84.1 33.6 %copy-start.4 = (bf16[288,512]{1,0:T(8,128)(2,1)S(1)}, bf16[288,512]{1,0:T(8,128)(2,1)}, u32[]{:S(2)}) copy-start(bf16[288,512]{1,0:T(8,128)(2,1)} %copy-done.3) | copy-start | bytes 884740
  84.1 15.8 %collective-permute-start.5 = (bf16[288,512]{1,0:T(8,128)(2,1)}, bf16[288,512]{1,0:T(8,128)(2,1)S(1)}, u32[]{:S(2)}, u32[]{:S(2)}) collective-permute-start(bf16[288,512]{1,0:T(8,128)(2,1)} %get-tuple-element.35), channel_id=1, source_target_pairs={{0,1},{1,2},{2,3},{3,0},{4,5},{5,6},{6,7},{7,4},{8,9},{9,10},{10,1... | collective-permute-start | bytes 884744 | tf_op jit(solution)/shard_map/ppermute | solution.py:23
  89.3 28.2 %collective-permute-start.6 = (bf16[288,512]{1,0:T(8,128)(2,1)}, bf16[288,512]{1,0:T(8,128)(2,1)S(1)}, u32[]{:S(2)}, u32[]{:S(2)}) collective-permute-start(bf16[288,512]{1,0:T(8,128)(2,1)} %get-tuple-element.36), channel_id=1, source_target_pairs={{0,2},{1,3},{2,0},{3,1},{4,6},{5,7},{6,4},{7,5},{8,10},{9,11},{10,... | collective-permute-start | bytes 884744 | tf_op jit(solution)/shard_map/ppermute | solution.py:23
  91.3 26.3 %collective-permute-start.7 = (bf16[288,512]{1,0:T(8,128)(2,1)}, bf16[288,512]{1,0:T(8,128)(2,1)S(1)}, u32[]{:S(2)}, u32[]{:S(2)}) collective-permute-start(bf16[288,512]{1,0:T(8,128)(2,1)} %get-tuple-element.37), channel_id=1, source_target_pairs={{0,3},{1,0},{2,1},{3,2},{4,7},{5,4},{6,5},{7,6},{8,11},{9,8},{10,9... | collective-permute-start | bytes 884744 | tf_op jit(solution)/shard_map/ppermute | solution.py:23
  97.3 22.0 %collective-permute-start.10 = (f32[2,8,1152]{2,1,0:T(8,128)S(1)}, f32[2,8,1152]{2,1,0:T(8,128)S(1)}, u32[]{:S(2)}, u32[]{:S(2)}) collective-permute-start(f32[2,8,1152]{2,1,0:T(8,128)S(1)} %get-tuple-element.43), channel_id=1, source_target_pairs={{0,32},{32,0},{1,33},{33,1},{2,34},{34,2},{3,35},{35,3},{4,36},{36... | collective-permute-start | bytes 221192 | tf_op jit(solution)/shard_map/ppermute | solution.py:23

commit v4 on v1

v4 whole, which is shorter than its diff:
```python
import jax
import jax.numpy as jnp
from jax import lax
from jax.experimental import pallas as pl
from jax.experimental.pallas import tpu as pltpu
from jax.sharding import Mesh
from jax.sharding import PartitionSpec as P

EPSILON = 1e-06
SIZES = (("x", 4), ("zl", 2), ("y", 4), ("c", 2), ("t", 4))
DP = ("x", "zl", "y", "c")
D, ROWS, PART, PEERS = 1152, 512, 288, 4
CHUNK, PIECE, HALF = 128, 32, 256
OWNED = (16, 16, D)
F32, BF16 = jnp.float32, jnp.bfloat16
VMEM, SMEM, HBM = (pl.BlockSpec(memory_space=space) for space in (pltpu.VMEM, pltpu.SMEM, pltpu.HBM))
DMA = pltpu.SemaphoreType.DMA


def like(*shape, dtype=BF16):
    return jax.ShapeDtypeStruct(shape, dtype)


def call(kernel, outs, ins, scratch=(), products=0, moved=1):
    single = not isinstance(outs, list)
    return pl.pallas_call(
        kernel,
        out_shape=outs,
        in_specs=ins,
        out_specs=VMEM if single else [VMEM] * len(outs),
        scratch_shapes=list(scratch),
        compiler_params=pltpu.CompilerParams(vmem_limit_bytes=16 << 20),
        cost_estimate=pl.CostEstimate(
            flops=2 * products * D * ROWS * ROWS, bytes_accessed=moved << 20, transcendentals=0
        ),
    )


def shift(value, axis, by, size):
    return lax.ppermute(value, axis, [(i, (i + by) % size) for i in range(size)])


def along(value, first, by):
    pairs = []
    for i in range(64):
        x, z, y, c = i >> 4, (i >> 3) & 1, (i >> 1) & 3, i & 1
        if (c == 0) == first:
            x = (x + by) % 4
        else:
            y = (y + by) % 4
        pairs.append((i, ((x * 2 + z) * 4 + y) * 2 + c))
    return lax.ppermute(value, DP, pairs)


def spot():
    x, y, c = lax.axis_index("x"), lax.axis_index("y"), lax.axis_index("c")
    return c, jnp.where(c == 0, x, y), jnp.where(c == 0, y, x)


def holder_of(start, other):
    step = (start[0] + lax.axis_index("c") + other) & 1
    return step, lax.rem(start[0] + step, 64)


def back(place, d):
    return lax.rem(place + (4 - d), 4)


def ahead(place, d):
    return lax.rem(place + d, 4)


def window(index, size):
    return pl.ds(pl.multiple_of(index * size, size), size)


def run(copies):
    for copy in copies:
        copy.start()
    for copy in copies:
        copy.wait()


def cut_kernel(pictures, own, one, three, two_low, two_high, done):
    mine = lax.axis_index("t")
    places = [(own, 0, 0), (one, 1, 0), (three, 3, 0), (two_low, 2, 0), (two_high, 2, HALF)]
    copies = []
    for i, (piece, d, at) in enumerate(places):
        size = piece.shape[1]
        rows = pl.ds(pl.multiple_of(ahead(mine, d) * ROWS + at, HALF), size)
        copies.append(pltpu.make_async_copy(pictures.at[:, rows], piece, done.at[i]))
    run(copies)


def arrange_kernel(captions, text, done):
    run(
        [
            pltpu.make_async_copy(captions.at[x, z], text.at[x, :, z], done.at[2 * x + z])
            for x in range(4)
            for z in range(2)
        ]
    )


def pick_kernel(start, parts, piece):
    chip = holder_of(start, 0)[1] >> 1
    piece[...] = parts[(chip >> 3) * 4 + (chip & 3)]


def unit_rows_kernel(start, here, there, piece):
    chip = holder_of(start, 0)[1] >> 1
    is_here = ((chip >> 2) & 1) == lax.axis_index("zl")
    wide = jnp.where(is_here, here[...].astype(F32), there[...].astype(F32))
    total = jnp.sum(wide * wide, axis=1, keepdims=True)
    piece[...] = (wide * lax.rsqrt(total + EPSILON)).astype(BF16)


def gather_kernel(*refs):
    chunk = refs[4]
    place = spot()[2]
    for d in range(4):
        chunk[window(back(place, d), PIECE), :] = refs[d][...]


def unit_columns_kernel(own, one, three, two_low, two_high, out):
    mine = lax.axis_index("t")
    total = [jnp.zeros((1, HALF), F32)] * 2
    parts = []
    for d, low, high in ((0, own, own), (1, one, one), (3, three, three), (2, two_low, two_high)):
        for side, piece in enumerate((low, high)):
            at = side * HALF if piece.shape[1] == ROWS else 0
            parts.append((d, side, piece, at))
            wide = piece[:, at : at + HALF].astype(F32)
            total[side] = total[side] + jnp.sum(wide * wide, axis=0, keepdims=True)
    scale = [lax.rsqrt(value + EPSILON) for value in total]
    for d, side, piece, at in parts:
        wide = piece[:, at : at + HALF].astype(F32)
        out[window(back(mine, d), PART), side * HALF : side * HALF + HALF] = (wide * scale[side]).astype(BF16)


def slab_weights(other, start, multiplier, offset, chunks, images, text, weights):
    core, first, second = spot()
    held = lax.axis_index(DP) == holder_of(start, other)[1]
    kind, place = (core, first) if other == 0 else (1 - core, second)
    times, plus = multiplier[0], offset[0]
    for d in range(4):
        rows = slice(CHUNK * d, CHUNK * d + CHUNK)
        text[rows, :] = chunks[d][...]
        logits = times * jnp.dot(chunks[d][...], images[...], preferred_element_type=F32) + plus
        at = lax.broadcasted_iota(jnp.int32, (CHUNK, 1), 0)
        inner, along_first = at >> 5, back(place, d)
        x = jnp.where(kind == 0, along_first, inner)
        y = jnp.where(kind == 0, inner, along_first)
        row = x * 128 + ((at >> 4) & 1) * 64 + y * 16 + (at & 15)
        same = row == lax.broadcasted_iota(jnp.int32, (CHUNK, ROWS), 1)
        positive = jnp.where(same & held, 1.0, 0.0)
        weights[rows, :] = ((jax.nn.sigmoid(logits) - positive) * times).astype(BF16)


def slab_terms(other, images, weights, by_owner, keep, send):
    core, first, second = spot()
    kind, place = (core, first) if other == 0 else (1 - core, second)
    for d in range(4):
        terms = lax.dot_general(
            weights[CHUNK * d : CHUNK * d + CHUNK, :],
            images[...],
            (((1,), (1,)), ((), ())),
            preferred_element_type=F32,
        )
        for inner in range(4):
            straight, turned = back(place, d) * 4 + inner, inner * 4 + back(place, d)
            spots = (jnp.where(kind == 0, straight, turned), jnp.where(kind == 0, turned, straight))
            for z in range(2):
                for c in range(2):
                    at = PIECE * inner + 16 * z + 8 * c
                    by_owner[c, spots[c], 8 * z : 8 * z + 8, :] = terms[at : at + 8, :]
    keep[...] = by_owner[core]
    send[...] = by_owner[1 - core].astype(BF16)


def turned_product(text, weights):
    return lax.dot_general(text[...], weights[...], (((0,), (0,)), ((), ())), preferred_element_type=F32)


def own_kernel(start, multiplier, offset, *refs):
    chunks, (images, keep, send, grad, text, weights, by_owner) = refs[:4], refs[4:]
    slab_weights(0, start, multiplier, offset, chunks, images, text, weights)
    slab_terms(0, images, weights, by_owner, keep, send)
    grad[...] = turned_product(text, weights)


def other_kernel(start, multiplier, offset, *refs):
    chunks, (images, keep, send, weights, text, by_owner) = refs[:4], refs[4:]
    slab_weights(1, start, multiplier, offset, chunks, images, text, weights)
    slab_terms(1, images, weights, by_owner, keep, send)


def pieces_kernel(*refs):
    chunks, (weights, before), pieces, (text, grad) = refs[:4], refs[4:6], refs[6:10], refs[10:]
    for d in range(4):
        text[CHUNK * d : CHUNK * d + CHUNK, :] = chunks[d][...]
    mine = lax.axis_index("t")
    grad[...] = before[...] + turned_product(text, weights)
    for d, piece in enumerate(pieces):
        piece[...] = grad[window(ahead(mine, d), PART), :].astype(BF16)


def join_kernel(own, from_other, other, from_own, *outs):
    place = spot()[1]
    for d, out in enumerate(outs):
        rows = window(ahead(place, d), 4)
        out[:, :16, :] = (own[rows] + from_other[rows].astype(F32)).astype(out.dtype)
        out[:, 16:, :] = (other[rows] + from_own[rows].astype(F32)).astype(out.dtype)


def first_sum_kernel(own, one, two, three, *refs):
    outs, total = refs[:4], refs[4]
    place = spot()[2]
    total[...] = (own[...] + one[...].astype(F32)) + (two[...].astype(F32) + three[...].astype(F32))
    for d, out in enumerate(outs):
        out[...] = total[ahead(place, d)].astype(out.dtype)


def second_sum_kernel(start, own, one, two, three, keep, send, total):
    z_lo = lax.axis_index("zl")
    step = holder_of(start, 0)[0]
    total[...] = (own[...] + one[...].astype(F32)) + (two[...].astype(F32) + three[...].astype(F32))
    for slab, at in ((0, step), (1, 1 - step)):
        keep[at] = total[window(2 * slab + z_lo, 8), :]
        send[at] = total[window(2 * slab + 1 - z_lo, 8), :]


def lay_kernel(*refs):
    pieces, out, done = refs[:4], refs[4], refs[5]
    mine = lax.axis_index("t")
    run(
        [
            pltpu.make_async_copy(piece, out.at[:, window(back(mine, d), ROWS)], done.at[d])
            for d, piece in enumerate(pieces)
        ]
    )


def lay(pieces):
    return pl.pallas_call(
        lay_kernel,
        out_shape=like(PART, PEERS * ROWS),
        in_specs=[VMEM] * PEERS,
        out_specs=HBM,
        scratch_shapes=[DMA((PEERS,))],
    )(*pieces)


def per_device(pictures, captions, start, multiplier, offset):
    start, multiplier, offset = (value.reshape(1) for value in (start, multiplier, offset))
    scalars, scalar_specs = (start, multiplier, offset), [SMEM] * 3

    shapes = [like(PART, ROWS)] * 3 + [like(PART, HALF)] * 2
    near, one, three, low, high = call(cut_kernel, shapes, [HBM], [DMA((5,))], moved=2)(pictures.T)
    one, three, low, high = (shift(v, "t", d, PEERS) for v, d in ((one, 1), (three, 3), (low, 2), (high, 2)))

    text = call(arrange_kernel, like(4, 4, 2, 16, D), [HBM], [DMA((8,))], moved=2)(captions.reshape(4, 2, 4, 16, D))
    text = lax.all_to_all(text.reshape(16, PIECE, D), ("x", "y"), split_axis=0, concat_axis=0, tiled=True)
    text, one, three, low = lax.optimization_barrier((text, one, three, low))
    piece = call(pick_kernel, like(PIECE, D), [SMEM, VMEM])(start, text)
    piece = call(unit_rows_kernel, like(PIECE, D), [SMEM] + [VMEM] * 2)(start, piece, shift(piece, "zl", 1, 2))

    pieces = [piece] + [along(piece, False, d) for d in (1, 2, 3)]
    chunk = call(gather_kernel, like(CHUNK, D), [VMEM] * 4)(*pieces)
    own = [chunk] + [along(chunk, True, d) for d in (1, 2, 3)]
    *own, high = lax.optimization_barrier((*own, high))
    theirs = [shift(chunk, "c", 1, 2) for chunk in own]
    images = call(unit_columns_kernel, like(D, ROWS), [VMEM] * 5, moved=3)(near, one, three, low, high)

    text_scratch, owner_scratch = pltpu.VMEM((ROWS, D), BF16), pltpu.VMEM((2,) + OWNED, F32)
    kept, sent, square = like(*OWNED, dtype=F32), like(*OWNED), like(ROWS, ROWS)
    keep_own, send_own, grad = call(
        own_kernel,
        [kept, sent, like(D, ROWS, dtype=F32)],
        scalar_specs + [VMEM] * 5,
        [text_scratch, pltpu.VMEM((ROWS, ROWS), BF16), owner_scratch],
        products=3,
        moved=8,
    )(*scalars, *own, images)
    keep_other, send_other, weights = call(
        other_kernel,
        [kept, sent, square],
        scalar_specs + [VMEM] * 5,
        [text_scratch, owner_scratch],
        products=2,
        moved=5,
    )(*scalars, *theirs, images)
    pieces = call(
        pieces_kernel,
        [like(PART, ROWS)] * PEERS,
        [VMEM] * 6,
        [text_scratch, pltpu.VMEM((D, ROWS), F32)],
        products=1,
        moved=5,
    )(*theirs, weights, grad)
    *pieces, keep_own = lax.optimization_barrier((*pieces, keep_own))
    returned = [pieces[0]] + [shift(pieces[d], "t", d, PEERS) for d in (1, 2, 3)]

    parts = call(
        join_kernel, [like(4, PIECE, D, dtype=F32)] + [like(4, PIECE, D)] * 3, [VMEM] * 4, moved=4
    )(keep_own, shift(send_other, "c", 1, 2), keep_other, shift(send_own, "c", 1, 2))
    parts = [parts[0]] + [along(parts[d], True, d) for d in (1, 2, 3)]
    *parts, returned[1], returned[3] = lax.optimization_barrier((*parts, returned[1], returned[3]))
    parts = call(
        first_sum_kernel,
        [like(PIECE, D, dtype=F32)] + [like(PIECE, D)] * 3,
        [VMEM] * 4,
        [pltpu.VMEM((4, PIECE, D), F32)],
    )(*parts)
    parts = [parts[0]] + [along(parts[d], False, d) for d in (1, 2, 3)]
    keep, send = call(
        second_sum_kernel, [like(2, 8, D, dtype=F32)] * 2, [SMEM] + [VMEM] * 4, [pltpu.VMEM((PIECE, D), F32)]
    )(start, *parts)
    text_grad = keep + shift(send, "zl", 1, 2)
    return lay(returned).T, text_grad[:, None]


def solution(mesh):
    names, sizes = zip(*SIZES)
    grid = Mesh(mesh.devices.reshape(sizes), names)
    return jax.shard_map(
        per_device,
        mesh=grid,
        in_specs=(P(DP, "t"), P(names, None), P(), P(), P()),
        out_specs=(P(DP, "t"), P(None, "t", DP, None)),
        check_vma=False,
    )
```

time: 143 us -> 121 us (0.85); the launches traced: 143 us -> 119 us
  local copies, waits for them, and re-layouts: 23.8 us -> 2.02 us
  Pallas kernels: 0 us -> 12.6 us
  matrix products: 10.5 us -> 0 us
  waiting for transfers between devices: 43.5 us -> 36.3 us
  starting transfers between devices: 59.3 us -> 64.8 us
  other arithmetic: 2.65 us -> 0.64 us
    ppermute x0 -> x12, starting transfers between devices: none -> 18.7 us  [along(): return lax.ppermute(value, DP, pairs)]
    all_to_all x3 -> x1, waiting for transfers between devices: 16 us -> 0.01 us  [per_device(): lax.all_to_all(text.reshape(16, PIECE, D), ('x', 'y'), split_axis=0, conc...]
    pallas_call x0 -> x13, Pallas kernels: none -> 12.6 us  [the longest x1 4.11 us: per_device(): call(own_kernel, [kept, sent, like(D, ROWS, dtype=F32)], scalar_specs + [...]
    all_to_all x3 -> x1, starting transfers between devices: 18.4 us -> 7.73 us  [per_device(): lax.all_to_all(text.reshape(16, PIECE, D), ('x', 'y'), split_axis=0, conc...]
    dot_general x6 -> x0, matrix products: 10.5 us -> none  [the longest x2 5.18 us: per_device(): lax.dot_general(weights, images, (((1,), (1,)), ((), ())), preferred_elem...]
    unnamed x29 -> x12, local copies, waits for them, and re-layouts: 12.1 us -> 2.02 us
    ppermute x0 -> x12, waiting for transfers between devices: none -> 5.53 us  [along(): return lax.ppermute(value, DP, pairs)]
    dynamic_slice x2 -> x0, local copies, waits for them, and re-layouts: 3.78 us -> none  [the longest x1 2.43 us: pick(): return lax.dynamic_index_in_dim(parts, index, 0, keepdims=False)]
  transfers between devices with their start and end apart: 14 -> 28, of which waited for: 8 -> 12; matrix products, arithmetic and copies ran while one was open for 16% -> 0% of each run, Pallas kernels for 0% -> 9%
where the time goes in v4:
time: 121 us; the launch traced here: 119 us
  starting transfers between devices  64.8 us (54%)
  waiting for transfers between devices  36.3 us (30%)
  Pallas kernels  12.6 us (10%)
  between operations  2.77 us (2%)
  local copies, waits for them, and re-layouts  2.02 us (2%)
    ppermute x15, starting transfers between devices, shift(): lax.ppermute(value, axis, [(i, (i + by) % size) for i in range(size)])  38.3 us
    ppermute x15, waiting for transfers between devices, shift(): lax.ppermute(value, axis, [(i, (i + by) % size) for i in range(size)])  30.7 us
    ppermute x12, starting transfers between devices, along(): return lax.ppermute(value, DP, pairs)  18.7 us
    all_to_all x1, starting transfers between devices, per_device(): lax.all_to_all(text.reshape(16, PIECE, D), ('x', 'y'), split_axis=0, conc...  7.73 us
    ppermute x12, waiting for transfers between devices, along(): return lax.ppermute(value, DP, pairs)  5.53 us
    pallas_call x1, Pallas kernels, per_device(): call(own_kernel, [kept, sent, like(D, ROWS, dtype=F32)], scalar_specs + [...  4.11 us
    pallas_call x1, Pallas kernels, per_device(): call(other_kernel, [kept, sent, square], scalar_specs + [VMEM] * 5, [text...  2.55 us
  transfers between devices with their start and end apart: 28, of which 12 were waited for; matrix products, arithmetic and copies ran while one was open for 0% of the time, Pallas kernels for 9%

profile of v4, /device:TPU:1, one launch (start us, length us, event | category | flops | bytes accessed | tf_op | source)
XLA Modules:
  0.0 119.0 jit_solution(9328440732070716822)
XLA Ops:
  1.9 1.5 %shard_map.68 = bf16[4,4,2,16,1152]{4,3,2,1,0:T(8,128)(2,1)} custom-call(bf16[4,2,4,16,1152]{4,3,2,1,0:T(8,128)(2,1)S(1)} %bitcast.20), custom_call_target="tpu_custom_call" | custom-call | bytes 2097152 | tf_op jit(solution)/shard_map/pallas_call | solution.py:262
  3.4 7.7 %all-to-all-start = ((bf16[16,32,1152]{2,1,0:T(8,128)(2,1)}), bf16[16,32,1152]{2,1,0:T(8,128)(2,1)S(1)}, u32[]{:S(2)}, u32[]{:S(2)}) async-start(bf16[16,32,1152]{2,1,0:T(8,128)(2,1)} %bitcast.2), calls=%async_computation | async-start | bytes 2359296 | tf_op jit(solution)/shard_map/all_to_all | solution.py:263
  11.3 3.1 %collective-permute-start = (bf16[288,512]{1,0:T(8,128)(2,1)S(1)}, bf16[288,512]{1,0:T(8,128)(2,1)S(1)}, u32[]{:S(2)}, u32[]{:S(2)}) collective-permute-start(bf16[288,512]{1,0:T(8,128)(2,1)S(1)} %get-tuple-element.47), channel_id=1, source_target_pairs={{0,1},{1,2},{2,3},{3,0},{4,5},{5,6},{6,7},{7,4},{8,9},{9,10},{10,1... | collective-permute-start | bytes 884744 | tf_op jit(solution)/shard_map/ppermute | solution.py:40
  14.4 3.1 %collective-permute-start.1 = (bf16[288,512]{1,0:T(8,128)(2,1)S(1)}, bf16[288,512]{1,0:T(8,128)(2,1)S(1)}, u32[]{:S(2)}, u32[]{:S(2)}) collective-permute-start(bf16[288,512]{1,0:T(8,128)(2,1)S(1)} %get-tuple-element.48), channel_id=1, source_target_pairs={{0,3},{1,0},{2,1},{3,2},{4,7},{5,4},{6,5},{7,6},{8,11},{9,8},{10,9... | collective-permute-start | bytes 884744 | tf_op jit(solution)/shard_map/ppermute | solution.py:40
  17.5 4.4 %collective-permute-start.2 = (bf16[288,256]{1,0:T(8,128)(2,1)S(1)}, bf16[288,256]{1,0:T(8,128)(2,1)S(1)}, u32[]{:S(2)}, u32[]{:S(2)}) collective-permute-start(bf16[288,256]{1,0:T(8,128)(2,1)S(1)} %get-tuple-element.49), channel_id=1, source_target_pairs={{0,2},{1,3},{2,0},{3,1},{4,6},{5,7},{6,4},{7,5},{8,10},{9,11},{10,... | collective-permute-start | bytes 442376 | tf_op jit(solution)/shard_map/ppermute | solution.py:40
  22.5 9.2 %collective-permute-done.2.two_low = bf16[288,256]{1,0:T(8,128)(2,1)S(1)} collective-permute-done((bf16[288,256]{1,0:T(8,128)(2,1)S(1)}, bf16[288,256]{1,0:T(8,128)(2,1)S(1)}, u32[]{:S(2)}, u32[]{:S(2)}) %collective-permute-start.2) | collective-permute-done | bytes 147488 | tf_op jit(solution)/shard_map/ppermute | solution.py:40
  31.7 4.0 %collective-permute-done.1.three = bf16[288,512]{1,0:T(8,128)(2,1)S(1)} collective-permute-done((bf16[288,512]{1,0:T(8,128)(2,1)S(1)}, bf16[288,512]{1,0:T(8,128)(2,1)S(1)}, u32[]{:S(2)}, u32[]{:S(2)}) %collective-permute-start.1) | collective-permute-done | bytes 294944 | tf_op jit(solution)/shard_map/ppermute | solution.py:40
  35.7 5.8 %collective-permute-start.3 = (bf16[32,1152]{1,0:T(8,128)(2,1)S(1)}, bf16[32,1152]{1,0:T(8,128)(2,1)S(1)}, u32[]{:S(2)}, u32[]{:S(2)}) collective-permute-start(bf16[32,1152]{1,0:T(8,128)(2,1)S(1)} %shard_map.70.here), channel_id=1, source_target_pairs={{0,32},{32,0},{1,33},{33,1},{2,34},{34,2},{3,35},{35,3},{4,36},{36... | collective-permute-start | bytes 221192 | tf_op jit(solution)/shard_map/ppermute | solution.py:40
  41.5 1.7 %collective-permute-done.3.there = bf16[32,1152]{1,0:T(8,128)(2,1)S(1)} collective-permute-done((bf16[32,1152]{1,0:T(8,128)(2,1)S(1)}, bf16[32,1152]{1,0:T(8,128)(2,1)S(1)}, u32[]{:S(2)}, u32[]{:S(2)}) %collective-permute-start.3) | collective-permute-done | bytes 73760 | tf_op jit(solution)/shard_map/ppermute | solution.py:40
  44.6 2.4 %collective-permute-start.5 = (bf16[32,1152]{1,0:T(8,128)(2,1)S(1)}, bf16[32,1152]{1,0:T(8,128)(2,1)S(1)}, u32[]{:S(2)}, u32[]{:S(2)}) collective-permute-start(bf16[32,1152]{1,0:T(8,128)(2,1)S(1)} %shard_map.71.refs_0_), channel_id=1, source_target_pairs={{0,16},{4,132},{8,24},{12,140},{16,0},{20,148},{24,8},{28,156},{32... | collective-permute-start | bytes 221192 | tf_op jit(solution)/shard_map/ppermute | solution.py:52
  51.5 2.4 %collective-permute-start.8 = (bf16[128,1152]{1,0:T(8,128)(2,1)S(1)}, bf16[128,1152]{1,0:T(8,128)(2,1)S(1)}, u32[]{:S(2)}, u32[]{:S(2)}) collective-permute-start(bf16[128,1152]{1,0:T(8,128)(2,1)S(1)} %shard_map.72.refs_0_), channel_id=1, source_target_pairs={{0,128},{4,20},{8,136},{12,28},{16,144},{20,4},{24,152},{28,12},{3... | collective-permute-start | bytes 884744 | tf_op jit(solution)/shard_map/ppermute | solution.py:52
  55.1 1.5 %collective-permute-start.10 = (bf16[288,256]{1,0:T(8,128)(2,1)S(1)}, bf16[288,256]{1,0:T(8,128)(2,1)S(1)}, u32[]{:S(2)}, u32[]{:S(2)}) collective-permute-start(bf16[288,256]{1,0:T(8,128)(2,1)S(1)} %get-tuple-element.51), channel_id=1, source_target_pairs={{0,2},{1,3},{2,0},{3,1},{4,6},{5,7},{6,4},{7,5},{8,10},{9,11},{10,... | collective-permute-start | bytes 442376 | tf_op jit(solution)/shard_map/ppermute | solution.py:40
  56.5 6.9 %collective-permute-done.10.two_high = bf16[288,256]{1,0:T(8,128)(2,1)S(1)} collective-permute-done((bf16[288,256]{1,0:T(8,128)(2,1)S(1)}, bf16[288,256]{1,0:T(8,128)(2,1)S(1)}, u32[]{:S(2)}, u32[]{:S(2)}) %collective-permute-start.10) | collective-permute-done | bytes 147488 | tf_op jit(solution)/shard_map/ppermute | solution.py:40
  63.4 5.9 %collective-permute-start.11 = (bf16[128,1152]{1,0:T(8,128)(2,1)S(1)}, bf16[128,1152]{1,0:T(8,128)(2,1)S(1)}, u32[]{:S(2)}, u32[]{:S(2)}) collective-permute-start(bf16[128,1152]{1,0:T(8,128)(2,1)S(1)} %shard_map.72.refs_0_), channel_id=1, source_target_pairs={{0,4},{4,0},{1,5},{5,1},{2,6},{6,2},{3,7},{7,3},{8,12},{12,8},{9,1... | collective-permute-start | bytes 884744 | tf_op jit(solution)/shard_map/ppermute | solution.py:40
  71.6 4.1 %shard_map.75 = (f32[16,16,1152]{2,1,0:T(8,128)S(1)}, bf16[16,16,1152]{2,1,0:T(8,128)(2,1)S(1)}, f32[1152,512]{1,0:T(8,128)S(1)}) custom-call(s32[1]{0:T(128)} %bitcast.14.start, f32[1]{0:T(128)} %bitcast.17.multiplier, f32[1]{0:T(128)} %bitcast.19.offset, bf16[128,1152]{1,0:T(8,128)(2,1)S(1)} %shard_map.72.refs_0_, ...), custom_call_target="tpu_custom_call" | custom-call | flops 1811939328 | bytes 8388608 | tf_op jit(solution)/shard_map/pallas_call | solution.py:277
  76.2 2.5 %shard_map.74 = (f32[16,16,1152]{2,1,0:T(8,128)S(1)}, bf16[16,16,1152]{2,1,0:T(8,128)(2,1)S(1)}, bf16[512,512]{1,0:T(8,128)(2,1)S(1)}) custom-call(s32[1]{0:T(128)} %bitcast.13.start, f32[1]{0:T(128)} %bitcast.16.multiplier, f32[1]{0:T(128)} %bitcast.18.offset, bf16[128,1152]{1,0:T(8,128)(2,1)S(1)} %collective-permute-done.11.refs_0_, ...), custom_call_target="tpu_custom_call" | custom-call | flops 1207959552 | bytes 5242880 | tf_op jit(solution)/shard_map/pallas_call | solution.py:285
  80.0 3.7 %collective-permute-start.20 = (bf16[288,512]{1,0:T(8,128)(2,1)S(1)}, bf16[288,512]{1,0:T(8,128)(2,1)S(1)}, u32[]{:S(2)}, u32[]{:S(2)}) collective-permute-start(bf16[288,512]{1,0:T(8,128)(2,1)S(1)} %get-tuple-element.77), channel_id=1, source_target_pairs={{0,1},{1,2},{2,3},{3,0},{4,5},{5,6},{6,7},{7,4},{8,9},{9,10},{10,1... | collective-permute-start | bytes 884744 | tf_op jit(solution)/shard_map/ppermute | solution.py:40
  83.9 2.2 %collective-permute-start.17 = (bf16[4,32,1152]{2,1,0:T(8,128)(2,1)S(1)}, bf16[4,32,1152]{2,1,0:T(8,128)(2,1)S(1)}, u32[]{:S(2)}, u32[]{:S(2)}) collective-permute-start(bf16[4,32,1152]{2,1,0:T(8,128)(2,1)S(1)} %get-tuple-element.74), channel_id=1, source_target_pairs={{0,64},{4,12},{8,72},{12,20},{16,80},{20,28},{24,88},{28,4},{32,96... | collective-permute-start | bytes 884744 | tf_op jit(solution)/shard_map/ppermute | solution.py:52
  86.1 2.0 %collective-permute-start.18 = (bf16[4,32,1152]{2,1,0:T(8,128)(2,1)S(1)}, bf16[4,32,1152]{2,1,0:T(8,128)(2,1)S(1)}, u32[]{:S(2)}, u32[]{:S(2)}) collective-permute-start(bf16[4,32,1152]{2,1,0:T(8,128)(2,1)S(1)} %get-tuple-element.75), channel_id=1, source_target_pairs={{0,128},{4,20},{8,136},{12,28},{16,144},{20,4},{24,152},{28,12},{3... | collective-permute-start | bytes 884744 | tf_op jit(solution)/shard_map/ppermute | solution.py:52
  88.6 6.9 %collective-permute-done.20.refs_1_ = bf16[288,512]{1,0:T(8,128)(2,1)S(1)} collective-permute-done((bf16[288,512]{1,0:T(8,128)(2,1)S(1)}, bf16[288,512]{1,0:T(8,128)(2,1)S(1)}, u32[]{:S(2)}, u32[]{:S(2)}) %collective-permute-start.20) | collective-permute-done | bytes 294944 | tf_op jit(solution)/shard_map/ppermute | solution.py:40
  98.0 3.7 %collective-permute-start.24 = (bf16[32,1152]{1,0:T(8,128)(2,1)S(1)}, bf16[32,1152]{1,0:T(8,128)(2,1)S(1)}, u32[]{:S(2)}, u32[]{:S(2)}) collective-permute-start(bf16[32,1152]{1,0:T(8,128)(2,1)S(1)} %get-tuple-element.88), channel_id=1, source_target_pairs={{0,16},{4,132},{8,24},{12,140},{16,0},{20,148},{24,8},{28,156},{32... | collective-permute-start | bytes 221192 | tf_op jit(solution)/shard_map/ppermute | solution.py:52
  102.2 2.0 %collective-permute-done.24.two = bf16[32,1152]{1,0:T(8,128)(2,1)S(1)} collective-permute-done((bf16[32,1152]{1,0:T(8,128)(2,1)S(1)}, bf16[32,1152]{1,0:T(8,128)(2,1)S(1)}, u32[]{:S(2)}, u32[]{:S(2)}) %collective-permute-start.24) | collective-permute-done | bytes 73760 | tf_op jit(solution)/shard_map/ppermute | solution.py:52
  104.9 8.4 %collective-permute-start.26 = (f32[2,8,1152]{2,1,0:T(8,128)S(1)}, f32[2,8,1152]{2,1,0:T(8,128)S(1)}, u32[]{:S(2)}, u32[]{:S(2)}) collective-permute-start(f32[2,8,1152]{2,1,0:T(8,128)S(1)} %get-tuple-element.91), channel_id=1, source_target_pairs={{0,32},{32,0},{1,33},{33,1},{2,34},{34,2},{3,35},{35,3},{4,36},{36... | collective-permute-start | bytes 221192 | tf_op jit(solution)/shard_map/ppermute | solution.py:40
  114.7 2.3 %shard_map.78 = bf16[288,2048]{1,0:T(8,128)(2,1)} custom-call(bf16[288,512]{1,0:T(8,128)(2,1)} %copy-done.2, bf16[288,512]{1,0:T(8,128)(2,1)} %copy-done.3, bf16[288,512]{1,0:T(8,128)(2,1)} %copy-done.5, bf16[288,512]{1,0:T(8,128)(2,1)} %copy-done.4), custom_call_target="tpu_custom_call" | custom-call | tf_op jit(solution)/shard_map/pallas_call | solution.py:245
  (58 shorter events, 19.0 us)
Async XLA Ops:
  3.4 32.3 %all-to-all-start = ((bf16[16,32,1152]{2,1,0:T(8,128)(2,1)}), bf16[16,32,1152]{2,1,0:T(8,128)(2,1)S(1)}, u32[]{:S(2)}, u32[]{:S(2)}) async-start(bf16[16,32,1152]{2,1,0:T(8,128)(2,1)} %bitcast.2), calls=%async_computation | async-start | bytes 2359296 | tf_op jit(solution)/shard_map/all_to_all | solution.py:263
  11.3 20.4 %collective-permute-start = (bf16[288,512]{1,0:T(8,128)(2,1)S(1)}, bf16[288,512]{1,0:T(8,128)(2,1)S(1)}, u32[]{:S(2)}, u32[]{:S(2)}) collective-permute-start(bf16[288,512]{1,0:T(8,128)(2,1)S(1)} %get-tuple-element.47), channel_id=1, source_target_pairs={{0,1},{1,2},{2,3},{3,0},{4,5},{5,6},{6,7},{7,4},{8,9},{9,10},{10,1... | collective-permute-start | bytes 884744 | tf_op jit(solution)/shard_map/ppermute | solution.py:40
  14.4 21.3 %collective-permute-start.1 = (bf16[288,512]{1,0:T(8,128)(2,1)S(1)}, bf16[288,512]{1,0:T(8,128)(2,1)S(1)}, u32[]{:S(2)}, u32[]{:S(2)}) collective-permute-start(bf16[288,512]{1,0:T(8,128)(2,1)S(1)} %get-tuple-element.48), channel_id=1, source_target_pairs={{0,3},{1,0},{2,1},{3,2},{4,7},{5,4},{6,5},{7,6},{8,11},{9,8},{10,9... | collective-permute-start | bytes 884744 | tf_op jit(solution)/shard_map/ppermute | solution.py:40
  17.5 14.2 %collective-permute-start.2 = (bf16[288,256]{1,0:T(8,128)(2,1)S(1)}, bf16[288,256]{1,0:T(8,128)(2,1)S(1)}, u32[]{:S(2)}, u32[]{:S(2)}) collective-permute-start(bf16[288,256]{1,0:T(8,128)(2,1)S(1)} %get-tuple-element.49), channel_id=1, source_target_pairs={{0,2},{1,3},{2,0},{3,1},{4,6},{5,7},{6,4},{7,5},{8,10},{9,11},{10,... | collective-permute-start | bytes 442376 | tf_op jit(solution)/shard_map/ppermute | solution.py:40
  35.7 7.6 %collective-permute-start.3 = (bf16[32,1152]{1,0:T(8,128)(2,1)S(1)}, bf16[32,1152]{1,0:T(8,128)(2,1)S(1)}, u32[]{:S(2)}, u32[]{:S(2)}) collective-permute-start(bf16[32,1152]{1,0:T(8,128)(2,1)S(1)} %shard_map.70.here), channel_id=1, source_target_pairs={{0,32},{32,0},{1,33},{33,1},{2,34},{34,2},{3,35},{35,3},{4,36},{36... | collective-permute-start | bytes 221192 | tf_op jit(solution)/shard_map/ppermute | solution.py:40
  44.6 4.9 %collective-permute-start.5 = (bf16[32,1152]{1,0:T(8,128)(2,1)S(1)}, bf16[32,1152]{1,0:T(8,128)(2,1)S(1)}, u32[]{:S(2)}, u32[]{:S(2)}) collective-permute-start(bf16[32,1152]{1,0:T(8,128)(2,1)S(1)} %shard_map.71.refs_0_), channel_id=1, source_target_pairs={{0,16},{4,132},{8,24},{12,140},{16,0},{20,148},{24,8},{28,156},{32... | collective-permute-start | bytes 221192 | tf_op jit(solution)/shard_map/ppermute | solution.py:52
  50.5 12.9 %collective-permute-start.7 = (bf16[128,1152]{1,0:T(8,128)(2,1)S(1)}, bf16[128,1152]{1,0:T(8,128)(2,1)S(1)}, u32[]{:S(2)}, u32[]{:S(2)}) collective-permute-start(bf16[128,1152]{1,0:T(8,128)(2,1)S(1)} %shard_map.72.refs_0_), channel_id=1, source_target_pairs={{0,64},{4,12},{8,72},{12,20},{16,80},{20,28},{24,88},{28,4},{32,96... | collective-permute-start | bytes 884744 | tf_op jit(solution)/shard_map/ppermute | solution.py:52
  51.5 11.9 %collective-permute-start.8 = (bf16[128,1152]{1,0:T(8,128)(2,1)S(1)}, bf16[128,1152]{1,0:T(8,128)(2,1)S(1)}, u32[]{:S(2)}, u32[]{:S(2)}) collective-permute-start(bf16[128,1152]{1,0:T(8,128)(2,1)S(1)} %shard_map.72.refs_0_), channel_id=1, source_target_pairs={{0,128},{4,20},{8,136},{12,28},{16,144},{20,4},{24,152},{28,12},{3... | collective-permute-start | bytes 884744 | tf_op jit(solution)/shard_map/ppermute | solution.py:52
  53.9 9.5 %collective-permute-start.9 = (bf16[128,1152]{1,0:T(8,128)(2,1)S(1)}, bf16[128,1152]{1,0:T(8,128)(2,1)}, u32[]{:S(2)}, u32[]{:S(2)}) collective-permute-start(bf16[128,1152]{1,0:T(8,128)(2,1)S(1)} %shard_map.72.refs_0_), channel_id=1, source_target_pairs={{0,192},{4,28},{8,200},{12,4},{16,208},{20,12},{24,216},{28,20},{3... | collective-permute-start | bytes 884744 | tf_op jit(solution)/shard_map/ppermute | solution.py:52
  55.1 8.3 %collective-permute-start.10 = (bf16[288,256]{1,0:T(8,128)(2,1)S(1)}, bf16[288,256]{1,0:T(8,128)(2,1)S(1)}, u32[]{:S(2)}, u32[]{:S(2)}) collective-permute-start(bf16[288,256]{1,0:T(8,128)(2,1)S(1)} %get-tuple-element.51), channel_id=1, source_target_pairs={{0,2},{1,3},{2,0},{3,1},{4,6},{5,7},{6,4},{7,5},{8,10},{9,11},{10,... | collective-permute-start | bytes 442376 | tf_op jit(solution)/shard_map/ppermute | solution.py:40
  63.4 12.8 %collective-permute-start.11 = (bf16[128,1152]{1,0:T(8,128)(2,1)S(1)}, bf16[128,1152]{1,0:T(8,128)(2,1)S(1)}, u32[]{:S(2)}, u32[]{:S(2)}) collective-permute-start(bf16[128,1152]{1,0:T(8,128)(2,1)S(1)} %shard_map.72.refs_0_), channel_id=1, source_target_pairs={{0,4},{4,0},{1,5},{5,1},{2,6},{6,2},{3,7},{7,3},{8,12},{12,8},{9,1... | collective-permute-start | bytes 884744 | tf_op jit(solution)/shard_map/ppermute | solution.py:40
  69.3 6.8 %collective-permute-start.12 = (bf16[128,1152]{1,0:T(8,128)(2,1)S(1)}, bf16[128,1152]{1,0:T(8,128)(2,1)S(1)}, u32[]{:S(2)}, u32[]{:S(2)}) collective-permute-start(bf16[128,1152]{1,0:T(8,128)(2,1)S(1)} %collective-permute-done.7.refs_1_), channel_id=1, source_target_pairs={{0,4},{4,0},{1,5},{5,1},{2,6},{6,2},{3,7},{7,3},{8,12},{12,8},{9,1... | collective-permute-start | bytes 884744 | tf_op jit(solution)/shard_map/ppermute | solution.py:40
  69.4 6.7 %collective-permute-start.13 = (bf16[128,1152]{1,0:T(8,128)(2,1)S(1)}, bf16[128,1152]{1,0:T(8,128)(2,1)S(1)}, u32[]{:S(2)}, u32[]{:S(2)}) collective-permute-start(bf16[128,1152]{1,0:T(8,128)(2,1)S(1)} %collective-permute-done.8.refs_2_), channel_id=1, source_target_pairs={{0,4},{4,0},{1,5},{5,1},{2,6},{6,2},{3,7},{7,3},{8,12},{12,8},{9,1... | collective-permute-start | bytes 884744 | tf_op jit(solution)/shard_map/ppermute | solution.py:40
  69.9 6.3 %collective-permute-start.14 = (bf16[128,1152]{1,0:T(8,128)(2,1)}, bf16[128,1152]{1,0:T(8,128)(2,1)S(1)}, u32[]{:S(2)}, u32[]{:S(2)}) collective-permute-start(bf16[128,1152]{1,0:T(8,128)(2,1)} %collective-permute-done.9.refs_3_), channel_id=1, source_target_pairs={{0,4},{4,0},{1,5},{5,1},{2,6},{6,2},{3,7},{7,3},{8,12},{12,8},{9,1... | collective-permute-start | bytes 884744 | tf_op jit(solution)/shard_map/ppermute | solution.py:40
  75.7 8.0 %collective-permute-start.16 = (bf16[16,16,1152]{2,1,0:T(8,128)(2,1)S(1)}, bf16[16,16,1152]{2,1,0:T(8,128)(2,1)S(1)}, u32[]{:S(2)}, u32[]{:S(2)}) collective-permute-start(bf16[16,16,1152]{2,1,0:T(8,128)(2,1)S(1)} %get-tuple-element.72), channel_id=1, source_target_pairs={{0,4},{4,0},{1,5},{5,1},{2,6},{6,2},{3,7},{7,3},{8,12},{12,8},{9,1... | collective-permute-start | bytes 1769480 | tf_op jit(solution)/shard_map/ppermute | solution.py:40
  80.0 15.5 %collective-permute-start.20 = (bf16[288,512]{1,0:T(8,128)(2,1)S(1)}, bf16[288,512]{1,0:T(8,128)(2,1)S(1)}, u32[]{:S(2)}, u32[]{:S(2)}) collective-permute-start(bf16[288,512]{1,0:T(8,128)(2,1)S(1)} %get-tuple-element.77), channel_id=1, source_target_pairs={{0,1},{1,2},{2,3},{3,0},{4,5},{5,6},{6,7},{7,4},{8,9},{9,10},{10,1... | collective-permute-start | bytes 884744 | tf_op jit(solution)/shard_map/ppermute | solution.py:40
  83.6 13.0 %collective-permute-start.21 = (bf16[288,512]{1,0:T(8,128)(2,1)S(1)}, bf16[288,512]{1,0:T(8,128)(2,1)S(1)}, u32[]{:S(2)}, u32[]{:S(2)}) collective-permute-start(bf16[288,512]{1,0:T(8,128)(2,1)S(1)} %get-tuple-element.78), channel_id=1, source_target_pairs={{0,3},{1,0},{2,1},{3,2},{4,7},{5,4},{6,5},{7,6},{8,11},{9,8},{10,9... | collective-permute-start | bytes 884744 | tf_op jit(solution)/shard_map/ppermute | solution.py:40
  83.9 12.8 %collective-permute-start.17 = (bf16[4,32,1152]{2,1,0:T(8,128)(2,1)S(1)}, bf16[4,32,1152]{2,1,0:T(8,128)(2,1)S(1)}, u32[]{:S(2)}, u32[]{:S(2)}) collective-permute-start(bf16[4,32,1152]{2,1,0:T(8,128)(2,1)S(1)} %get-tuple-element.74), channel_id=1, source_target_pairs={{0,64},{4,12},{8,72},{12,20},{16,80},{20,28},{24,88},{28,4},{32,96... | collective-permute-start | bytes 884744 | tf_op jit(solution)/shard_map/ppermute | solution.py:52
  86.1 10.6 %collective-permute-start.18 = (bf16[4,32,1152]{2,1,0:T(8,128)(2,1)S(1)}, bf16[4,32,1152]{2,1,0:T(8,128)(2,1)S(1)}, u32[]{:S(2)}, u32[]{:S(2)}) collective-permute-start(bf16[4,32,1152]{2,1,0:T(8,128)(2,1)S(1)} %get-tuple-element.75), channel_id=1, source_target_pairs={{0,128},{4,20},{8,136},{12,28},{16,144},{20,4},{24,152},{28,12},{3... | collective-permute-start | bytes 884744 | tf_op jit(solution)/shard_map/ppermute | solution.py:52
  88.1 8.6 %collective-permute-start.19 = (bf16[4,32,1152]{2,1,0:T(8,128)(2,1)S(1)}, bf16[4,32,1152]{2,1,0:T(8,128)(2,1)S(1)}, u32[]{:S(2)}, u32[]{:S(2)}) collective-permute-start(bf16[4,32,1152]{2,1,0:T(8,128)(2,1)S(1)} %get-tuple-element.76), channel_id=1, source_target_pairs={{0,192},{4,28},{8,200},{12,4},{16,208},{20,12},{24,216},{28,20},{3... | collective-permute-start | bytes 884744 | tf_op jit(solution)/shard_map/ppermute | solution.py:52
  95.5 18.5 %collective-permute-start.22 = (bf16[288,512]{1,0:T(8,128)(2,1)S(1)}, bf16[288,512]{1,0:T(8,128)(2,1)S(1)}, u32[]{:S(2)}, u32[]{:S(2)}) collective-permute-start(bf16[288,512]{1,0:T(8,128)(2,1)S(1)} %get-tuple-element.80), channel_id=1, source_target_pairs={{0,2},{1,3},{2,0},{3,1},{4,6},{5,7},{6,4},{7,5},{8,10},{9,11},{10,... | collective-permute-start | bytes 884744 | tf_op jit(solution)/shard_map/ppermute | solution.py:40
  96.9 5.3 %collective-permute-start.23 = (bf16[32,1152]{1,0:T(8,128)(2,1)S(1)}, bf16[32,1152]{1,0:T(8,128)(2,1)S(1)}, u32[]{:S(2)}, u32[]{:S(2)}) collective-permute-start(bf16[32,1152]{1,0:T(8,128)(2,1)S(1)} %get-tuple-element.87), channel_id=1, source_target_pairs={{0,8},{4,68},{8,16},{12,76},{16,24},{20,84},{24,0},{28,92},{32,40}... | collective-permute-start | bytes 221192 | tf_op jit(solution)/shard_map/ppermute | solution.py:52
  98.0 6.2 %collective-permute-start.24 = (bf16[32,1152]{1,0:T(8,128)(2,1)S(1)}, bf16[32,1152]{1,0:T(8,128)(2,1)S(1)}, u32[]{:S(2)}, u32[]{:S(2)}) collective-permute-start(bf16[32,1152]{1,0:T(8,128)(2,1)S(1)} %get-tuple-element.88), channel_id=1, source_target_pairs={{0,16},{4,132},{8,24},{12,140},{16,0},{20,148},{24,8},{28,156},{32... | collective-permute-start | bytes 221192 | tf_op jit(solution)/shard_map/ppermute | solution.py:52
  104.9 13.5 %collective-permute-start.26 = (f32[2,8,1152]{2,1,0:T(8,128)S(1)}, f32[2,8,1152]{2,1,0:T(8,128)S(1)}, u32[]{:S(2)}, u32[]{:S(2)}) collective-permute-start(f32[2,8,1152]{2,1,0:T(8,128)S(1)} %get-tuple-element.91), channel_id=1, source_target_pairs={{0,32},{32,0},{1,33},{33,1},{2,34},{34,2},{3,35},{35,3},{4,36},{36... | collective-permute-start | bytes 221192 | tf_op jit(solution)/shard_map/ppermute | solution.py:40
  (10 other events, 65.9 us)

commit v5 on v4

--- a/solution.py
+++ b/solution.py
@@ -90,16 +90,6 @@
         rows = pl.ds(pl.multiple_of(ahead(mine, d) * ROWS + at, HALF), size)
         copies.append(pltpu.make_async_copy(pictures.at[:, rows], piece, done.at[i]))
     run(copies)
-
-
-def arrange_kernel(captions, text, done):
-    run(
-        [
-            pltpu.make_async_copy(captions.at[x, z], text.at[x, :, z], done.at[2 * x + z])
-            for x in range(4)
-            for z in range(2)
-        ]
-    )
 
 
 def pick_kernel(start, parts, piece):
@@ -151,7 +141,7 @@
         inner, along_first = at >> 5, back(place, d)
         x = jnp.where(kind == 0, along_first, inner)
         y = jnp.where(kind == 0, inner, along_first)
-        row = x * 128 + ((at >> 4) & 1) * 64 + y * 16 + (at & 15)
+        row = x * 128 + y * PIECE + (at & (PIECE - 1))
         same = row == lax.broadcasted_iota(jnp.int32, (CHUNK, ROWS), 1)
         positive = jnp.where(same & held, 1.0, 0.0)
         weights[rows, :] = ((jax.nn.sigmoid(logits) - positive) * times).astype(BF16)
@@ -168,12 +158,16 @@
             preferred_element_type=F32,
         )
         for inner in range(4):
-            straight, turned = back(place, d) * 4 + inner, inner * 4 + back(place, d)
-            spots = (jnp.where(kind == 0, straight, turned), jnp.where(kind == 0, turned, straight))
-            for z in range(2):
+            outer = back(place, d)
+            x = jnp.where(kind == 0, outer, inner)
+            part = jnp.where(kind == 0, inner, outer)
+            rows = pl.ds(pl.multiple_of((part >> 1) * 8, 8), 8)
+            for low in range(2):
+                y = (part & 1) * 2 + low
+                spots = (x * 4 + y, y * 4 + x)
                 for c in range(2):
-                    at = PIECE * inner + 16 * z + 8 * c
-                    by_owner[c, spots[c], 8 * z : 8 * z + 8, :] = terms[at : at + 8, :]
+                    at = PIECE * inner + 16 * low + 8 * c
+                    by_owner[c, spots[c], rows, :] = terms[at : at + 8, :]
     keep[...] = by_owner[core]
     send[...] = by_owner[1 - core].astype(BF16)
 
@@ -230,25 +224,43 @@
         send[at] = total[window(2 * slab + 1 - z_lo, 8), :]
 
 
-def lay_kernel(*refs):
-    pieces, out, done = refs[:4], refs[4], refs[5]
+def lay_copies(places, out, done):
     mine = lax.axis_index("t")
     run(
         [
-            pltpu.make_async_copy(piece, out.at[:, window(back(mine, d), ROWS)], done.at[d])
-            for d, piece in enumerate(pieces)
+            pltpu.make_async_copy(piece, out.at[:, window(back(mine, d), ROWS)], done.at[i])
+            for i, (d, piece) in enumerate(places)
         ]
     )
 
 
-def lay(pieces):
+def lay_near_kernel(own, one, three, out, done):
+    lay_copies([(0, own), (1, one), (3, three)], out, done)
+
+
+def lay_far_kernel(two, before, out, done):
+    lay_copies([(2, two)], out, done)
+
+
+def lay_near(own, one, three):
     return pl.pallas_call(
-        lay_kernel,
+        lay_near_kernel,
         out_shape=like(PART, PEERS * ROWS),
-        in_specs=[VMEM] * PEERS,
+        in_specs=[VMEM] * 3,
         out_specs=HBM,
-        scratch_shapes=[DMA((PEERS,))],
-    )(*pieces)
+        scratch_shapes=[DMA((3,))],
+    )(own, one, three)
+
+
+def lay_far(two, before):
+    return pl.pallas_call(
+        lay_far_kernel,
+        out_shape=like(PART, PEERS * ROWS),
+        in_specs=[VMEM, HBM],
+        out_specs=HBM,
+        scratch_shapes=[DMA((1,))],
+        input_output_aliases={1: 0},
+    )(two, before)
 
 
 def per_device(pictures, captions, start, multiplier, offset):
@@ -259,13 +271,13 @@
     near, one, three, low, high = call(cut_kernel, shapes, [HBM], [DMA((5,))], moved=2)(pictures.T)
     one, three, low, high = (shift(v, "t", d, PEERS) for v, d in ((one, 1), (three, 3), (low, 2), (high, 2)))
 
-    text = call(arrange_kernel, like(4, 4, 2, 16, D), [HBM], [DMA((8,))], moved=2)(captions.reshape(4, 2, 4, 16, D))
-    text = lax.all_to_all(text.reshape(16, PIECE, D), ("x", "y"), split_axis=0, concat_axis=0, tiled=True)
-    text, one, three, low = lax.optimization_barrier((text, one, three, low))
+    text = lax.all_to_all(captions.reshape(16, PIECE, D), ("x", "y"), split_axis=0, concat_axis=0, tiled=True)
+    text, one, three = lax.optimization_barrier((text, one, three))
     piece = call(pick_kernel, like(PIECE, D), [SMEM, VMEM])(start, text)
     piece = call(unit_rows_kernel, like(PIECE, D), [SMEM] + [VMEM] * 2)(start, piece, shift(piece, "zl", 1, 2))
 
     pieces = [piece] + [along(piece, False, d) for d in (1, 2, 3)]
+    *pieces, low = lax.optimization_barrier((*pieces, low))
     chunk = call(gather_kernel, like(CHUNK, D), [VMEM] * 4)(*pieces)
     own = [chunk] + [along(chunk, True, d) for d in (1, 2, 3)]
     *own, high = lax.optimization_barrier((*own, high))
@@ -317,7 +329,8 @@
         second_sum_kernel, [like(2, 8, D, dtype=F32)] * 2, [SMEM] + [VMEM] * 4, [pltpu.VMEM((PIECE, D), F32)]
     )(start, *parts)
     text_grad = keep + shift(send, "zl", 1, 2)
-    return lay(returned).T, text_grad[:, None]
+    image_grad = lay_far(returned[2], lay_near(returned[0], returned[1], returned[3]))
+    return image_grad.T, text_grad[:, None]
 
 
 def solution(mesh):

time: 121 us -> 113 us (0.934)
  starting transfers between devices: 64.8 us -> 59.3 us
  local copies, waits for them, and re-layouts: 2.02 us -> 0.72 us
    ppermute x15, starting transfers between devices: 38.3 us -> 34.6 us  [shift(): lax.ppermute(value, axis, [(i, (i + by) % size) for i in range(size)])]
    ppermute x12, starting transfers between devices: 18.7 us -> 17 us  [along(): return lax.ppermute(value, DP, pairs)]
    ppermute x15, waiting for transfers between devices: 30.7 us -> 29.3 us  [shift(): lax.ppermute(value, axis, [(i, (i + by) % size) for i in range(size)])]
    unnamed x12 -> x10, local copies, waits for them, and re-layouts: 2.02 us -> 0.72 us
  transfers between devices with their start and end apart: 28 -> 28, of which waited for: 12 -> 9; matrix products, arithmetic and copies ran while one was open for 0% -> 0% of each run, Pallas kernels for 9% -> 11%
where the time goes in v5:
time: 113 us; the launch traced here: 111 us
  starting transfers between devices  59.3 us (52%)
  waiting for transfers between devices  35.1 us (31%)
  Pallas kernels  12.6 us (11%)
  between operations  2.8 us (2%)
    ppermute x15, starting transfers between devices, shift(): lax.ppermute(value, axis, [(i, (i + by) % size) for i in range(size)])  34.6 us
    ppermute x15, waiting for transfers between devices, shift(): lax.ppermute(value, axis, [(i, (i + by) % size) for i in range(size)])  29.3 us
    ppermute x12, starting transfers between devices, along(): return lax.ppermute(value, DP, pairs)  17 us
    all_to_all x1, starting transfers between devices, per_device(): lax.all_to_all(captions.reshape(16, PIECE, D), ('x', 'y'), split_axis=0,...  7.73 us
    ppermute x12, waiting for transfers between devices, along(): return lax.ppermute(value, DP, pairs)  5.72 us
    pallas_call x1, Pallas kernels, per_device(): call(own_kernel, [kept, sent, like(D, ROWS, dtype=F32)], scalar_specs + [...  4.12 us
    pallas_call x1, Pallas kernels, per_device(): call(other_kernel, [kept, sent, square], scalar_specs + [VMEM] * 5, [text...  2.51 us
  transfers between devices with their start and end apart: 28, of which 9 were waited for; matrix products, arithmetic and copies ran while one was open for 0% of the time, Pallas kernels for 11%

profile of v5, /device:TPU:1, one launch (start us, length us, event | category | flops | bytes accessed | tf_op | source)
XLA Modules:
  0.0 111.1 jit_solution(7241264006477759074)
XLA Ops:
  0.6 7.7 %all-to-all-start = ((bf16[16,32,1152]{2,1,0:T(8,128)(2,1)}), bf16[16,32,1152]{2,1,0:T(8,128)(2,1)S(1)}, u32[]{:S(2)}, u32[]{:S(2)}) async-start(bf16[16,32,1152]{2,1,0:T(8,128)(2,1)} %bitcast.21), calls=%async_computation | async-start | bytes 2359296 | tf_op jit(solution)/shard_map/all_to_all | solution.py:274
  8.6 3.1 %collective-permute-start = (bf16[288,512]{1,0:T(8,128)(2,1)S(1)}, bf16[288,512]{1,0:T(8,128)(2,1)S(1)}, u32[]{:S(2)}, u32[]{:S(2)}) collective-permute-start(bf16[288,512]{1,0:T(8,128)(2,1)S(1)} %get-tuple-element.51), channel_id=1, source_target_pairs={{0,1},{1,2},{2,3},{3,0},{4,5},{5,6},{6,7},{7,4},{8,9},{9,10},{10,1... | collective-permute-start | bytes 884744 | tf_op jit(solution)/shard_map/ppermute | solution.py:40
  11.6 3.1 %collective-permute-start.1 = (bf16[288,512]{1,0:T(8,128)(2,1)S(1)}, bf16[288,512]{1,0:T(8,128)(2,1)S(1)}, u32[]{:S(2)}, u32[]{:S(2)}) collective-permute-start(bf16[288,512]{1,0:T(8,128)(2,1)S(1)} %get-tuple-element.52), channel_id=1, source_target_pairs={{0,3},{1,0},{2,1},{3,2},{4,7},{5,4},{6,5},{7,6},{8,11},{9,8},{10,9... | collective-permute-start | bytes 884744 | tf_op jit(solution)/shard_map/ppermute | solution.py:40
  15.4 7.3 %collective-permute-done.one = bf16[288,512]{1,0:T(8,128)(2,1)S(1)} collective-permute-done((bf16[288,512]{1,0:T(8,128)(2,1)S(1)}, bf16[288,512]{1,0:T(8,128)(2,1)S(1)}, u32[]{:S(2)}, u32[]{:S(2)}) %collective-permute-start) | collective-permute-done | bytes 294944 | tf_op jit(solution)/shard_map/ppermute | solution.py:40
  22.7 6.4 %collective-permute-done.1.three = bf16[288,512]{1,0:T(8,128)(2,1)S(1)} collective-permute-done((bf16[288,512]{1,0:T(8,128)(2,1)S(1)}, bf16[288,512]{1,0:T(8,128)(2,1)S(1)}, u32[]{:S(2)}, u32[]{:S(2)}) %collective-permute-start.1) | collective-permute-done | bytes 294944 | tf_op jit(solution)/shard_map/ppermute | solution.py:40
  29.2 3.6 %collective-permute-start.6 = (bf16[288,256]{1,0:T(8,128)(2,1)S(1)}, bf16[288,256]{1,0:T(8,128)(2,1)S(1)}, u32[]{:S(2)}, u32[]{:S(2)}) collective-permute-start(bf16[288,256]{1,0:T(8,128)(2,1)S(1)} %get-tuple-element.54), channel_id=1, source_target_pairs={{0,2},{1,3},{2,0},{3,1},{4,6},{5,7},{6,4},{7,5},{8,10},{9,11},{10,... | collective-permute-start | bytes 442376 | tf_op jit(solution)/shard_map/ppermute | solution.py:40
  34.0 2.4 %collective-permute-start.4 = (bf16[32,1152]{1,0:T(8,128)(2,1)S(1)}, bf16[32,1152]{1,0:T(8,128)(2,1)S(1)}, u32[]{:S(2)}, u32[]{:S(2)}) collective-permute-start(bf16[32,1152]{1,0:T(8,128)(2,1)S(1)} %shard_map.70.refs_0_), channel_id=1, source_target_pairs={{0,16},{4,132},{8,24},{12,140},{16,0},{20,148},{24,8},{28,156},{32... | collective-permute-start | bytes 221192 | tf_op jit(solution)/shard_map/ppermute | solution.py:52
  37.6 1.3 %collective-permute-done.4.refs_2_ = bf16[32,1152]{1,0:T(8,128)(2,1)S(1)} collective-permute-done((bf16[32,1152]{1,0:T(8,128)(2,1)S(1)}, bf16[32,1152]{1,0:T(8,128)(2,1)S(1)}, u32[]{:S(2)}, u32[]{:S(2)}) %collective-permute-start.4) | collective-permute-done | bytes 73760 | tf_op jit(solution)/shard_map/ppermute | solution.py:52
  39.9 1.3 %collective-permute-start.7 = (bf16[128,1152]{1,0:T(8,128)(2,1)S(1)}, bf16[128,1152]{1,0:T(8,128)(2,1)S(1)}, u32[]{:S(2)}, u32[]{:S(2)}) collective-permute-start(bf16[128,1152]{1,0:T(8,128)(2,1)S(1)} %shard_map.71.refs_0_), channel_id=1, source_target_pairs={{0,64},{4,12},{8,72},{12,20},{16,80},{20,28},{24,88},{28,4},{32,96... | collective-permute-start | bytes 884744 | tf_op jit(solution)/shard_map/ppermute | solution.py:52
  41.2 2.4 %collective-permute-start.8 = (bf16[128,1152]{1,0:T(8,128)(2,1)S(1)}, bf16[128,1152]{1,0:T(8,128)(2,1)S(1)}, u32[]{:S(2)}, u32[]{:S(2)}) collective-permute-start(bf16[128,1152]{1,0:T(8,128)(2,1)S(1)} %shard_map.71.refs_0_), channel_id=1, source_target_pairs={{0,128},{4,20},{8,136},{12,28},{16,144},{20,4},{24,152},{28,12},{3... | collective-permute-start | bytes 884744 | tf_op jit(solution)/shard_map/ppermute | solution.py:52
  44.8 2.8 %collective-permute-start.10 = (bf16[288,256]{1,0:T(8,128)(2,1)S(1)}, bf16[288,256]{1,0:T(8,128)(2,1)S(1)}, u32[]{:S(2)}, u32[]{:S(2)}) collective-permute-start(bf16[288,256]{1,0:T(8,128)(2,1)S(1)} %get-tuple-element.59), channel_id=1, source_target_pairs={{0,2},{1,3},{2,0},{3,1},{4,6},{5,7},{6,4},{7,5},{8,10},{9,11},{10,... | collective-permute-start | bytes 442376 | tf_op jit(solution)/shard_map/ppermute | solution.py:40
  47.5 5.1 %collective-permute-done.10.two_high = bf16[288,256]{1,0:T(8,128)(2,1)S(1)} collective-permute-done((bf16[288,256]{1,0:T(8,128)(2,1)S(1)}, bf16[288,256]{1,0:T(8,128)(2,1)S(1)}, u32[]{:S(2)}, u32[]{:S(2)}) %collective-permute-start.10) | collective-permute-done | bytes 147488 | tf_op jit(solution)/shard_map/ppermute | solution.py:40
  52.7 6.4 %collective-permute-start.11 = (bf16[128,1152]{1,0:T(8,128)(2,1)S(1)}, bf16[128,1152]{1,0:T(8,128)(2,1)S(1)}, u32[]{:S(2)}, u32[]{:S(2)}) collective-permute-start(bf16[128,1152]{1,0:T(8,128)(2,1)S(1)} %shard_map.71.refs_0_), channel_id=1, source_target_pairs={{0,4},{4,0},{1,5},{5,1},{2,6},{6,2},{3,7},{7,3},{8,12},{12,8},{9,1... | collective-permute-start | bytes 884744 | tf_op jit(solution)/shard_map/ppermute | solution.py:40
  61.3 4.1 %shard_map.74 = (f32[16,16,1152]{2,1,0:T(8,128)S(1)}, bf16[16,16,1152]{2,1,0:T(8,128)(2,1)S(1)}, f32[1152,512]{1,0:T(8,128)S(1)}) custom-call(s32[1]{0:T(128)} %bitcast.13.start, f32[1]{0:T(128)} %bitcast.16.multiplier, f32[1]{0:T(128)} %bitcast.18.offset, bf16[128,1152]{1,0:T(8,128)(2,1)S(1)} %shard_map.71.refs_0_, ...), custom_call_target="tpu_custom_call" | custom-call | flops 1811939328 | bytes 8388608 | tf_op jit(solution)/shard_map/pallas_call | solution.py:289
  65.9 2.5 %shard_map.73 = (f32[16,16,1152]{2,1,0:T(8,128)S(1)}, bf16[16,16,1152]{2,1,0:T(8,128)(2,1)S(1)}, bf16[512,512]{1,0:T(8,128)(2,1)S(1)}) custom-call(s32[1]{0:T(128)} %bitcast.12.start, f32[1]{0:T(128)} %bitcast.15.multiplier, f32[1]{0:T(128)} %bitcast.17.offset, bf16[128,1152]{1,0:T(8,128)(2,1)S(1)} %collective-permute-done.11.refs_0_, ...), custom_call_target="tpu_custom_call" | custom-call | flops 1207959552 | bytes 5242880 | tf_op jit(solution)/shard_map/pallas_call | solution.py:297
  69.7 8.1 %collective-permute-start.21 = (bf16[288,512]{1,0:T(8,128)(2,1)S(1)}, bf16[288,512]{1,0:T(8,128)(2,1)S(1)}, u32[]{:S(2)}, u32[]{:S(2)}) collective-permute-start(bf16[288,512]{1,0:T(8,128)(2,1)S(1)} %get-tuple-element.86), channel_id=1, source_target_pairs={{0,1},{1,2},{2,3},{3,0},{4,5},{5,6},{6,7},{7,4},{8,9},{9,10},{10,1... | collective-permute-start | bytes 884744 | tf_op jit(solution)/shard_map/ppermute | solution.py:40
  78.9 4.0 %collective-permute-start.19 = (bf16[4,32,1152]{2,1,0:T(8,128)(2,1)S(1)}, bf16[4,32,1152]{2,1,0:T(8,128)(2,1)S(1)}, u32[]{:S(2)}, u32[]{:S(2)}) collective-permute-start(bf16[4,32,1152]{2,1,0:T(8,128)(2,1)S(1)} %get-tuple-element.84), channel_id=1, source_target_pairs={{0,128},{4,20},{8,136},{12,28},{16,144},{20,4},{24,152},{28,12},{3... | collective-permute-start | bytes 884744 | tf_op jit(solution)/shard_map/ppermute | solution.py:52
  82.9 6.0 %collective-permute-done.21.one = bf16[288,512]{1,0:T(8,128)(2,1)S(1)} collective-permute-done((bf16[288,512]{1,0:T(8,128)(2,1)S(1)}, bf16[288,512]{1,0:T(8,128)(2,1)S(1)}, u32[]{:S(2)}, u32[]{:S(2)}) %collective-permute-start.21) | collective-permute-done | bytes 294944 | tf_op jit(solution)/shard_map/ppermute | solution.py:40
  88.9 6.0 %collective-permute-start.15 = (bf16[288,512]{1,0:T(8,128)(2,1)S(1)}, bf16[288,512]{1,0:T(8,128)(2,1)S(1)}, u32[]{:S(2)}, u32[]{:S(2)}) collective-permute-start(bf16[288,512]{1,0:T(8,128)(2,1)S(1)} %get-tuple-element.76), channel_id=1, source_target_pairs={{0,2},{1,3},{2,0},{3,1},{4,6},{5,7},{6,4},{7,5},{8,10},{9,11},{10,... | collective-permute-start | bytes 884744 | tf_op jit(solution)/shard_map/ppermute | solution.py:40
  96.1 1.8 %collective-permute-start.25 = (bf16[32,1152]{1,0:T(8,128)(2,1)S(1)}, bf16[32,1152]{1,0:T(8,128)(2,1)S(1)}, u32[]{:S(2)}, u32[]{:S(2)}) collective-permute-start(bf16[32,1152]{1,0:T(8,128)(2,1)S(1)} %get-tuple-element.97), channel_id=1, source_target_pairs={{0,24},{4,196},{8,0},{12,204},{16,8},{20,212},{24,16},{28,220},{32... | collective-permute-start | bytes 221192 | tf_op jit(solution)/shard_map/ppermute | solution.py:52
  97.9 2.8 %collective-permute-done.23.one = bf16[32,1152]{1,0:T(8,128)(2,1)S(1)} collective-permute-done((bf16[32,1152]{1,0:T(8,128)(2,1)S(1)}, bf16[32,1152]{1,0:T(8,128)(2,1)S(1)}, u32[]{:S(2)}, u32[]{:S(2)}) %collective-permute-start.23) | collective-permute-done | bytes 73760 | tf_op jit(solution)/shard_map/ppermute | solution.py:52
  101.5 2.1 %shard_map.77.before = bf16[288,2048]{1,0:T(8,128)(2,1)} custom-call(bf16[288,512]{1,0:T(8,128)(2,1)} %copy-done.1, bf16[288,512]{1,0:T(8,128)(2,1)} %copy-done.2, bf16[288,512]{1,0:T(8,128)(2,1)} %copy-done.3), custom_call_target="tpu_custom_call" | custom-call | tf_op jit(solution)/shard_map/pallas_call | solution.py:246
  103.5 4.5 %collective-permute-done.15.two = bf16[288,512]{1,0:T(8,128)(2,1)S(1)} collective-permute-done((bf16[288,512]{1,0:T(8,128)(2,1)S(1)}, bf16[288,512]{1,0:T(8,128)(2,1)S(1)}, u32[]{:S(2)}, u32[]{:S(2)}) %collective-permute-start.15) | collective-permute-done | bytes 294944 | tf_op jit(solution)/shard_map/ppermute | solution.py:40
  108.8 1.7 %shard_map.78 = bf16[288,2048]{1,0:T(8,128)(2,1)} custom-call(bf16[288,512]{1,0:T(8,128)(2,1)} %copy-done.4, bf16[288,2048]{1,0:T(8,128)(2,1)} %shard_map.77.before), custom_call_target="tpu_custom_call", output_to_operand_aliasing={{}: (1, {})} | custom-call | tf_op jit(solution)/shard_map/pallas_call | solution.py:256
  (56 shorter events, 11.8 us)
Async XLA Ops:
  0.6 28.5 %all-to-all-start = ((bf16[16,32,1152]{2,1,0:T(8,128)(2,1)}), bf16[16,32,1152]{2,1,0:T(8,128)(2,1)S(1)}, u32[]{:S(2)}, u32[]{:S(2)}) async-start(bf16[16,32,1152]{2,1,0:T(8,128)(2,1)} %bitcast.21), calls=%async_computation | async-start | bytes 2359296 | tf_op jit(solution)/shard_map/all_to_all | solution.py:274
  8.6 14.1 %collective-permute-start = (bf16[288,512]{1,0:T(8,128)(2,1)S(1)}, bf16[288,512]{1,0:T(8,128)(2,1)S(1)}, u32[]{:S(2)}, u32[]{:S(2)}) collective-permute-start(bf16[288,512]{1,0:T(8,128)(2,1)S(1)} %get-tuple-element.51), channel_id=1, source_target_pairs={{0,1},{1,2},{2,3},{3,0},{4,5},{5,6},{6,7},{7,4},{8,9},{9,10},{10,1... | collective-permute-start | bytes 884744 | tf_op jit(solution)/shard_map/ppermute | solution.py:40
  11.6 17.5 %collective-permute-start.1 = (bf16[288,512]{1,0:T(8,128)(2,1)S(1)}, bf16[288,512]{1,0:T(8,128)(2,1)S(1)}, u32[]{:S(2)}, u32[]{:S(2)}) collective-permute-start(bf16[288,512]{1,0:T(8,128)(2,1)S(1)} %get-tuple-element.52), channel_id=1, source_target_pairs={{0,3},{1,0},{2,1},{3,2},{4,7},{5,4},{6,5},{7,6},{8,11},{9,8},{10,9... | collective-permute-start | bytes 884744 | tf_op jit(solution)/shard_map/ppermute | solution.py:40
  29.2 8.3 %collective-permute-start.6 = (bf16[288,256]{1,0:T(8,128)(2,1)S(1)}, bf16[288,256]{1,0:T(8,128)(2,1)S(1)}, u32[]{:S(2)}, u32[]{:S(2)}) collective-permute-start(bf16[288,256]{1,0:T(8,128)(2,1)S(1)} %get-tuple-element.54), channel_id=1, source_target_pairs={{0,2},{1,3},{2,0},{3,1},{4,6},{5,7},{6,4},{7,5},{8,10},{9,11},{10,... | collective-permute-start | bytes 442376 | tf_op jit(solution)/shard_map/ppermute | solution.py:40
  39.9 12.7 %collective-permute-start.7 = (bf16[128,1152]{1,0:T(8,128)(2,1)S(1)}, bf16[128,1152]{1,0:T(8,128)(2,1)S(1)}, u32[]{:S(2)}, u32[]{:S(2)}) collective-permute-start(bf16[128,1152]{1,0:T(8,128)(2,1)S(1)} %shard_map.71.refs_0_), channel_id=1, source_target_pairs={{0,64},{4,12},{8,72},{12,20},{16,80},{20,28},{24,88},{28,4},{32,96... | collective-permute-start | bytes 884744 | tf_op jit(solution)/shard_map/ppermute | solution.py:52
  41.2 11.5 %collective-permute-start.8 = (bf16[128,1152]{1,0:T(8,128)(2,1)S(1)}, bf16[128,1152]{1,0:T(8,128)(2,1)S(1)}, u32[]{:S(2)}, u32[]{:S(2)}) collective-permute-start(bf16[128,1152]{1,0:T(8,128)(2,1)S(1)} %shard_map.71.refs_0_), channel_id=1, source_target_pairs={{0,128},{4,20},{8,136},{12,28},{16,144},{20,4},{24,152},{28,12},{3... | collective-permute-start | bytes 884744 | tf_op jit(solution)/shard_map/ppermute | solution.py:52
  43.6 9.1 %collective-permute-start.9 = (bf16[128,1152]{1,0:T(8,128)(2,1)S(1)}, bf16[128,1152]{1,0:T(8,128)(2,1)}, u32[]{:S(2)}, u32[]{:S(2)}) collective-permute-start(bf16[128,1152]{1,0:T(8,128)(2,1)S(1)} %shard_map.71.refs_0_), channel_id=1, source_target_pairs={{0,192},{4,28},{8,200},{12,4},{16,208},{20,12},{24,216},{28,20},{3... | collective-permute-start | bytes 884744 | tf_op jit(solution)/shard_map/ppermute | solution.py:52
  44.8 7.9 %collective-permute-start.10 = (bf16[288,256]{1,0:T(8,128)(2,1)S(1)}, bf16[288,256]{1,0:T(8,128)(2,1)S(1)}, u32[]{:S(2)}, u32[]{:S(2)}) collective-permute-start(bf16[288,256]{1,0:T(8,128)(2,1)S(1)} %get-tuple-element.59), channel_id=1, source_target_pairs={{0,2},{1,3},{2,0},{3,1},{4,6},{5,7},{6,4},{7,5},{8,10},{9,11},{10,... | collective-permute-start | bytes 442376 | tf_op jit(solution)/shard_map/ppermute | solution.py:40
  52.7 13.2 %collective-permute-start.11 = (bf16[128,1152]{1,0:T(8,128)(2,1)S(1)}, bf16[128,1152]{1,0:T(8,128)(2,1)S(1)}, u32[]{:S(2)}, u32[]{:S(2)}) collective-permute-start(bf16[128,1152]{1,0:T(8,128)(2,1)S(1)} %shard_map.71.refs_0_), channel_id=1, source_target_pairs={{0,4},{4,0},{1,5},{5,1},{2,6},{6,2},{3,7},{7,3},{8,12},{12,8},{9,1... | collective-permute-start | bytes 884744 | tf_op jit(solution)/shard_map/ppermute | solution.py:40
  59.1 6.8 %collective-permute-start.12 = (bf16[128,1152]{1,0:T(8,128)(2,1)S(1)}, bf16[128,1152]{1,0:T(8,128)(2,1)S(1)}, u32[]{:S(2)}, u32[]{:S(2)}) collective-permute-start(bf16[128,1152]{1,0:T(8,128)(2,1)S(1)} %collective-permute-done.7.refs_1_), channel_id=1, source_target_pairs={{0,4},{4,0},{1,5},{5,1},{2,6},{6,2},{3,7},{7,3},{8,12},{12,8},{9,1... | collective-permute-start | bytes 884744 | tf_op jit(solution)/shard_map/ppermute | solution.py:40
  59.2 6.7 %collective-permute-start.13 = (bf16[128,1152]{1,0:T(8,128)(2,1)S(1)}, bf16[128,1152]{1,0:T(8,128)(2,1)S(1)}, u32[]{:S(2)}, u32[]{:S(2)}) collective-permute-start(bf16[128,1152]{1,0:T(8,128)(2,1)S(1)} %collective-permute-done.8.refs_2_), channel_id=1, source_target_pairs={{0,4},{4,0},{1,5},{5,1},{2,6},{6,2},{3,7},{7,3},{8,12},{12,8},{9,1... | collective-permute-start | bytes 884744 | tf_op jit(solution)/shard_map/ppermute | solution.py:40
  59.6 6.3 %collective-permute-start.14 = (bf16[128,1152]{1,0:T(8,128)(2,1)}, bf16[128,1152]{1,0:T(8,128)(2,1)S(1)}, u32[]{:S(2)}, u32[]{:S(2)}) collective-permute-start(bf16[128,1152]{1,0:T(8,128)(2,1)} %collective-permute-done.9.refs_3_), channel_id=1, source_target_pairs={{0,4},{4,0},{1,5},{5,1},{2,6},{6,2},{3,7},{7,3},{8,12},{12,8},{9,1... | collective-permute-start | bytes 884744 | tf_op jit(solution)/shard_map/ppermute | solution.py:40
  65.4 12.4 %collective-permute-start.17 = (bf16[16,16,1152]{2,1,0:T(8,128)(2,1)S(1)}, bf16[16,16,1152]{2,1,0:T(8,128)(2,1)S(1)}, u32[]{:S(2)}, u32[]{:S(2)}) collective-permute-start(bf16[16,16,1152]{2,1,0:T(8,128)(2,1)S(1)} %get-tuple-element.81), channel_id=1, source_target_pairs={{0,4},{4,0},{1,5},{5,1},{2,6},{6,2},{3,7},{7,3},{8,12},{12,8},{9,1... | collective-permute-start | bytes 1769480 | tf_op jit(solution)/shard_map/ppermute | solution.py:40
  68.5 9.4 %collective-permute-start.16 = (bf16[16,16,1152]{2,1,0:T(8,128)(2,1)S(1)}, bf16[16,16,1152]{2,1,0:T(8,128)(2,1)S(1)}, u32[]{:S(2)}, u32[]{:S(2)}) collective-permute-start(bf16[16,16,1152]{2,1,0:T(8,128)(2,1)S(1)} %get-tuple-element.79), channel_id=1, source_target_pairs={{0,4},{4,0},{1,5},{5,1},{2,6},{6,2},{3,7},{7,3},{8,12},{12,8},{9,1... | collective-permute-start | bytes 1769480 | tf_op jit(solution)/shard_map/ppermute | solution.py:40
  69.7 19.2 %collective-permute-start.21 = (bf16[288,512]{1,0:T(8,128)(2,1)S(1)}, bf16[288,512]{1,0:T(8,128)(2,1)S(1)}, u32[]{:S(2)}, u32[]{:S(2)}) collective-permute-start(bf16[288,512]{1,0:T(8,128)(2,1)S(1)} %get-tuple-element.86), channel_id=1, source_target_pairs={{0,1},{1,2},{2,3},{3,0},{4,5},{5,6},{6,7},{7,4},{8,9},{9,10},{10,1... | collective-permute-start | bytes 884744 | tf_op jit(solution)/shard_map/ppermute | solution.py:40
  77.8 17.0 %collective-permute-start.22 = (bf16[288,512]{1,0:T(8,128)(2,1)S(1)}, bf16[288,512]{1,0:T(8,128)(2,1)S(1)}, u32[]{:S(2)}, u32[]{:S(2)}) collective-permute-start(bf16[288,512]{1,0:T(8,128)(2,1)S(1)} %get-tuple-element.87), channel_id=1, source_target_pairs={{0,3},{1,0},{2,1},{3,2},{4,7},{5,4},{6,5},{7,6},{8,11},{9,8},{10,9... | collective-permute-start | bytes 884744 | tf_op jit(solution)/shard_map/ppermute | solution.py:40
  78.1 16.8 %collective-permute-start.18 = (bf16[4,32,1152]{2,1,0:T(8,128)(2,1)S(1)}, bf16[4,32,1152]{2,1,0:T(8,128)(2,1)S(1)}, u32[]{:S(2)}, u32[]{:S(2)}) collective-permute-start(bf16[4,32,1152]{2,1,0:T(8,128)(2,1)S(1)} %get-tuple-element.83), channel_id=1, source_target_pairs={{0,64},{4,12},{8,72},{12,20},{16,80},{20,28},{24,88},{28,4},{32,96... | collective-permute-start | bytes 884744 | tf_op jit(solution)/shard_map/ppermute | solution.py:52
  78.9 16.0 %collective-permute-start.19 = (bf16[4,32,1152]{2,1,0:T(8,128)(2,1)S(1)}, bf16[4,32,1152]{2,1,0:T(8,128)(2,1)S(1)}, u32[]{:S(2)}, u32[]{:S(2)}) collective-permute-start(bf16[4,32,1152]{2,1,0:T(8,128)(2,1)S(1)} %get-tuple-element.84), channel_id=1, source_target_pairs={{0,128},{4,20},{8,136},{12,28},{16,144},{20,4},{24,152},{28,12},{3... | collective-permute-start | bytes 884744 | tf_op jit(solution)/shard_map/ppermute | solution.py:52
  82.9 12.0 %collective-permute-start.20 = (bf16[4,32,1152]{2,1,0:T(8,128)(2,1)S(1)}, bf16[4,32,1152]{2,1,0:T(8,128)(2,1)S(1)}, u32[]{:S(2)}, u32[]{:S(2)}) collective-permute-start(bf16[4,32,1152]{2,1,0:T(8,128)(2,1)S(1)} %get-tuple-element.85), channel_id=1, source_target_pairs={{0,192},{4,28},{8,200},{12,4},{16,208},{20,12},{24,216},{28,20},{3... | collective-permute-start | bytes 884744 | tf_op jit(solution)/shard_map/ppermute | solution.py:52
  88.9 19.2 %collective-permute-start.15 = (bf16[288,512]{1,0:T(8,128)(2,1)S(1)}, bf16[288,512]{1,0:T(8,128)(2,1)S(1)}, u32[]{:S(2)}, u32[]{:S(2)}) collective-permute-start(bf16[288,512]{1,0:T(8,128)(2,1)S(1)} %get-tuple-element.76), channel_id=1, source_target_pairs={{0,2},{1,3},{2,0},{3,1},{4,6},{5,7},{6,4},{7,5},{8,10},{9,11},{10,... | collective-permute-start | bytes 884744 | tf_op jit(solution)/shard_map/ppermute | solution.py:40
  95.1 5.6 %collective-permute-start.23 = (bf16[32,1152]{1,0:T(8,128)(2,1)S(1)}, bf16[32,1152]{1,0:T(8,128)(2,1)S(1)}, u32[]{:S(2)}, u32[]{:S(2)}) collective-permute-start(bf16[32,1152]{1,0:T(8,128)(2,1)S(1)} %get-tuple-element.95), channel_id=1, source_target_pairs={{0,8},{4,68},{8,16},{12,76},{16,24},{20,84},{24,0},{28,92},{32,40}... | collective-permute-start | bytes 221192 | tf_op jit(solution)/shard_map/ppermute | solution.py:52
  95.4 5.3 %collective-permute-start.24 = (bf16[32,1152]{1,0:T(8,128)(2,1)S(1)}, bf16[32,1152]{1,0:T(8,128)(2,1)S(1)}, u32[]{:S(2)}, u32[]{:S(2)}) collective-permute-start(bf16[32,1152]{1,0:T(8,128)(2,1)S(1)} %get-tuple-element.96), channel_id=1, source_target_pairs={{0,16},{4,132},{8,24},{12,140},{16,0},{20,148},{24,8},{28,156},{32... | collective-permute-start | bytes 221192 | tf_op jit(solution)/shard_map/ppermute | solution.py:52
  96.1 5.2 %collective-permute-start.25 = (bf16[32,1152]{1,0:T(8,128)(2,1)S(1)}, bf16[32,1152]{1,0:T(8,128)(2,1)S(1)}, u32[]{:S(2)}, u32[]{:S(2)}) collective-permute-start(bf16[32,1152]{1,0:T(8,128)(2,1)S(1)} %get-tuple-element.97), channel_id=1, source_target_pairs={{0,24},{4,196},{8,0},{12,204},{16,8},{20,212},{24,16},{28,220},{32... | collective-permute-start | bytes 221192 | tf_op jit(solution)/shard_map/ppermute | solution.py:52
  101.3 9.1 %collective-permute-start.26 = (f32[2,8,1152]{2,1,0:T(8,128)S(1)}, f32[2,8,1152]{2,1,0:T(8,128)S(1)}, u32[]{:S(2)}, u32[]{:S(2)}) collective-permute-start(f32[2,8,1152]{2,1,0:T(8,128)S(1)} %get-tuple-element.99), channel_id=1, source_target_pairs={{0,32},{32,0},{1,33},{33,1},{2,34},{34,2},{3,35},{35,3},{4,36},{36... | collective-permute-start | bytes 221192 | tf_op jit(solution)/shard_map/ppermute | solution.py:40
  (9 other events, 52.8 us)

commit v6 on v5

--- a/solution.py
+++ b/solution.py
@@ -21,7 +21,7 @@
     return jax.ShapeDtypeStruct(shape, dtype)
 
 
-def call(kernel, outs, ins, scratch=(), products=0, moved=1):
+def call(kernel, outs, ins, scratch=(), products=0, moved=1, vmem=16 << 20):
     single = not isinstance(outs, list)
     return pl.pallas_call(
         kernel,
@@ -29,7 +29,7 @@
         in_specs=ins,
         out_specs=VMEM if single else [VMEM] * len(outs),
         scratch_shapes=list(scratch),
-        compiler_params=pltpu.CompilerParams(vmem_limit_bytes=16 << 20),
+        compiler_params=pltpu.CompilerParams(vmem_limit_bytes=vmem),
         cost_estimate=pl.CostEstimate(
             flops=2 * products * D * ROWS * ROWS, bytes_accessed=moved << 20, transcendentals=0
         ),
@@ -81,9 +81,8 @@
         copy.wait()
 
 
-def cut_kernel(pictures, own, one, three, two_low, two_high, done):
+def cut_pieces(places, pictures, done):
     mine = lax.axis_index("t")
-    places = [(own, 0, 0), (one, 1, 0), (three, 3, 0), (two_low, 2, 0), (two_high, 2, HALF)]
     copies = []
     for i, (piece, d, at) in enumerate(places):
         size = piece.shape[1]
@@ -92,14 +91,53 @@
     run(copies)
 
 
-def pick_kernel(start, parts, piece):
+def cut_kernel(captions, pictures, *refs):
+    chunks, (own, one, three, text_done, done) = refs[:4], refs[4:]
+    place = spot()[1]
+    copies = [
+        pltpu.make_async_copy(captions.at[ahead(place, d)], chunk, text_done.at[d]) for d, chunk in enumerate(chunks)
+    ]
+    for copy in copies:
+        copy.start()
+    cut_pieces([(own, 0, 0), (one, 1, 0), (three, 3, 0)], pictures, done)
+    for copy in copies:
+        copy.wait()
+
+
+def cut_far_kernel(pictures, low, high, done):
+    cut_pieces([(low, 2, 0), (high, 2, HALF)], pictures, done)
+
+
+def root_of(start):
     chip = holder_of(start, 0)[1] >> 1
-    piece[...] = parts[(chip >> 3) * 4 + (chip & 3)]
+    x, y, core = chip >> 3, chip & 3, lax.axis_index("c")
+    return jnp.where(core == 0, x, y), jnp.where(core == 0, y, x), (chip >> 2) & 1
+
+
+def first_pick_kernel(start, *refs):
+    chunks, outs = refs[:4], refs[4:]
+    _, first, second = spot()
+    came = lax.rem(first + 4 - root_of(start)[0], 4)
+    for d, chunk in enumerate(chunks):
+
+        @pl.when(came == d)
+        def _():
+            for by, out in enumerate(outs):
+                out[...] = chunk[ahead(second, by)]
+
+
+def second_pick_kernel(start, *refs):
+    pieces, out = refs[:4], refs[4]
+    came = lax.rem(spot()[2] + 4 - root_of(start)[1], 4)
+    for d, piece in enumerate(pieces):
+
+        @pl.when(came == d)
+        def _():
+            out[...] = piece[...]
 
 
 def unit_rows_kernel(start, here, there, piece):
-    chip = holder_of(start, 0)[1] >> 1
-    is_here = ((chip >> 2) & 1) == lax.axis_index("zl")
+    is_here = root_of(start)[2] == lax.axis_index("zl")
     wide = jnp.where(is_here, here[...].astype(F32), there[...].astype(F32))
     total = jnp.sum(wide * wide, axis=1, keepdims=True)
     piece[...] = (wide * lax.rsqrt(total + EPSILON)).astype(BF16)
@@ -129,27 +167,22 @@
 
 
 def slab_weights(other, start, multiplier, offset, chunks, images, text, weights):
-    core, first, second = spot()
+    place = spot()[1 + other]
     held = lax.axis_index(DP) == holder_of(start, other)[1]
-    kind, place = (core, first) if other == 0 else (1 - core, second)
     times, plus = multiplier[0], offset[0]
     for d in range(4):
         rows = slice(CHUNK * d, CHUNK * d + CHUNK)
         text[rows, :] = chunks[d][...]
         logits = times * jnp.dot(chunks[d][...], images[...], preferred_element_type=F32) + plus
-        at = lax.broadcasted_iota(jnp.int32, (CHUNK, 1), 0)
-        inner, along_first = at >> 5, back(place, d)
-        x = jnp.where(kind == 0, along_first, inner)
-        y = jnp.where(kind == 0, inner, along_first)
-        row = x * 128 + y * PIECE + (at & (PIECE - 1))
+        row = lax.broadcasted_iota(jnp.int32, (CHUNK, 1), 0) + back(place, d) * CHUNK
         same = row == lax.broadcasted_iota(jnp.int32, (CHUNK, ROWS), 1)
         positive = jnp.where(same & held, 1.0, 0.0)
-        weights[rows, :] = ((jax.nn.sigmoid(logits) - positive) * times).astype(BF16)
+        share = 0.5 * jnp.tanh(0.5 * logits) + 0.5
+        weights[rows, :] = ((share - positive) * times).astype(BF16)
 
 
 def slab_terms(other, images, weights, by_owner, keep, send):
-    core, first, second = spot()
-    kind, place = (core, first) if other == 0 else (1 - core, second)
+    core, place = lax.axis_index("c"), spot()[1 + other]
     for d in range(4):
         terms = lax.dot_general(
             weights[CHUNK * d : CHUNK * d + CHUNK, :],
@@ -158,16 +191,13 @@
             preferred_element_type=F32,
         )
         for inner in range(4):
-            outer = back(place, d)
-            x = jnp.where(kind == 0, outer, inner)
-            part = jnp.where(kind == 0, inner, outer)
-            rows = pl.ds(pl.multiple_of((part >> 1) * 8, 8), 8)
+            x, z = back(place, d), inner >> 1
             for low in range(2):
-                y = (part & 1) * 2 + low
+                y = (inner & 1) * 2 + low
                 spots = (x * 4 + y, y * 4 + x)
                 for c in range(2):
                     at = PIECE * inner + 16 * low + 8 * c
-                    by_owner[c, spots[c], rows, :] = terms[at : at + 8, :]
+                    by_owner[c, spots[c], 8 * z : 8 * z + 8, :] = terms[at : at + 8, :]
     keep[...] = by_owner[core]
     send[...] = by_owner[1 - core].astype(BF16)
 
@@ -248,6 +278,7 @@
         out_shape=like(PART, PEERS * ROWS),
         in_specs=[VMEM] * 3,
         out_specs=HBM,
+        compiler_params=pltpu.CompilerParams(vmem_limit_bytes=4 << 20),
         scratch_shapes=[DMA((3,))],
     )(own, one, three)
 
@@ -258,6 +289,7 @@
         out_shape=like(PART, PEERS * ROWS),
         in_specs=[VMEM, HBM],
         out_specs=HBM,
+        compiler_params=pltpu.CompilerParams(vmem_limit_bytes=4 << 20),
         scratch_shapes=[DMA((1,))],
         input_output_aliases={1: 0},
     )(two, before)
@@ -267,14 +299,26 @@
     start, multiplier, offset = (value.reshape(1) for value in (start, multiplier, offset))
     scalars, scalar_specs = (start, multiplier, offset), [SMEM] * 3
 
-    shapes = [like(PART, ROWS)] * 3 + [like(PART, HALF)] * 2
-    near, one, three, low, high = call(cut_kernel, shapes, [HBM], [DMA((5,))], moved=2)(pictures.T)
-    one, three, low, high = (shift(v, "t", d, PEERS) for v, d in ((one, 1), (three, 3), (low, 2), (high, 2)))
-
-    text = lax.all_to_all(captions.reshape(16, PIECE, D), ("x", "y"), split_axis=0, concat_axis=0, tiled=True)
-    text, one, three = lax.optimization_barrier((text, one, three))
-    piece = call(pick_kernel, like(PIECE, D), [SMEM, VMEM])(start, text)
-    piece = call(unit_rows_kernel, like(PIECE, D), [SMEM] + [VMEM] * 2)(start, piece, shift(piece, "zl", 1, 2))
+    pictures = pictures.T
+    *chunks, near, one, three = call(
+        cut_kernel,
+        [like(4, PIECE, D)] * 4 + [like(PART, ROWS)] * 3,
+        [HBM] * 2,
+        [DMA((4,)), DMA((3,))],
+        moved=4,
+        vmem=58 << 20,
+    )(captions.reshape(4, 4, PIECE, D), pictures)
+
+    chunks = [chunks[0]] + [along(chunks[d], True, d) for d in (1, 2, 3)]
+    one, three = shift(one, "t", 1, PEERS), shift(three, "t", 3, PEERS)
+    pieces = call(first_pick_kernel, [like(PIECE, D)] * 4, [SMEM] + [VMEM] * 4)(start, *chunks)
+    pieces = [pieces[0]] + [along(pieces[d], False, d) for d in (1, 2, 3)]
+    piece = call(second_pick_kernel, like(PIECE, D), [SMEM] + [VMEM] * 4)(start, *pieces)
+    there = shift(piece, "zl", 1, 2)
+    there, one, three = lax.optimization_barrier((there, one, three))
+    low, high = call(cut_far_kernel, [like(PART, HALF)] * 2, [HBM], [DMA((2,))])(pictures)
+    low, high = shift(low, "t", 2, PEERS), shift(high, "t", 2, PEERS)
+    piece = call(unit_rows_kernel, like(PIECE, D), [SMEM] + [VMEM] * 2)(start, piece, there)
 
     pieces = [piece] + [along(piece, False, d) for d in (1, 2, 3)]
     *pieces, low = lax.optimization_barrier((*pieces, low))

time: 113 us -> 110 us (0.973); the launches traced: 111 us -> 110 us
  waiting for transfers between devices: 35.1 us -> 31.9 us
  starting transfers between devices: 59.3 us -> 60.9 us
    ppermute x12 -> x18, starting transfers between devices: 17 us -> 25.2 us  [along(): return lax.ppermute(value, DP, pairs)]
    all_to_all x1 -> x0, starting transfers between devices: 7.73 us -> none  [per_device(): lax.all_to_all(captions.reshape(16, PIECE, D), ('x', 'y'), split_axis=0,...]
    ppermute x15, waiting for transfers between devices: 29.3 us -> 22.3 us  [shift(): lax.ppermute(value, axis, [(i, (i + by) % size) for i in range(size)])]
    ppermute x12 -> x18, waiting for transfers between devices: 5.72 us -> 9.59 us  [along(): return lax.ppermute(value, DP, pairs)]
    pallas_call x2 -> x4, Pallas kernels: 0.19 us -> 2.98 us  [the longest x1 2.89 us: per_device(): call(cut_kernel, [like(4, PIECE, D)] * 4 + [like(PART, ROWS)] * 3, [HBM]...]
    ppermute x15, starting transfers between devices: 34.6 us -> 35.7 us  [shift(): lax.ppermute(value, axis, [(i, (i + by) % size) for i in range(size)])]
  transfers between devices with their start and end apart: 28 -> 33, of which waited for: 9 -> 11; matrix products, arithmetic and copies ran while one was open for 0% -> 0% of each run, Pallas kernels for 11% -> 9%
where the time goes in v6:
time: 110 us
  starting transfers between devices  60.9 us (55%)
  waiting for transfers between devices  31.9 us (29%)
  Pallas kernels  12.3 us (11%)
  between operations  2.79 us (3%)
    ppermute x15, starting transfers between devices, shift(): lax.ppermute(value, axis, [(i, (i + by) % size) for i in range(size)])  35.7 us
    ppermute x18, starting transfers between devices, along(): return lax.ppermute(value, DP, pairs)  25.2 us
    ppermute x15, waiting for transfers between devices, shift(): lax.ppermute(value, axis, [(i, (i + by) % size) for i in range(size)])  22.3 us
    ppermute x18, waiting for transfers between devices, along(): return lax.ppermute(value, DP, pairs)  9.59 us
    pallas_call x1, Pallas kernels, per_device(): call(own_kernel, [kept, sent, like(D, ROWS, dtype=F32)], scalar_specs + [...  3.2 us
    pallas_call x1, Pallas kernels, per_device(): call(cut_kernel, [like(4, PIECE, D)] * 4 + [like(PART, ROWS)] * 3, [HBM]...  2.89 us
    pallas_call x1, Pallas kernels, per_device(): call(other_kernel, [kept, sent, square], scalar_specs + [VMEM] * 5, [text...  2.47 us
  transfers between devices with their start and end apart: 33, of which 11 were waited for; matrix products, arithmetic and copies ran while one was open for 0% of the time, Pallas kernels for 9%

profile of v6, /device:TPU:1, one launch (start us, length us, event | category | flops | bytes accessed | tf_op | source)
XLA Modules:
  0.0 109.5 jit_solution(700670404374709813)
XLA Ops:
  0.6 2.9 %shard_map.68 = (bf16[4,32,1152]{2,1,0:T(8,128)(2,1)}, bf16[4,32,1152]{2,1,0:T(8,128)(2,1)}, bf16[4,32,1152]{2,1,0:T(8,128)(2,1)}, bf16[4,32,1152]{2,1,0:T(8,128...) custom-call(bf16[4,4,32,1152]{3,2,1,0:T(8,128)(2,1)} %bitcast.23, ...), custom_call_target="tpu_custom_call" | custom-call | bytes 4194304 | tf_op jit(solution)/shard_map/pallas_call | solution.py:303
  3.5 2.2 %collective-permute-start = (bf16[4,32,1152]{2,1,0:T(8,128)(2,1)}, bf16[4,32,1152]{2,1,0:T(8,128)(2,1)S(1)}, u32[]{:S(2)}, u32[]{:S(2)}) collective-permute-start(bf16[4,32,1152]{2,1,0:T(8,128)(2,1)} %get-tuple-element.60), channel_id=1, source_target_pairs={{0,64},{4,12},{8,72},{12,20},{16,80},{20,28},{24,88},{28,4},{32,96... | collective-permute-start | bytes 884744 | tf_op jit(solution)/shard_map/ppermute | solution.py:52
  5.7 2.6 %collective-permute-start.1 = (bf16[4,32,1152]{2,1,0:T(8,128)(2,1)}, bf16[4,32,1152]{2,1,0:T(8,128)(2,1)S(1)}, u32[]{:S(2)}, u32[]{:S(2)}) collective-permute-start(bf16[4,32,1152]{2,1,0:T(8,128)(2,1)} %get-tuple-element.61), channel_id=1, source_target_pairs={{0,128},{4,20},{8,136},{12,28},{16,144},{20,4},{24,152},{28,12},{3... | collective-permute-start | bytes 884744 | tf_op jit(solution)/shard_map/ppermute | solution.py:52
  9.4 3.0 %collective-permute-start.7 = (bf16[288,512]{1,0:T(8,128)(2,1)}, bf16[288,512]{1,0:T(8,128)(2,1)S(1)}, u32[]{:S(2)}, u32[]{:S(2)}) collective-permute-start(bf16[288,512]{1,0:T(8,128)(2,1)} %get-tuple-element.67), channel_id=1, source_target_pairs={{0,1},{1,2},{2,3},{3,0},{4,5},{5,6},{6,7},{7,4},{8,9},{9,10},{10,1... | collective-permute-start | bytes 884744 | tf_op jit(solution)/shard_map/ppermute | solution.py:40
  12.4 3.0 %collective-permute-start.8 = (bf16[288,512]{1,0:T(8,128)(2,1)}, bf16[288,512]{1,0:T(8,128)(2,1)S(1)}, u32[]{:S(2)}, u32[]{:S(2)}) collective-permute-start(bf16[288,512]{1,0:T(8,128)(2,1)} %get-tuple-element.68), channel_id=1, source_target_pairs={{0,3},{1,0},{2,1},{3,2},{4,7},{5,4},{6,5},{7,6},{8,11},{9,8},{10,9... | collective-permute-start | bytes 884744 | tf_op jit(solution)/shard_map/ppermute | solution.py:40
  18.4 2.5 %collective-permute-start.4 = (bf16[32,1152]{1,0:T(8,128)(2,1)S(1)}, bf16[32,1152]{1,0:T(8,128)(2,1)S(1)}, u32[]{:S(2)}, u32[]{:S(2)}) collective-permute-start(bf16[32,1152]{1,0:T(8,128)(2,1)S(1)} %get-tuple-element.65), channel_id=1, source_target_pairs={{0,16},{4,132},{8,24},{12,140},{16,0},{20,148},{24,8},{28,156},{32... | collective-permute-start | bytes 221192 | tf_op jit(solution)/shard_map/ppermute | solution.py:52
  24.4 1.7 %collective-permute-start.6 = (bf16[32,1152]{1,0:T(8,128)(2,1)S(1)}, bf16[32,1152]{1,0:T(8,128)(2,1)S(1)}, u32[]{:S(2)}, u32[]{:S(2)}) collective-permute-start(bf16[32,1152]{1,0:T(8,128)(2,1)S(1)} %shard_map.70.here), channel_id=1, source_target_pairs={{0,32},{32,0},{1,33},{33,1},{2,34},{34,2},{3,35},{35,3},{4,36},{36... | collective-permute-start | bytes 221192 | tf_op jit(solution)/shard_map/ppermute | solution.py:40
  26.2 6.1 %collective-permute-start.12 = (bf16[288,256]{1,0:T(8,128)(2,1)S(1)}, bf16[288,256]{1,0:T(8,128)(2,1)S(1)}, u32[]{:S(2)}, u32[]{:S(2)}) collective-permute-start(bf16[288,256]{1,0:T(8,128)(2,1)S(1)} %get-tuple-element.70), channel_id=1, source_target_pairs={{0,2},{1,3},{2,0},{3,1},{4,6},{5,7},{6,4},{7,5},{8,10},{9,11},{10,... | collective-permute-start | bytes 442376 | tf_op jit(solution)/shard_map/ppermute | solution.py:40
  32.4 1.8 %collective-permute-start.10 = (bf16[32,1152]{1,0:T(8,128)(2,1)S(1)}, bf16[32,1152]{1,0:T(8,128)(2,1)S(1)}, u32[]{:S(2)}, u32[]{:S(2)}) collective-permute-start(bf16[32,1152]{1,0:T(8,128)(2,1)S(1)} %shard_map.71.refs_0_), channel_id=1, source_target_pairs={{0,16},{4,132},{8,24},{12,140},{16,0},{20,148},{24,8},{28,156},{32... | collective-permute-start | bytes 221192 | tf_op jit(solution)/shard_map/ppermute | solution.py:52
  34.2 1.7 %collective-permute-start.11 = (bf16[32,1152]{1,0:T(8,128)(2,1)S(1)}, bf16[32,1152]{1,0:T(8,128)(2,1)S(1)}, u32[]{:S(2)}, u32[]{:S(2)}) collective-permute-start(bf16[32,1152]{1,0:T(8,128)(2,1)S(1)} %shard_map.71.refs_0_), channel_id=1, source_target_pairs={{0,24},{4,196},{8,0},{12,204},{16,8},{20,212},{24,16},{28,220},{32... | collective-permute-start | bytes 221192 | tf_op jit(solution)/shard_map/ppermute | solution.py:52
  38.0 2.6 %collective-permute-done.9.refs_1_ = bf16[32,1152]{1,0:T(8,128)(2,1)S(1)} collective-permute-done((bf16[32,1152]{1,0:T(8,128)(2,1)S(1)}, bf16[32,1152]{1,0:T(8,128)(2,1)S(1)}, u32[]{:S(2)}, u32[]{:S(2)}) %collective-permute-start.9) | collective-permute-done | bytes 73760 | tf_op jit(solution)/shard_map/ppermute | solution.py:52
  40.8 2.3 %collective-permute-start.14 = (bf16[128,1152]{1,0:T(8,128)(2,1)S(1)}, bf16[128,1152]{1,0:T(8,128)(2,1)S(1)}, u32[]{:S(2)}, u32[]{:S(2)}) collective-permute-start(bf16[128,1152]{1,0:T(8,128)(2,1)S(1)} %shard_map.73.refs_0_), channel_id=1, source_target_pairs={{0,128},{4,20},{8,136},{12,28},{16,144},{20,4},{24,152},{28,12},{3... | collective-permute-start | bytes 884744 | tf_op jit(solution)/shard_map/ppermute | solution.py:52
  44.2 2.5 %collective-permute-start.16 = (bf16[288,256]{1,0:T(8,128)(2,1)S(1)}, bf16[288,256]{1,0:T(8,128)(2,1)S(1)}, u32[]{:S(2)}, u32[]{:S(2)}) collective-permute-start(bf16[288,256]{1,0:T(8,128)(2,1)S(1)} %get-tuple-element.75), channel_id=1, source_target_pairs={{0,2},{1,3},{2,0},{3,1},{4,6},{5,7},{6,4},{7,5},{8,10},{9,11},{10,... | collective-permute-start | bytes 442376 | tf_op jit(solution)/shard_map/ppermute | solution.py:40
  46.8 6.5 %collective-permute-done.16.two_high = bf16[288,256]{1,0:T(8,128)(2,1)S(1)} collective-permute-done((bf16[288,256]{1,0:T(8,128)(2,1)S(1)}, bf16[288,256]{1,0:T(8,128)(2,1)S(1)}, u32[]{:S(2)}, u32[]{:S(2)}) %collective-permute-start.16) | collective-permute-done | bytes 147488 | tf_op jit(solution)/shard_map/ppermute | solution.py:40
  53.3 7.9 %collective-permute-start.17 = (bf16[128,1152]{1,0:T(8,128)(2,1)S(1)}, bf16[128,1152]{1,0:T(8,128)(2,1)S(1)}, u32[]{:S(2)}, u32[]{:S(2)}) collective-permute-start(bf16[128,1152]{1,0:T(8,128)(2,1)S(1)} %shard_map.73.refs_0_), channel_id=1, source_target_pairs={{0,4},{4,0},{1,5},{5,1},{2,6},{6,2},{3,7},{7,3},{8,12},{12,8},{9,1... | collective-permute-start | bytes 884744 | tf_op jit(solution)/shard_map/ppermute | solution.py:40
  63.4 3.2 %shard_map.76 = (f32[16,16,1152]{2,1,0:T(8,128)S(1)}, bf16[16,16,1152]{2,1,0:T(8,128)(2,1)S(1)}, f32[1152,512]{1,0:T(8,128)S(1)}) custom-call(s32[1]{0:T(128)} %bitcast.14.start, f32[1]{0:T(128)} %bitcast.17.multiplier, f32[1]{0:T(128)} %bitcast.19.offset, bf16[128,1152]{1,0:T(8,128)(2,1)S(1)} %shard_map.73.refs_0_, ...), custom_call_target="tpu_custom_call" | custom-call | flops 1811939328 | bytes 8388608 | tf_op jit(solution)/shard_map/pallas_call | solution.py:333
  67.1 2.5 %shard_map.75 = (f32[16,16,1152]{2,1,0:T(8,128)S(1)}, bf16[16,16,1152]{2,1,0:T(8,128)(2,1)S(1)}, bf16[512,512]{1,0:T(8,128)(2,1)S(1)}) custom-call(s32[1]{0:T(128)} %bitcast.13.start, f32[1]{0:T(128)} %bitcast.16.multiplier, f32[1]{0:T(128)} %bitcast.18.offset, bf16[128,1152]{1,0:T(8,128)(2,1)S(1)} %collective-permute-done.17.refs_0_, ...), custom_call_target="tpu_custom_call" | custom-call | flops 1207959552 | bytes 5242880 | tf_op jit(solution)/shard_map/pallas_call | solution.py:341
  70.9 3.6 %collective-permute-start.28 = (bf16[288,512]{1,0:T(8,128)(2,1)S(1)}, bf16[288,512]{1,0:T(8,128)(2,1)S(1)}, u32[]{:S(2)}, u32[]{:S(2)}) collective-permute-start(bf16[288,512]{1,0:T(8,128)(2,1)S(1)} %get-tuple-element.103), channel_id=1, source_target_pairs={{0,3},{1,0},{2,1},{3,2},{4,7},{5,4},{6,5},{7,6},{8,11},{9,8},{10,9... | collective-permute-start | bytes 884744 | tf_op jit(solution)/shard_map/ppermute | solution.py:40
  77.4 9.3 %collective-permute-done.27.one = bf16[288,512]{1,0:T(8,128)(2,1)S(1)} collective-permute-done((bf16[288,512]{1,0:T(8,128)(2,1)S(1)}, bf16[288,512]{1,0:T(8,128)(2,1)S(1)}, u32[]{:S(2)}, u32[]{:S(2)}) %collective-permute-start.27) | collective-permute-done | bytes 294944 | tf_op jit(solution)/shard_map/ppermute | solution.py:40
  86.7 6.4 %collective-permute-start.21 = (bf16[288,512]{1,0:T(8,128)(2,1)S(1)}, bf16[288,512]{1,0:T(8,128)(2,1)S(1)}, u32[]{:S(2)}, u32[]{:S(2)}) collective-permute-start(bf16[288,512]{1,0:T(8,128)(2,1)S(1)} %get-tuple-element.92), channel_id=1, source_target_pairs={{0,2},{1,3},{2,0},{3,1},{4,6},{5,7},{6,4},{7,5},{8,10},{9,11},{10,... | collective-permute-start | bytes 884744 | tf_op jit(solution)/shard_map/ppermute | solution.py:40
  93.4 2.1 %collective-permute-start.29 = (bf16[32,1152]{1,0:T(8,128)(2,1)S(1)}, bf16[32,1152]{1,0:T(8,128)(2,1)S(1)}, u32[]{:S(2)}, u32[]{:S(2)}) collective-permute-start(bf16[32,1152]{1,0:T(8,128)(2,1)S(1)} %get-tuple-element.111), channel_id=1, source_target_pairs={{0,8},{4,68},{8,16},{12,76},{16,24},{20,84},{24,0},{28,92},{32,40}... | collective-permute-start | bytes 221192 | tf_op jit(solution)/shard_map/ppermute | solution.py:52
  95.5 2.5 %collective-permute-start.31 = (bf16[32,1152]{1,0:T(8,128)(2,1)S(1)}, bf16[32,1152]{1,0:T(8,128)(2,1)S(1)}, u32[]{:S(2)}, u32[]{:S(2)}) collective-permute-start(bf16[32,1152]{1,0:T(8,128)(2,1)S(1)} %get-tuple-element.113), channel_id=1, source_target_pairs={{0,24},{4,196},{8,0},{12,204},{16,8},{20,212},{24,16},{28,220},{32... | collective-permute-start | bytes 221192 | tf_op jit(solution)/shard_map/ppermute | solution.py:52
  98.2 2.3 %collective-permute-done.30.two = bf16[32,1152]{1,0:T(8,128)(2,1)S(1)} collective-permute-done((bf16[32,1152]{1,0:T(8,128)(2,1)S(1)}, bf16[32,1152]{1,0:T(8,128)(2,1)S(1)}, u32[]{:S(2)}, u32[]{:S(2)}) %collective-permute-start.30) | collective-permute-done | bytes 73760 | tf_op jit(solution)/shard_map/ppermute | solution.py:52
  102.7 6.2 %collective-permute-done.32 = f32[2,8,1152]{2,1,0:T(8,128)S(1)} collective-permute-done((f32[2,8,1152]{2,1,0:T(8,128)S(1)}, f32[2,8,1152]{2,1,0:T(8,128)S(1)}, u32[]{:S(2)}, u32[]{:S(2)}) %collective-permute-start.32) | collective-permute-done | bytes 73760 | tf_op jit(solution)/shard_map/ppermute | solution.py:40
  (64 shorter events, 19.4 us)
Async XLA Ops:
  3.5 12.6 %collective-permute-start = (bf16[4,32,1152]{2,1,0:T(8,128)(2,1)}, bf16[4,32,1152]{2,1,0:T(8,128)(2,1)S(1)}, u32[]{:S(2)}, u32[]{:S(2)}) collective-permute-start(bf16[4,32,1152]{2,1,0:T(8,128)(2,1)} %get-tuple-element.60), channel_id=1, source_target_pairs={{0,64},{4,12},{8,72},{12,20},{16,80},{20,28},{24,88},{28,4},{32,96... | collective-permute-start | bytes 884744 | tf_op jit(solution)/shard_map/ppermute | solution.py:52
  5.7 10.4 %collective-permute-start.1 = (bf16[4,32,1152]{2,1,0:T(8,128)(2,1)}, bf16[4,32,1152]{2,1,0:T(8,128)(2,1)S(1)}, u32[]{:S(2)}, u32[]{:S(2)}) collective-permute-start(bf16[4,32,1152]{2,1,0:T(8,128)(2,1)} %get-tuple-element.61), channel_id=1, source_target_pairs={{0,128},{4,20},{8,136},{12,28},{16,144},{20,4},{24,152},{28,12},{3... | collective-permute-start | bytes 884744 | tf_op jit(solution)/shard_map/ppermute | solution.py:52
  8.4 7.8 %collective-permute-start.2 = (bf16[4,32,1152]{2,1,0:T(8,128)(2,1)}, bf16[4,32,1152]{2,1,0:T(8,128)(2,1)S(1)}, u32[]{:S(2)}, u32[]{:S(2)}) collective-permute-start(bf16[4,32,1152]{2,1,0:T(8,128)(2,1)} %get-tuple-element.62), channel_id=1, source_target_pairs={{0,192},{4,28},{8,200},{12,4},{16,208},{20,12},{24,216},{28,20},{3... | collective-permute-start | bytes 884744 | tf_op jit(solution)/shard_map/ppermute | solution.py:52
  9.4 22.8 %collective-permute-start.7 = (bf16[288,512]{1,0:T(8,128)(2,1)}, bf16[288,512]{1,0:T(8,128)(2,1)S(1)}, u32[]{:S(2)}, u32[]{:S(2)}) collective-permute-start(bf16[288,512]{1,0:T(8,128)(2,1)} %get-tuple-element.67), channel_id=1, source_target_pairs={{0,1},{1,2},{2,3},{3,0},{4,5},{5,6},{6,7},{7,4},{8,9},{9,10},{10,1... | collective-permute-start | bytes 884744 | tf_op jit(solution)/shard_map/ppermute | solution.py:40
  12.4 19.9 %collective-permute-start.8 = (bf16[288,512]{1,0:T(8,128)(2,1)}, bf16[288,512]{1,0:T(8,128)(2,1)S(1)}, u32[]{:S(2)}, u32[]{:S(2)}) collective-permute-start(bf16[288,512]{1,0:T(8,128)(2,1)} %get-tuple-element.68), channel_id=1, source_target_pairs={{0,3},{1,0},{2,1},{3,2},{4,7},{5,4},{6,5},{7,6},{8,11},{9,8},{10,9... | collective-permute-start | bytes 884744 | tf_op jit(solution)/shard_map/ppermute | solution.py:40
  18.4 5.3 %collective-permute-start.4 = (bf16[32,1152]{1,0:T(8,128)(2,1)S(1)}, bf16[32,1152]{1,0:T(8,128)(2,1)S(1)}, u32[]{:S(2)}, u32[]{:S(2)}) collective-permute-start(bf16[32,1152]{1,0:T(8,128)(2,1)S(1)} %get-tuple-element.65), channel_id=1, source_target_pairs={{0,16},{4,132},{8,24},{12,140},{16,0},{20,148},{24,8},{28,156},{32... | collective-permute-start | bytes 221192 | tf_op jit(solution)/shard_map/ppermute | solution.py:52
  24.4 7.9 %collective-permute-start.6 = (bf16[32,1152]{1,0:T(8,128)(2,1)S(1)}, bf16[32,1152]{1,0:T(8,128)(2,1)S(1)}, u32[]{:S(2)}, u32[]{:S(2)}) collective-permute-start(bf16[32,1152]{1,0:T(8,128)(2,1)S(1)} %shard_map.70.here), channel_id=1, source_target_pairs={{0,32},{32,0},{1,33},{33,1},{2,34},{34,2},{3,35},{35,3},{4,36},{36... | collective-permute-start | bytes 221192 | tf_op jit(solution)/shard_map/ppermute | solution.py:40
  26.2 9.7 %collective-permute-start.12 = (bf16[288,256]{1,0:T(8,128)(2,1)S(1)}, bf16[288,256]{1,0:T(8,128)(2,1)S(1)}, u32[]{:S(2)}, u32[]{:S(2)}) collective-permute-start(bf16[288,256]{1,0:T(8,128)(2,1)S(1)} %get-tuple-element.70), channel_id=1, source_target_pairs={{0,2},{1,3},{2,0},{3,1},{4,6},{5,7},{6,4},{7,5},{8,10},{9,11},{10,... | collective-permute-start | bytes 442376 | tf_op jit(solution)/shard_map/ppermute | solution.py:40
  40.6 12.6 %collective-permute-start.13 = (bf16[128,1152]{1,0:T(8,128)(2,1)S(1)}, bf16[128,1152]{1,0:T(8,128)(2,1)S(1)}, u32[]{:S(2)}, u32[]{:S(2)}) collective-permute-start(bf16[128,1152]{1,0:T(8,128)(2,1)S(1)} %shard_map.73.refs_0_), channel_id=1, source_target_pairs={{0,64},{4,12},{8,72},{12,20},{16,80},{20,28},{24,88},{28,4},{32,96... | collective-permute-start | bytes 884744 | tf_op jit(solution)/shard_map/ppermute | solution.py:52
  40.8 12.4 %collective-permute-start.14 = (bf16[128,1152]{1,0:T(8,128)(2,1)S(1)}, bf16[128,1152]{1,0:T(8,128)(2,1)S(1)}, u32[]{:S(2)}, u32[]{:S(2)}) collective-permute-start(bf16[128,1152]{1,0:T(8,128)(2,1)S(1)} %shard_map.73.refs_0_), channel_id=1, source_target_pairs={{0,128},{4,20},{8,136},{12,28},{16,144},{20,4},{24,152},{28,12},{3... | collective-permute-start | bytes 884744 | tf_op jit(solution)/shard_map/ppermute | solution.py:52
  43.2 10.1 %collective-permute-start.15 = (bf16[128,1152]{1,0:T(8,128)(2,1)S(1)}, bf16[128,1152]{1,0:T(8,128)(2,1)S(1)}, u32[]{:S(2)}, u32[]{:S(2)}) collective-permute-start(bf16[128,1152]{1,0:T(8,128)(2,1)S(1)} %shard_map.73.refs_0_), channel_id=1, source_target_pairs={{0,192},{4,28},{8,200},{12,4},{16,208},{20,12},{24,216},{28,20},{3... | collective-permute-start | bytes 884744 | tf_op jit(solution)/shard_map/ppermute | solution.py:52
  44.2 9.0 %collective-permute-start.16 = (bf16[288,256]{1,0:T(8,128)(2,1)S(1)}, bf16[288,256]{1,0:T(8,128)(2,1)S(1)}, u32[]{:S(2)}, u32[]{:S(2)}) collective-permute-start(bf16[288,256]{1,0:T(8,128)(2,1)S(1)} %get-tuple-element.75), channel_id=1, source_target_pairs={{0,2},{1,3},{2,0},{3,1},{4,6},{5,7},{6,4},{7,5},{8,10},{9,11},{10,... | collective-permute-start | bytes 442376 | tf_op jit(solution)/shard_map/ppermute | solution.py:40
  53.3 13.9 %collective-permute-start.17 = (bf16[128,1152]{1,0:T(8,128)(2,1)S(1)}, bf16[128,1152]{1,0:T(8,128)(2,1)S(1)}, u32[]{:S(2)}, u32[]{:S(2)}) collective-permute-start(bf16[128,1152]{1,0:T(8,128)(2,1)S(1)} %shard_map.73.refs_0_), channel_id=1, source_target_pairs={{0,4},{4,0},{1,5},{5,1},{2,6},{6,2},{3,7},{7,3},{8,12},{12,8},{9,1... | collective-permute-start | bytes 884744 | tf_op jit(solution)/shard_map/ppermute | solution.py:40
  61.2 5.9 %collective-permute-start.18 = (bf16[128,1152]{1,0:T(8,128)(2,1)S(1)}, bf16[128,1152]{1,0:T(8,128)(2,1)S(1)}, u32[]{:S(2)}, u32[]{:S(2)}) collective-permute-start(bf16[128,1152]{1,0:T(8,128)(2,1)S(1)} %collective-permute-done.13.refs_1_), channel_id=1, source_target_pairs={{0,4},{4,0},{1,5},{5,1},{2,6},{6,2},{3,7},{7,3},{8,12},{12,8},{9,1... | collective-permute-start | bytes 884744 | tf_op jit(solution)/shard_map/ppermute | solution.py:40
  61.3 5.8 %collective-permute-start.19 = (bf16[128,1152]{1,0:T(8,128)(2,1)S(1)}, bf16[128,1152]{1,0:T(8,128)(2,1)S(1)}, u32[]{:S(2)}, u32[]{:S(2)}) collective-permute-start(bf16[128,1152]{1,0:T(8,128)(2,1)S(1)} %collective-permute-done.14.refs_2_), channel_id=1, source_target_pairs={{0,4},{4,0},{1,5},{5,1},{2,6},{6,2},{3,7},{7,3},{8,12},{12,8},{9,1... | collective-permute-start | bytes 884744 | tf_op jit(solution)/shard_map/ppermute | solution.py:40
  61.7 5.4 %collective-permute-start.20 = (bf16[128,1152]{1,0:T(8,128)(2,1)S(1)}, bf16[128,1152]{1,0:T(8,128)(2,1)S(1)}, u32[]{:S(2)}, u32[]{:S(2)}) collective-permute-start(bf16[128,1152]{1,0:T(8,128)(2,1)S(1)} %collective-permute-done.15.refs_3_), channel_id=1, source_target_pairs={{0,4},{4,0},{1,5},{5,1},{2,6},{6,2},{3,7},{7,3},{8,12},{12,8},{9,1... | collective-permute-start | bytes 884744 | tf_op jit(solution)/shard_map/ppermute | solution.py:40
  66.6 7.9 %collective-permute-start.23 = (bf16[16,16,1152]{2,1,0:T(8,128)(2,1)S(1)}, bf16[16,16,1152]{2,1,0:T(8,128)(2,1)S(1)}, u32[]{:S(2)}, u32[]{:S(2)}) collective-permute-start(bf16[16,16,1152]{2,1,0:T(8,128)(2,1)S(1)} %get-tuple-element.97), channel_id=1, source_target_pairs={{0,4},{4,0},{1,5},{5,1},{2,6},{6,2},{3,7},{7,3},{8,12},{12,8},{9,1... | collective-permute-start | bytes 1769480 | tf_op jit(solution)/shard_map/ppermute | solution.py:40
  70.8 15.9 %collective-permute-start.27 = (bf16[288,512]{1,0:T(8,128)(2,1)S(1)}, bf16[288,512]{1,0:T(8,128)(2,1)S(1)}, u32[]{:S(2)}, u32[]{:S(2)}) collective-permute-start(bf16[288,512]{1,0:T(8,128)(2,1)S(1)} %get-tuple-element.102), channel_id=1, source_target_pairs={{0,1},{1,2},{2,3},{3,0},{4,5},{5,6},{6,7},{7,4},{8,9},{9,10},{10,1... | collective-permute-start | bytes 884744 | tf_op jit(solution)/shard_map/ppermute | solution.py:40
  70.9 22.2 %collective-permute-start.28 = (bf16[288,512]{1,0:T(8,128)(2,1)S(1)}, bf16[288,512]{1,0:T(8,128)(2,1)S(1)}, u32[]{:S(2)}, u32[]{:S(2)}) collective-permute-start(bf16[288,512]{1,0:T(8,128)(2,1)S(1)} %get-tuple-element.103), channel_id=1, source_target_pairs={{0,3},{1,0},{2,1},{3,2},{4,7},{5,4},{6,5},{7,6},{8,11},{9,8},{10,9... | collective-permute-start | bytes 884744 | tf_op jit(solution)/shard_map/ppermute | solution.py:40
  74.7 18.4 %collective-permute-start.24 = (bf16[4,32,1152]{2,1,0:T(8,128)(2,1)S(1)}, bf16[4,32,1152]{2,1,0:T(8,128)(2,1)S(1)}, u32[]{:S(2)}, u32[]{:S(2)}) collective-permute-start(bf16[4,32,1152]{2,1,0:T(8,128)(2,1)S(1)} %get-tuple-element.99), channel_id=1, source_target_pairs={{0,64},{4,12},{8,72},{12,20},{16,80},{20,28},{24,88},{28,4},{32,96... | collective-permute-start | bytes 884744 | tf_op jit(solution)/shard_map/ppermute | solution.py:52
  74.8 18.3 %collective-permute-start.25 = (bf16[4,32,1152]{2,1,0:T(8,128)(2,1)S(1)}, bf16[4,32,1152]{2,1,0:T(8,128)(2,1)S(1)}, u32[]{:S(2)}, u32[]{:S(2)}) collective-permute-start(bf16[4,32,1152]{2,1,0:T(8,128)(2,1)S(1)} %get-tuple-element.100), channel_id=1, source_target_pairs={{0,128},{4,20},{8,136},{12,28},{16,144},{20,4},{24,152},{28,12},{3... | collective-permute-start | bytes 884744 | tf_op jit(solution)/shard_map/ppermute | solution.py:52
  75.9 17.3 %collective-permute-start.26 = (bf16[4,32,1152]{2,1,0:T(8,128)(2,1)S(1)}, bf16[4,32,1152]{2,1,0:T(8,128)(2,1)S(1)}, u32[]{:S(2)}, u32[]{:S(2)}) collective-permute-start(bf16[4,32,1152]{2,1,0:T(8,128)(2,1)S(1)} %get-tuple-element.101), channel_id=1, source_target_pairs={{0,192},{4,28},{8,200},{12,4},{16,208},{20,12},{24,216},{28,20},{3... | collective-permute-start | bytes 884744 | tf_op jit(solution)/shard_map/ppermute | solution.py:52
  86.7 15.2 %collective-permute-start.21 = (bf16[288,512]{1,0:T(8,128)(2,1)S(1)}, bf16[288,512]{1,0:T(8,128)(2,1)S(1)}, u32[]{:S(2)}, u32[]{:S(2)}) collective-permute-start(bf16[288,512]{1,0:T(8,128)(2,1)S(1)} %get-tuple-element.92), channel_id=1, source_target_pairs={{0,2},{1,3},{2,0},{3,1},{4,6},{5,7},{6,4},{7,5},{8,10},{9,11},{10,... | collective-permute-start | bytes 884744 | tf_op jit(solution)/shard_map/ppermute | solution.py:40
  100.6 8.3 %collective-permute-start.32 = (f32[2,8,1152]{2,1,0:T(8,128)S(1)}, f32[2,8,1152]{2,1,0:T(8,128)S(1)}, u32[]{:S(2)}, u32[]{:S(2)}) collective-permute-start(f32[2,8,1152]{2,1,0:T(8,128)S(1)} %get-tuple-element.115), channel_id=1, source_target_pairs={{0,32},{32,0},{1,33},{33,1},{2,34},{34,2},{3,35},{35,3},{4,36},{36... | collective-permute-start | bytes 221192 | tf_op jit(solution)/shard_map/ppermute | solution.py:40
  (12 other events, 103.6 us)

commit v7 on v6

--- a/solution.py
+++ b/solution.py
@@ -91,17 +91,19 @@
     run(copies)
 
 
-def cut_kernel(captions, pictures, *refs):
-    chunks, (own, one, three, text_done, done) = refs[:4], refs[4:]
+def cut_text_kernel(captions, *refs):
+    chunks, done = refs[:4], refs[4]
     place = spot()[1]
-    copies = [
-        pltpu.make_async_copy(captions.at[ahead(place, d)], chunk, text_done.at[d]) for d, chunk in enumerate(chunks)
-    ]
-    for copy in copies:
-        copy.start()
+    run(
+        [
+            pltpu.make_async_copy(captions.at[ahead(place, d)], chunk, done.at[d])
+            for d, chunk in enumerate(chunks)
+        ]
+    )
+
+
+def cut_near_kernel(pictures, own, one, three, done):
     cut_pieces([(own, 0, 0), (one, 1, 0), (three, 3, 0)], pictures, done)
-    for copy in copies:
-        copy.wait()
 
 
 def cut_far_kernel(pictures, low, high, done):
@@ -181,8 +183,8 @@
         weights[rows, :] = ((share - positive) * times).astype(BF16)
 
 
-def slab_terms(other, images, weights, by_owner, keep, send):
-    core, place = lax.axis_index("c"), spot()[1 + other]
+def slab_terms(other, images, weights, keep, send):
+    core, x = lax.axis_index("c"), spot()[1 + other]
     for d in range(4):
         terms = lax.dot_general(
             weights[CHUNK * d : CHUNK * d + CHUNK, :],
@@ -190,16 +192,16 @@
             (((1,), (1,)), ((), ())),
             preferred_element_type=F32,
         )
-        for inner in range(4):
-            x, z = back(place, d), inner >> 1
-            for low in range(2):
-                y = (inner & 1) * 2 + low
-                spots = (x * 4 + y, y * 4 + x)
-                for c in range(2):
-                    at = PIECE * inner + 16 * low + 8 * c
-                    by_owner[c, spots[c], 8 * z : 8 * z + 8, :] = terms[at : at + 8, :]
-    keep[...] = by_owner[core]
-    send[...] = by_owner[1 - core].astype(BF16)
+        outer = back(x, d)
+        for y in range(4):
+            rows = []
+            for c in range(2):
+                at = 16 * y + 8 * c
+                rows.append(jnp.concatenate([terms[at : at + 8, :], terms[at + 64 : at + 72, :]]))
+            straight, turned = outer * 4 + y, y * 4 + outer
+            kept, sent = (jnp.where(core == 0, *pair) for pair in (rows, rows[::-1]))
+            keep[jnp.where(core == 0, straight, turned)] = kept
+            send[jnp.where(core == 0, turned, straight)] = sent.astype(BF16)
 
 
 def turned_product(text, weights):
@@ -207,16 +209,16 @@
 
 
 def own_kernel(start, multiplier, offset, *refs):
-    chunks, (images, keep, send, grad, text, weights, by_owner) = refs[:4], refs[4:]
+    chunks, (images, keep, send, grad, text, weights) = refs[:4], refs[4:]
     slab_weights(0, start, multiplier, offset, chunks, images, text, weights)
-    slab_terms(0, images, weights, by_owner, keep, send)
+    slab_terms(0, images, weights, keep, send)
     grad[...] = turned_product(text, weights)
 
 
 def other_kernel(start, multiplier, offset, *refs):
-    chunks, (images, keep, send, weights, text, by_owner) = refs[:4], refs[4:]
+    chunks, (images, keep, send, weights, text) = refs[:4], refs[4:]
     slab_weights(1, start, multiplier, offset, chunks, images, text, weights)
-    slab_terms(1, images, weights, by_owner, keep, send)
+    slab_terms(1, images, weights, keep, send)
 
 
 def pieces_kernel(*refs):
@@ -251,7 +253,7 @@
     total[...] = (own[...] + one[...].astype(F32)) + (two[...].astype(F32) + three[...].astype(F32))
     for slab, at in ((0, step), (1, 1 - step)):
         keep[at] = total[window(2 * slab + z_lo, 8), :]
-        send[at] = total[window(2 * slab + 1 - z_lo, 8), :]
+        send[at] = total[window(2 * slab + 1 - z_lo, 8), :].astype(BF16)
 
 
 def lay_copies(places, out, done):
@@ -300,15 +302,11 @@
     scalars, scalar_specs = (start, multiplier, offset), [SMEM] * 3
 
     pictures = pictures.T
-    *chunks, near, one, three = call(
-        cut_kernel,
-        [like(4, PIECE, D)] * 4 + [like(PART, ROWS)] * 3,
-        [HBM] * 2,
-        [DMA((4,)), DMA((3,))],
-        moved=4,
-        vmem=58 << 20,
-    )(captions.reshape(4, 4, PIECE, D), pictures)
-
+    near, one, three = call(cut_near_kernel, [like(PART, ROWS)] * 3, [HBM], [DMA((3,))], moved=2)(pictures)
+
+    chunks = call(cut_text_kernel, [like(4, PIECE, D)] * 4, [HBM], [DMA((4,))], moved=2, vmem=60 << 20)(
+        captions.reshape(4, 4, PIECE, D)
+    )
     chunks = [chunks[0]] + [along(chunks[d], True, d) for d in (1, 2, 3)]
     one, three = shift(one, "t", 1, PEERS), shift(three, "t", 3, PEERS)
     pieces = call(first_pick_kernel, [like(PIECE, D)] * 4, [SMEM] + [VMEM] * 4)(start, *chunks)
@@ -328,13 +326,13 @@
     theirs = [shift(chunk, "c", 1, 2) for chunk in own]
     images = call(unit_columns_kernel, like(D, ROWS), [VMEM] * 5, moved=3)(near, one, three, low, high)
 
-    text_scratch, owner_scratch = pltpu.VMEM((ROWS, D), BF16), pltpu.VMEM((2,) + OWNED, F32)
+    text_scratch = pltpu.VMEM((ROWS, D), BF16)
     kept, sent, square = like(*OWNED, dtype=F32), like(*OWNED), like(ROWS, ROWS)
     keep_own, send_own, grad = call(
         own_kernel,
         [kept, sent, like(D, ROWS, dtype=F32)],
         scalar_specs + [VMEM] * 5,
-        [text_scratch, pltpu.VMEM((ROWS, ROWS), BF16), owner_scratch],
+        [text_scratch, pltpu.VMEM((ROWS, ROWS), BF16)],
         products=3,
         moved=8,
     )(*scalars, *own, images)
@@ -342,7 +340,7 @@
         other_kernel,
         [kept, sent, square],
         scalar_specs + [VMEM] * 5,
-        [text_scratch, owner_scratch],
+        [text_scratch],
         products=2,
         moved=5,
     )(*scalars, *theirs, images)
@@ -361,7 +359,6 @@
         join_kernel, [like(4, PIECE, D, dtype=F32)] + [like(4, PIECE, D)] * 3, [VMEM] * 4, moved=4
     )(keep_own, shift(send_other, "c", 1, 2), keep_other, shift(send_own, "c", 1, 2))
     parts = [parts[0]] + [along(parts[d], True, d) for d in (1, 2, 3)]
-    *parts, returned[1], returned[3] = lax.optimization_barrier((*parts, returned[1], returned[3]))
     parts = call(
         first_sum_kernel,
         [like(PIECE, D, dtype=F32)] + [like(PIECE, D)] * 3,
@@ -370,9 +367,9 @@
     )(*parts)
     parts = [parts[0]] + [along(parts[d], False, d) for d in (1, 2, 3)]
     keep, send = call(
-        second_sum_kernel, [like(2, 8, D, dtype=F32)] * 2, [SMEM] + [VMEM] * 4, [pltpu.VMEM((PIECE, D), F32)]
+        second_sum_kernel, [like(2, 8, D, dtype=F32), like(2, 8, D)], [SMEM] + [VMEM] * 4, [pltpu.VMEM((PIECE, D), F32)]
     )(start, *parts)
-    text_grad = keep + shift(send, "zl", 1, 2)
+    text_grad = keep + shift(send, "zl", 1, 2).astype(F32)
     image_grad = lay_far(returned[2], lay_near(returned[0], returned[1], returned[3]))
     return image_grad.T, text_grad[:, None]
 

time: 110 us -> 107 us (0.973)
  the two profiles are of different devices: /device:TPU:1 before, /device:TPU:96 now
where the time goes in v7:
time: 107 us; the launch traced here: 106 us
  starting transfers between devices  51.3 us (48%)
  waiting for transfers between devices  39.4 us (37%)
  Pallas kernels  12.3 us (11%)
  between operations  2.82 us (3%)
    ppermute x15, starting transfers between devices, shift(): lax.ppermute(value, axis, [(i, (i + by) % size) for i in range(size)])  25.8 us
    ppermute x18, starting transfers between devices, along(): return lax.ppermute(value, DP, pairs)  25.5 us
    ppermute x18, waiting for transfers between devices, along(): return lax.ppermute(value, DP, pairs)  23 us
    ppermute x15, waiting for transfers between devices, shift(): lax.ppermute(value, axis, [(i, (i + by) % size) for i in range(size)])  16.4 us
    pallas_call x1, Pallas kernels, per_device(): call(own_kernel, [kept, sent, like(D, ROWS, dtype=F32)], scalar_specs + [...  3.02 us
    pallas_call x1, Pallas kernels, per_device(): call(cut_text_kernel, [like(4, PIECE, D)] * 4, [HBM], [DMA((4,))], moved=...  2.39 us
    pallas_call x1, Pallas kernels, per_device(): call(other_kernel, [kept, sent, square], scalar_specs + [VMEM] * 5, [text...  2.37 us
  transfers between devices with their start and end apart: 33, of which 13 were waited for; matrix products, arithmetic and copies ran while one was open for 0% of the time, Pallas kernels for 9%

profile of v7, /device:TPU:96, one launch (start us, length us, event | category | flops | bytes accessed | tf_op | source)
XLA Modules:
  0.0 106.4 jit_solution(5041946713316487217)
XLA Ops:
  0.6 2.4 %shard_map.68 = (bf16[4,32,1152]{2,1,0:T(8,128)(2,1)}, bf16[4,32,1152]{2,1,0:T(8,128)(2,1)}, bf16[4,32,1152]{2,1,0:T(8,128)(2,1)}, bf16[4,32,1152]{2,1,0:T(8,128)(2,1)}) custom-call(bf16[4,4,32,1152]{3,2,1,0:T(8,128)(2,1)} %bitcast.23), custom_call_target="tpu_custom_call" | custom-call | bytes 2097152 | tf_op jit(solution)/shard_map/pallas_call | solution.py:307
  4.6 2.7 %collective-permute-start.1 = (bf16[4,32,1152]{2,1,0:T(8,128)(2,1)}, bf16[4,32,1152]{2,1,0:T(8,128)(2,1)S(1)}, u32[]{:S(2)}, u32[]{:S(2)}) collective-permute-start(bf16[4,32,1152]{2,1,0:T(8,128)(2,1)} %get-tuple-element.55), channel_id=1, source_target_pairs={{0,128},{4,20},{8,136},{12,28},{16,144},{20,4},{24,152},{28,12},{3... | collective-permute-start | bytes 884744 | tf_op jit(solution)/shard_map/ppermute | solution.py:52
  9.6 3.7 %collective-permute-start.7 = (bf16[288,512]{1,0:T(8,128)(2,1)}, bf16[288,512]{1,0:T(8,128)(2,1)S(1)}, u32[]{:S(2)}, u32[]{:S(2)}) collective-permute-start(bf16[288,512]{1,0:T(8,128)(2,1)} %get-tuple-element.61), channel_id=1, source_target_pairs={{0,1},{1,2},{2,3},{3,0},{4,5},{5,6},{6,7},{7,4},{8,9},{9,10},{10,1... | collective-permute-start | bytes 884744 | tf_op jit(solution)/shard_map/ppermute | solution.py:40
  15.5 1.7 %collective-permute-start.3 = (bf16[32,1152]{1,0:T(8,128)(2,1)S(1)}, bf16[32,1152]{1,0:T(8,128)(2,1)S(1)}, u32[]{:S(2)}, u32[]{:S(2)}) collective-permute-start(bf16[32,1152]{1,0:T(8,128)(2,1)S(1)} %get-tuple-element.58), channel_id=1, source_target_pairs={{0,8},{4,68},{8,16},{12,76},{16,24},{20,84},{24,0},{28,92},{32,40}... | collective-permute-start | bytes 221192 | tf_op jit(solution)/shard_map/ppermute | solution.py:52
  17.1 2.9 %collective-permute-start.4 = (bf16[32,1152]{1,0:T(8,128)(2,1)S(1)}, bf16[32,1152]{1,0:T(8,128)(2,1)S(1)}, u32[]{:S(2)}, u32[]{:S(2)}) collective-permute-start(bf16[32,1152]{1,0:T(8,128)(2,1)S(1)} %get-tuple-element.59), channel_id=1, source_target_pairs={{0,16},{4,132},{8,24},{12,140},{16,0},{20,148},{24,8},{28,156},{32... | collective-permute-start | bytes 221192 | tf_op jit(solution)/shard_map/ppermute | solution.py:52
  21.4 1.8 %collective-permute-done.4.refs_2_ = bf16[32,1152]{1,0:T(8,128)(2,1)S(1)} collective-permute-done((bf16[32,1152]{1,0:T(8,128)(2,1)S(1)}, bf16[32,1152]{1,0:T(8,128)(2,1)S(1)}, u32[]{:S(2)}, u32[]{:S(2)}) %collective-permute-start.4) | collective-permute-done | bytes 73760 | tf_op jit(solution)/shard_map/ppermute | solution.py:52
  24.5 5.5 %collective-permute-start.12 = (bf16[288,256]{1,0:T(8,128)(2,1)S(1)}, bf16[288,256]{1,0:T(8,128)(2,1)S(1)}, u32[]{:S(2)}, u32[]{:S(2)}) collective-permute-start(bf16[288,256]{1,0:T(8,128)(2,1)S(1)} %get-tuple-element.64), channel_id=1, source_target_pairs={{0,2},{1,3},{2,0},{3,1},{4,6},{5,7},{6,4},{7,5},{8,10},{9,11},{10,... | collective-permute-start | bytes 442376 | tf_op jit(solution)/shard_map/ppermute | solution.py:40
  31.9 1.7 %collective-permute-start.11 = (bf16[32,1152]{1,0:T(8,128)(2,1)S(1)}, bf16[32,1152]{1,0:T(8,128)(2,1)S(1)}, u32[]{:S(2)}, u32[]{:S(2)}) collective-permute-start(bf16[32,1152]{1,0:T(8,128)(2,1)S(1)} %shard_map.72.refs_0_), channel_id=1, source_target_pairs={{0,24},{4,196},{8,0},{12,204},{16,8},{20,212},{24,16},{28,220},{32... | collective-permute-start | bytes 221192 | tf_op jit(solution)/shard_map/ppermute | solution.py:52
  33.9 2.3 %collective-permute-done.12.two_low = bf16[288,256]{1,0:T(8,128)(2,1)S(1)} collective-permute-done((bf16[288,256]{1,0:T(8,128)(2,1)S(1)}, bf16[288,256]{1,0:T(8,128)(2,1)S(1)}, u32[]{:S(2)}, u32[]{:S(2)}) %collective-permute-start.12) | collective-permute-done | bytes 147488 | tf_op jit(solution)/shard_map/ppermute | solution.py:40
  36.8 2.4 %collective-permute-done.9.refs_1_ = bf16[32,1152]{1,0:T(8,128)(2,1)S(1)} collective-permute-done((bf16[32,1152]{1,0:T(8,128)(2,1)S(1)}, bf16[32,1152]{1,0:T(8,128)(2,1)S(1)}, u32[]{:S(2)}, u32[]{:S(2)}) %collective-permute-start.9) | collective-permute-done | bytes 73760 | tf_op jit(solution)/shard_map/ppermute | solution.py:52
  39.2 3.0 %collective-permute-start.13 = (bf16[128,1152]{1,0:T(8,128)(2,1)S(1)}, bf16[128,1152]{1,0:T(8,128)(2,1)S(1)}, u32[]{:S(2)}, u32[]{:S(2)}) collective-permute-start(bf16[128,1152]{1,0:T(8,128)(2,1)S(1)} %shard_map.74.refs_0_), channel_id=1, source_target_pairs={{0,64},{4,12},{8,72},{12,20},{16,80},{20,28},{24,88},{28,4},{32,96... | collective-permute-start | bytes 884744 | tf_op jit(solution)/shard_map/ppermute | solution.py:52
  42.2 1.9 %collective-permute-start.14 = (bf16[128,1152]{1,0:T(8,128)(2,1)S(1)}, bf16[128,1152]{1,0:T(8,128)(2,1)S(1)}, u32[]{:S(2)}, u32[]{:S(2)}) collective-permute-start(bf16[128,1152]{1,0:T(8,128)(2,1)S(1)} %shard_map.74.refs_0_), channel_id=1, source_target_pairs={{0,128},{4,20},{8,136},{12,28},{16,144},{20,4},{24,152},{28,12},{3... | collective-permute-start | bytes 884744 | tf_op jit(solution)/shard_map/ppermute | solution.py:52
  44.1 1.8 %collective-permute-start.15 = (bf16[128,1152]{1,0:T(8,128)(2,1)S(1)}, bf16[128,1152]{1,0:T(8,128)(2,1)S(1)}, u32[]{:S(2)}, u32[]{:S(2)}) collective-permute-start(bf16[128,1152]{1,0:T(8,128)(2,1)S(1)} %shard_map.74.refs_0_), channel_id=1, source_target_pairs={{0,192},{4,28},{8,200},{12,4},{16,208},{20,12},{24,216},{28,20},{3... | collective-permute-start | bytes 884744 | tf_op jit(solution)/shard_map/ppermute | solution.py:52
  45.9 7.2 %collective-permute-start.16 = (bf16[288,256]{1,0:T(8,128)(2,1)S(1)}, bf16[288,256]{1,0:T(8,128)(2,1)S(1)}, u32[]{:S(2)}, u32[]{:S(2)}) collective-permute-start(bf16[288,256]{1,0:T(8,128)(2,1)S(1)} %get-tuple-element.69), channel_id=1, source_target_pairs={{0,2},{1,3},{2,0},{3,1},{4,6},{5,7},{6,4},{7,5},{8,10},{9,11},{10,... | collective-permute-start | bytes 442376 | tf_op jit(solution)/shard_map/ppermute | solution.py:40
  53.1 4.7 %collective-permute-done.16.two_high = bf16[288,256]{1,0:T(8,128)(2,1)S(1)} collective-permute-done((bf16[288,256]{1,0:T(8,128)(2,1)S(1)}, bf16[288,256]{1,0:T(8,128)(2,1)S(1)}, u32[]{:S(2)}, u32[]{:S(2)}) %collective-permute-start.16) | collective-permute-done | bytes 147488 | tf_op jit(solution)/shard_map/ppermute | solution.py:40
  60.7 3.0 %shard_map.77 = (f32[16,16,1152]{2,1,0:T(8,128)S(1)}, bf16[16,16,1152]{2,1,0:T(8,128)(2,1)S(1)}, f32[1152,512]{1,0:T(8,128)S(1)}) custom-call(s32[1]{0:T(128)} %bitcast.14.start, f32[1]{0:T(128)} %bitcast.17.multiplier, f32[1]{0:T(128)} %bitcast.19.offset, bf16[128,1152]{1,0:T(8,128)(2,1)S(1)} %shard_map.74.refs_0_, ...), custom_call_target="tpu_custom_call" | custom-call | flops 1811939328 | bytes 8388608 | tf_op jit(solution)/shard_map/pallas_call | solution.py:331
  63.9 2.4 %shard_map.76 = (f32[16,16,1152]{2,1,0:T(8,128)S(1)}, bf16[16,16,1152]{2,1,0:T(8,128)(2,1)S(1)}, bf16[512,512]{1,0:T(8,128)(2,1)S(1)}) custom-call(s32[1]{0:T(128)} %bitcast.13.start, f32[1]{0:T(128)} %bitcast.16.multiplier, f32[1]{0:T(128)} %bitcast.18.offset, bf16[128,1152]{1,0:T(8,128)(2,1)S(1)} %collective-permute-done.17.refs_0_, ...), custom_call_target="tpu_custom_call" | custom-call | flops 1207959552 | bytes 5242880 | tf_op jit(solution)/shard_map/pallas_call | solution.py:339
  70.2 1.8 %collective-permute-start.28 = (bf16[4,32,1152]{2,1,0:T(8,128)(2,1)S(1)}, bf16[4,32,1152]{2,1,0:T(8,128)(2,1)S(1)}, u32[]{:S(2)}, u32[]{:S(2)}) collective-permute-start(bf16[4,32,1152]{2,1,0:T(8,128)(2,1)S(1)} %get-tuple-element.97), channel_id=1, source_target_pairs={{0,192},{4,28},{8,200},{12,4},{16,208},{20,12},{24,216},{28,20},{3... | collective-permute-start | bytes 884744 | tf_op jit(solution)/shard_map/ppermute | solution.py:52
  72.0 2.9 %collective-permute-start.23 = (bf16[288,512]{1,0:T(8,128)(2,1)S(1)}, bf16[288,512]{1,0:T(8,128)(2,1)S(1)}, u32[]{:S(2)}, u32[]{:S(2)}) collective-permute-start(bf16[288,512]{1,0:T(8,128)(2,1)S(1)} %get-tuple-element.89), channel_id=1, source_target_pairs={{0,3},{1,0},{2,1},{3,2},{4,7},{5,4},{6,5},{7,6},{8,11},{9,8},{10,9... | collective-permute-start | bytes 884744 | tf_op jit(solution)/shard_map/ppermute | solution.py:40
  74.9 4.9 %collective-permute-done.26.one = bf16[4,32,1152]{2,1,0:T(8,128)(2,1)S(1)} collective-permute-done((bf16[4,32,1152]{2,1,0:T(8,128)(2,1)S(1)}, bf16[4,32,1152]{2,1,0:T(8,128)(2,1)S(1)}, u32[]{:S(2)}, u32[]{:S(2)}) %collective-permute-start.26) | collective-permute-done | bytes 294944 | tf_op jit(solution)/shard_map/ppermute | solution.py:52
  79.8 4.3 %collective-permute-start.21 = (bf16[288,512]{1,0:T(8,128)(2,1)S(1)}, bf16[288,512]{1,0:T(8,128)(2,1)S(1)}, u32[]{:S(2)}, u32[]{:S(2)}) collective-permute-start(bf16[288,512]{1,0:T(8,128)(2,1)S(1)} %get-tuple-element.86), channel_id=1, source_target_pairs={{0,2},{1,3},{2,0},{3,1},{4,6},{5,7},{6,4},{7,5},{8,10},{9,11},{10,... | collective-permute-start | bytes 884744 | tf_op jit(solution)/shard_map/ppermute | solution.py:40
  84.6 6.2 %collective-permute-done.29.one = bf16[32,1152]{1,0:T(8,128)(2,1)S(1)} collective-permute-done((bf16[32,1152]{1,0:T(8,128)(2,1)S(1)}, bf16[32,1152]{1,0:T(8,128)(2,1)S(1)}, u32[]{:S(2)}, u32[]{:S(2)}) %collective-permute-start.29) | collective-permute-done | bytes 73760 | tf_op jit(solution)/shard_map/ppermute | solution.py:52
  90.9 4.3 %collective-permute-done.31.three = bf16[32,1152]{1,0:T(8,128)(2,1)S(1)} collective-permute-done((bf16[32,1152]{1,0:T(8,128)(2,1)S(1)}, bf16[32,1152]{1,0:T(8,128)(2,1)S(1)}, u32[]{:S(2)}, u32[]{:S(2)}) %collective-permute-start.31) | collective-permute-done | bytes 73760 | tf_op jit(solution)/shard_map/ppermute | solution.py:52
  96.3 8.7 %collective-permute-done.21.two = bf16[288,512]{1,0:T(8,128)(2,1)S(1)} collective-permute-done((bf16[288,512]{1,0:T(8,128)(2,1)S(1)}, bf16[288,512]{1,0:T(8,128)(2,1)S(1)}, u32[]{:S(2)}, u32[]{:S(2)}) %collective-permute-start.21) | collective-permute-done | bytes 294944 | tf_op jit(solution)/shard_map/ppermute | solution.py:40
  (63 shorter events, 19.5 us)
Async XLA Ops:
  3.0 10.9 %collective-permute-start = (bf16[4,32,1152]{2,1,0:T(8,128)(2,1)}, bf16[4,32,1152]{2,1,0:T(8,128)(2,1)S(1)}, u32[]{:S(2)}, u32[]{:S(2)}) collective-permute-start(bf16[4,32,1152]{2,1,0:T(8,128)(2,1)} %get-tuple-element.54), channel_id=1, source_target_pairs={{0,64},{4,12},{8,72},{12,20},{16,80},{20,28},{24,88},{28,4},{32,96... | collective-permute-start | bytes 884744 | tf_op jit(solution)/shard_map/ppermute | solution.py:52
  4.6 10.8 %collective-permute-start.1 = (bf16[4,32,1152]{2,1,0:T(8,128)(2,1)}, bf16[4,32,1152]{2,1,0:T(8,128)(2,1)S(1)}, u32[]{:S(2)}, u32[]{:S(2)}) collective-permute-start(bf16[4,32,1152]{2,1,0:T(8,128)(2,1)} %get-tuple-element.55), channel_id=1, source_target_pairs={{0,128},{4,20},{8,136},{12,28},{16,144},{20,4},{24,152},{28,12},{3... | collective-permute-start | bytes 884744 | tf_op jit(solution)/shard_map/ppermute | solution.py:52
  7.3 8.1 %collective-permute-start.2 = (bf16[4,32,1152]{2,1,0:T(8,128)(2,1)}, bf16[4,32,1152]{2,1,0:T(8,128)(2,1)S(1)}, u32[]{:S(2)}, u32[]{:S(2)}) collective-permute-start(bf16[4,32,1152]{2,1,0:T(8,128)(2,1)} %get-tuple-element.56), channel_id=1, source_target_pairs={{0,192},{4,28},{8,200},{12,4},{16,208},{20,12},{24,216},{28,20},{3... | collective-permute-start | bytes 884744 | tf_op jit(solution)/shard_map/ppermute | solution.py:52
  9.6 20.4 %collective-permute-start.7 = (bf16[288,512]{1,0:T(8,128)(2,1)}, bf16[288,512]{1,0:T(8,128)(2,1)S(1)}, u32[]{:S(2)}, u32[]{:S(2)}) collective-permute-start(bf16[288,512]{1,0:T(8,128)(2,1)} %get-tuple-element.61), channel_id=1, source_target_pairs={{0,1},{1,2},{2,3},{3,0},{4,5},{5,6},{6,7},{7,4},{8,9},{9,10},{10,1... | collective-permute-start | bytes 884744 | tf_op jit(solution)/shard_map/ppermute | solution.py:40
  13.3 16.8 %collective-permute-start.8 = (bf16[288,512]{1,0:T(8,128)(2,1)S(1)}, bf16[288,512]{1,0:T(8,128)(2,1)S(1)}, u32[]{:S(2)}, u32[]{:S(2)}) collective-permute-start(bf16[288,512]{1,0:T(8,128)(2,1)S(1)} %get-tuple-element.62), channel_id=1, source_target_pairs={{0,3},{1,0},{2,1},{3,2},{4,7},{5,4},{6,5},{7,6},{8,11},{9,8},{10,9... | collective-permute-start | bytes 884744 | tf_op jit(solution)/shard_map/ppermute | solution.py:40
  15.5 5.9 %collective-permute-start.3 = (bf16[32,1152]{1,0:T(8,128)(2,1)S(1)}, bf16[32,1152]{1,0:T(8,128)(2,1)S(1)}, u32[]{:S(2)}, u32[]{:S(2)}) collective-permute-start(bf16[32,1152]{1,0:T(8,128)(2,1)S(1)} %get-tuple-element.58), channel_id=1, source_target_pairs={{0,8},{4,68},{8,16},{12,76},{16,24},{20,84},{24,0},{28,92},{32,40}... | collective-permute-start | bytes 221192 | tf_op jit(solution)/shard_map/ppermute | solution.py:52
  17.1 6.0 %collective-permute-start.4 = (bf16[32,1152]{1,0:T(8,128)(2,1)S(1)}, bf16[32,1152]{1,0:T(8,128)(2,1)S(1)}, u32[]{:S(2)}, u32[]{:S(2)}) collective-permute-start(bf16[32,1152]{1,0:T(8,128)(2,1)S(1)} %get-tuple-element.59), channel_id=1, source_target_pairs={{0,16},{4,132},{8,24},{12,140},{16,0},{20,148},{24,8},{28,156},{32... | collective-permute-start | bytes 221192 | tf_op jit(solution)/shard_map/ppermute | solution.py:52
  24.5 11.6 %collective-permute-start.12 = (bf16[288,256]{1,0:T(8,128)(2,1)S(1)}, bf16[288,256]{1,0:T(8,128)(2,1)S(1)}, u32[]{:S(2)}, u32[]{:S(2)}) collective-permute-start(bf16[288,256]{1,0:T(8,128)(2,1)S(1)} %get-tuple-element.64), channel_id=1, source_target_pairs={{0,2},{1,3},{2,0},{3,1},{4,6},{5,7},{6,4},{7,5},{8,10},{9,11},{10,... | collective-permute-start | bytes 442376 | tf_op jit(solution)/shard_map/ppermute | solution.py:40
  30.3 5.9 %collective-permute-start.10 = (bf16[32,1152]{1,0:T(8,128)(2,1)S(1)}, bf16[32,1152]{1,0:T(8,128)(2,1)S(1)}, u32[]{:S(2)}, u32[]{:S(2)}) collective-permute-start(bf16[32,1152]{1,0:T(8,128)(2,1)S(1)} %shard_map.72.refs_0_), channel_id=1, source_target_pairs={{0,16},{4,132},{8,24},{12,140},{16,0},{20,148},{24,8},{28,156},{32... | collective-permute-start | bytes 221192 | tf_op jit(solution)/shard_map/ppermute | solution.py:52
  39.2 18.6 %collective-permute-start.13 = (bf16[128,1152]{1,0:T(8,128)(2,1)S(1)}, bf16[128,1152]{1,0:T(8,128)(2,1)S(1)}, u32[]{:S(2)}, u32[]{:S(2)}) collective-permute-start(bf16[128,1152]{1,0:T(8,128)(2,1)S(1)} %shard_map.74.refs_0_), channel_id=1, source_target_pairs={{0,64},{4,12},{8,72},{12,20},{16,80},{20,28},{24,88},{28,4},{32,96... | collective-permute-start | bytes 884744 | tf_op jit(solution)/shard_map/ppermute | solution.py:52
  42.2 15.6 %collective-permute-start.14 = (bf16[128,1152]{1,0:T(8,128)(2,1)S(1)}, bf16[128,1152]{1,0:T(8,128)(2,1)S(1)}, u32[]{:S(2)}, u32[]{:S(2)}) collective-permute-start(bf16[128,1152]{1,0:T(8,128)(2,1)S(1)} %shard_map.74.refs_0_), channel_id=1, source_target_pairs={{0,128},{4,20},{8,136},{12,28},{16,144},{20,4},{24,152},{28,12},{3... | collective-permute-start | bytes 884744 | tf_op jit(solution)/shard_map/ppermute | solution.py:52
  44.1 13.7 %collective-permute-start.15 = (bf16[128,1152]{1,0:T(8,128)(2,1)S(1)}, bf16[128,1152]{1,0:T(8,128)(2,1)S(1)}, u32[]{:S(2)}, u32[]{:S(2)}) collective-permute-start(bf16[128,1152]{1,0:T(8,128)(2,1)S(1)} %shard_map.74.refs_0_), channel_id=1, source_target_pairs={{0,192},{4,28},{8,200},{12,4},{16,208},{20,12},{24,216},{28,20},{3... | collective-permute-start | bytes 884744 | tf_op jit(solution)/shard_map/ppermute | solution.py:52
  45.9 11.9 %collective-permute-start.16 = (bf16[288,256]{1,0:T(8,128)(2,1)S(1)}, bf16[288,256]{1,0:T(8,128)(2,1)S(1)}, u32[]{:S(2)}, u32[]{:S(2)}) collective-permute-start(bf16[288,256]{1,0:T(8,128)(2,1)S(1)} %get-tuple-element.69), channel_id=1, source_target_pairs={{0,2},{1,3},{2,0},{3,1},{4,6},{5,7},{6,4},{7,5},{8,10},{9,11},{10,... | collective-permute-start | bytes 442376 | tf_op jit(solution)/shard_map/ppermute | solution.py:40
  57.8 6.1 %collective-permute-start.17 = (bf16[128,1152]{1,0:T(8,128)(2,1)S(1)}, bf16[128,1152]{1,0:T(8,128)(2,1)S(1)}, u32[]{:S(2)}, u32[]{:S(2)}) collective-permute-start(bf16[128,1152]{1,0:T(8,128)(2,1)S(1)} %shard_map.74.refs_0_), channel_id=1, source_target_pairs={{0,4},{4,0},{1,5},{5,1},{2,6},{6,2},{3,7},{7,3},{8,12},{12,8},{9,1... | collective-permute-start | bytes 884744 | tf_op jit(solution)/shard_map/ppermute | solution.py:40
  58.1 5.8 %collective-permute-start.18 = (bf16[128,1152]{1,0:T(8,128)(2,1)S(1)}, bf16[128,1152]{1,0:T(8,128)(2,1)S(1)}, u32[]{:S(2)}, u32[]{:S(2)}) collective-permute-start(bf16[128,1152]{1,0:T(8,128)(2,1)S(1)} %collective-permute-done.13.refs_1_), channel_id=1, source_target_pairs={{0,4},{4,0},{1,5},{5,1},{2,6},{6,2},{3,7},{7,3},{8,12},{12,8},{9,1... | collective-permute-start | bytes 884744 | tf_op jit(solution)/shard_map/ppermute | solution.py:40
  68.7 11.2 %collective-permute-start.26 = (bf16[4,32,1152]{2,1,0:T(8,128)(2,1)S(1)}, bf16[4,32,1152]{2,1,0:T(8,128)(2,1)S(1)}, u32[]{:S(2)}, u32[]{:S(2)}) collective-permute-start(bf16[4,32,1152]{2,1,0:T(8,128)(2,1)S(1)} %get-tuple-element.95), channel_id=1, source_target_pairs={{0,64},{4,12},{8,72},{12,20},{16,80},{20,28},{24,88},{28,4},{32,96... | collective-permute-start | bytes 884744 | tf_op jit(solution)/shard_map/ppermute | solution.py:52
  68.8 15.4 %collective-permute-start.27 = (bf16[4,32,1152]{2,1,0:T(8,128)(2,1)S(1)}, bf16[4,32,1152]{2,1,0:T(8,128)(2,1)S(1)}, u32[]{:S(2)}, u32[]{:S(2)}) collective-permute-start(bf16[4,32,1152]{2,1,0:T(8,128)(2,1)S(1)} %get-tuple-element.96), channel_id=1, source_target_pairs={{0,128},{4,20},{8,136},{12,28},{16,144},{20,4},{24,152},{28,12},{3... | collective-permute-start | bytes 884744 | tf_op jit(solution)/shard_map/ppermute | solution.py:52
  70.2 14.0 %collective-permute-start.28 = (bf16[4,32,1152]{2,1,0:T(8,128)(2,1)S(1)}, bf16[4,32,1152]{2,1,0:T(8,128)(2,1)S(1)}, u32[]{:S(2)}, u32[]{:S(2)}) collective-permute-start(bf16[4,32,1152]{2,1,0:T(8,128)(2,1)S(1)} %get-tuple-element.97), channel_id=1, source_target_pairs={{0,192},{4,28},{8,200},{12,4},{16,208},{20,12},{24,216},{28,20},{3... | collective-permute-start | bytes 884744 | tf_op jit(solution)/shard_map/ppermute | solution.py:52
  72.0 23.4 %collective-permute-start.22 = (bf16[288,512]{1,0:T(8,128)(2,1)S(1)}, bf16[288,512]{1,0:T(8,128)(2,1)S(1)}, u32[]{:S(2)}, u32[]{:S(2)}) collective-permute-start(bf16[288,512]{1,0:T(8,128)(2,1)S(1)} %get-tuple-element.88), channel_id=1, source_target_pairs={{0,1},{1,2},{2,3},{3,0},{4,5},{5,6},{6,7},{7,4},{8,9},{9,10},{10,1... | collective-permute-start | bytes 884744 | tf_op jit(solution)/shard_map/ppermute | solution.py:40
  72.0 23.4 %collective-permute-start.23 = (bf16[288,512]{1,0:T(8,128)(2,1)S(1)}, bf16[288,512]{1,0:T(8,128)(2,1)S(1)}, u32[]{:S(2)}, u32[]{:S(2)}) collective-permute-start(bf16[288,512]{1,0:T(8,128)(2,1)S(1)} %get-tuple-element.89), channel_id=1, source_target_pairs={{0,3},{1,0},{2,1},{3,2},{4,7},{5,4},{6,5},{7,6},{8,11},{9,8},{10,9... | collective-permute-start | bytes 884744 | tf_op jit(solution)/shard_map/ppermute | solution.py:40
  79.8 25.2 %collective-permute-start.21 = (bf16[288,512]{1,0:T(8,128)(2,1)S(1)}, bf16[288,512]{1,0:T(8,128)(2,1)S(1)}, u32[]{:S(2)}, u32[]{:S(2)}) collective-permute-start(bf16[288,512]{1,0:T(8,128)(2,1)S(1)} %get-tuple-element.86), channel_id=1, source_target_pairs={{0,2},{1,3},{2,0},{3,1},{4,6},{5,7},{6,4},{7,5},{8,10},{9,11},{10,... | collective-permute-start | bytes 884744 | tf_op jit(solution)/shard_map/ppermute | solution.py:40
  84.4 6.4 %collective-permute-start.29 = (bf16[32,1152]{1,0:T(8,128)(2,1)S(1)}, bf16[32,1152]{1,0:T(8,128)(2,1)S(1)}, u32[]{:S(2)}, u32[]{:S(2)}) collective-permute-start(bf16[32,1152]{1,0:T(8,128)(2,1)S(1)} %get-tuple-element.99), channel_id=1, source_target_pairs={{0,8},{4,68},{8,16},{12,76},{16,24},{20,84},{24,0},{28,92},{32,40}... | collective-permute-start | bytes 221192 | tf_op jit(solution)/shard_map/ppermute | solution.py:52
  84.5 6.3 %collective-permute-start.30 = (bf16[32,1152]{1,0:T(8,128)(2,1)S(1)}, bf16[32,1152]{1,0:T(8,128)(2,1)S(1)}, u32[]{:S(2)}, u32[]{:S(2)}) collective-permute-start(bf16[32,1152]{1,0:T(8,128)(2,1)S(1)} %get-tuple-element.100), channel_id=1, source_target_pairs={{0,16},{4,132},{8,24},{12,140},{16,0},{20,148},{24,8},{28,156},{32... | collective-permute-start | bytes 221192 | tf_op jit(solution)/shard_map/ppermute | solution.py:52
  95.3 10.5 %collective-permute-start.32 = (bf16[2,8,1152]{2,1,0:T(8,128)(2,1)S(1)}, bf16[2,8,1152]{2,1,0:T(8,128)(2,1)S(1)}, u32[]{:S(2)}, u32[]{:S(2)}) collective-permute-start(bf16[2,8,1152]{2,1,0:T(8,128)(2,1)S(1)} %get-tuple-element.103), channel_id=1, source_target_pairs={{0,32},{32,0},{1,33},{33,1},{2,34},{34,2},{3,35},{35,3},{4,36},{36... | collective-permute-start | bytes 110600 | tf_op jit(solution)/shard_map/ppermute | solution.py:40
  (11 other events, 62.3 us)

commit v8 on v7

--- a/solution.py
+++ b/solution.py
@@ -21,7 +21,7 @@
     return jax.ShapeDtypeStruct(shape, dtype)
 
 
-def call(kernel, outs, ins, scratch=(), products=0, moved=1, vmem=16 << 20):
+def call(kernel, outs, ins, scratch=(), products=0, moved=1, vmem=12 << 20):
     single = not isinstance(outs, list)
     return pl.pallas_call(
         kernel,
@@ -322,7 +322,6 @@
     *pieces, low = lax.optimization_barrier((*pieces, low))
     chunk = call(gather_kernel, like(CHUNK, D), [VMEM] * 4)(*pieces)
     own = [chunk] + [along(chunk, True, d) for d in (1, 2, 3)]
-    *own, high = lax.optimization_barrier((*own, high))
     theirs = [shift(chunk, "c", 1, 2) for chunk in own]
     images = call(unit_columns_kernel, like(D, ROWS), [VMEM] * 5, moved=3)(near, one, three, low, high)
 

time: 107 us -> 106 us (level)
  the two profiles are of different devices: /device:TPU:96 before, /device:TPU:1 now
where the time goes in v8:
time: 106 us; the launch traced here: 104 us
  starting transfers between devices  62.1 us (59%)
  waiting for transfers between devices  25.8 us (24%)
  Pallas kernels  13 us (12%)
  between operations  2.82 us (3%)
    ppermute x15, starting transfers between devices, shift(): lax.ppermute(value, axis, [(i, (i + by) % size) for i in range(size)])  39.6 us
    ppermute x18, starting transfers between devices, along(): return lax.ppermute(value, DP, pairs)  22.5 us
    ppermute x18, waiting for transfers between devices, along(): return lax.ppermute(value, DP, pairs)  15.9 us
    ppermute x15, waiting for transfers between devices, shift(): lax.ppermute(value, axis, [(i, (i + by) % size) for i in range(size)])  9.9 us
    pallas_call x1, Pallas kernels, per_device(): call(own_kernel, [kept, sent, like(D, ROWS, dtype=F32)], scalar_specs + [...  3.01 us
    pallas_call x1, Pallas kernels, per_device(): call(cut_text_kernel, [like(4, PIECE, D)] * 4, [HBM], [DMA((4,))], moved=...  2.39 us
    pallas_call x1, Pallas kernels, per_device(): call(other_kernel, [kept, sent, square], scalar_specs + [VMEM] * 5, [text...  2.38 us
  transfers between devices with their start and end apart: 33, of which 12 were waited for; matrix products, arithmetic and copies ran while one was open for 0% of the time, Pallas kernels for 10%

profile of v8, /device:TPU:1, one launch (start us, length us, event | category | flops | bytes accessed | tf_op | source)
XLA Modules:
  0.0 104.4 jit_solution(13262521462403629524)
XLA Ops:
  0.6 2.4 %shard_map.68 = (bf16[4,32,1152]{2,1,0:T(8,128)(2,1)}, bf16[4,32,1152]{2,1,0:T(8,128)(2,1)}, bf16[4,32,1152]{2,1,0:T(8,128)(2,1)}, bf16[4,32,1152]{2,1,0:T(8,128)(2,1)}) custom-call(bf16[4,4,32,1152]{3,2,1,0:T(8,128)(2,1)} %bitcast.23), custom_call_target="tpu_custom_call" | custom-call | bytes 2097152 | tf_op jit(solution)/shard_map/pallas_call | solution.py:307
  3.0 2.2 %collective-permute-start = (bf16[4,32,1152]{2,1,0:T(8,128)(2,1)}, bf16[4,32,1152]{2,1,0:T(8,128)(2,1)S(1)}, u32[]{:S(2)}, u32[]{:S(2)}) collective-permute-start(bf16[4,32,1152]{2,1,0:T(8,128)(2,1)} %get-tuple-element.49), channel_id=1, source_target_pairs={{0,64},{4,12},{8,72},{12,20},{16,80},{20,28},{24,88},{28,4},{32,96... | collective-permute-start | bytes 884744 | tf_op jit(solution)/shard_map/ppermute | solution.py:52
  5.3 2.6 %collective-permute-start.1 = (bf16[4,32,1152]{2,1,0:T(8,128)(2,1)}, bf16[4,32,1152]{2,1,0:T(8,128)(2,1)S(1)}, u32[]{:S(2)}, u32[]{:S(2)}) collective-permute-start(bf16[4,32,1152]{2,1,0:T(8,128)(2,1)} %get-tuple-element.50), channel_id=1, source_target_pairs={{0,128},{4,20},{8,136},{12,28},{16,144},{20,4},{24,152},{28,12},{3... | collective-permute-start | bytes 884744 | tf_op jit(solution)/shard_map/ppermute | solution.py:52
  9.8 3.1 %collective-permute-start.7 = (bf16[288,512]{1,0:T(8,128)(2,1)}, bf16[288,512]{1,0:T(8,128)(2,1)S(1)}, u32[]{:S(2)}, u32[]{:S(2)}) collective-permute-start(bf16[288,512]{1,0:T(8,128)(2,1)} %get-tuple-element.56), channel_id=1, source_target_pairs={{0,1},{1,2},{2,3},{3,0},{4,5},{5,6},{6,7},{7,4},{8,9},{9,10},{10,1... | collective-permute-start | bytes 884744 | tf_op jit(solution)/shard_map/ppermute | solution.py:40
  12.8 3.1 %collective-permute-start.8 = (bf16[288,512]{1,0:T(8,128)(2,1)S(1)}, bf16[288,512]{1,0:T(8,128)(2,1)S(1)}, u32[]{:S(2)}, u32[]{:S(2)}) collective-permute-start(bf16[288,512]{1,0:T(8,128)(2,1)S(1)} %get-tuple-element.57), channel_id=1, source_target_pairs={{0,3},{1,0},{2,1},{3,2},{4,7},{5,4},{6,5},{7,6},{8,11},{9,8},{10,9... | collective-permute-start | bytes 884744 | tf_op jit(solution)/shard_map/ppermute | solution.py:40
  18.0 2.5 %collective-permute-start.4 = (bf16[32,1152]{1,0:T(8,128)(2,1)S(1)}, bf16[32,1152]{1,0:T(8,128)(2,1)S(1)}, u32[]{:S(2)}, u32[]{:S(2)}) collective-permute-start(bf16[32,1152]{1,0:T(8,128)(2,1)S(1)} %get-tuple-element.54), channel_id=1, source_target_pairs={{0,16},{4,132},{8,24},{12,140},{16,0},{20,148},{24,8},{28,156},{32... | collective-permute-start | bytes 221192 | tf_op jit(solution)/shard_map/ppermute | solution.py:52
  21.6 1.7 %collective-permute-done.4.refs_2_ = bf16[32,1152]{1,0:T(8,128)(2,1)S(1)} collective-permute-done((bf16[32,1152]{1,0:T(8,128)(2,1)S(1)}, bf16[32,1152]{1,0:T(8,128)(2,1)S(1)}, u32[]{:S(2)}, u32[]{:S(2)}) %collective-permute-start.4) | collective-permute-done | bytes 73760 | tf_op jit(solution)/shard_map/ppermute | solution.py:52
  25.4 6.0 %collective-permute-start.12 = (bf16[288,256]{1,0:T(8,128)(2,1)S(1)}, bf16[288,256]{1,0:T(8,128)(2,1)S(1)}, u32[]{:S(2)}, u32[]{:S(2)}) collective-permute-start(bf16[288,256]{1,0:T(8,128)(2,1)S(1)} %get-tuple-element.59), channel_id=1, source_target_pairs={{0,2},{1,3},{2,0},{3,1},{4,6},{5,7},{6,4},{7,5},{8,10},{9,11},{10,... | collective-permute-start | bytes 442376 | tf_op jit(solution)/shard_map/ppermute | solution.py:40
  32.5 1.9 %collective-permute-start.10 = (bf16[32,1152]{1,0:T(8,128)(2,1)S(1)}, bf16[32,1152]{1,0:T(8,128)(2,1)S(1)}, u32[]{:S(2)}, u32[]{:S(2)}) collective-permute-start(bf16[32,1152]{1,0:T(8,128)(2,1)S(1)} %shard_map.72.refs_0_), channel_id=1, source_target_pairs={{0,16},{4,132},{8,24},{12,140},{16,0},{20,148},{24,8},{28,156},{32... | collective-permute-start | bytes 221192 | tf_op jit(solution)/shard_map/ppermute | solution.py:52
  35.9 1.7 %collective-permute-done.10.refs_2_ = bf16[32,1152]{1,0:T(8,128)(2,1)S(1)} collective-permute-done((bf16[32,1152]{1,0:T(8,128)(2,1)S(1)}, bf16[32,1152]{1,0:T(8,128)(2,1)S(1)}, u32[]{:S(2)}, u32[]{:S(2)}) %collective-permute-start.10) | collective-permute-done | bytes 73760 | tf_op jit(solution)/shard_map/ppermute | solution.py:52
  37.9 2.3 %collective-permute-done.9.refs_1_ = bf16[32,1152]{1,0:T(8,128)(2,1)S(1)} collective-permute-done((bf16[32,1152]{1,0:T(8,128)(2,1)S(1)}, bf16[32,1152]{1,0:T(8,128)(2,1)S(1)}, u32[]{:S(2)}, u32[]{:S(2)}) %collective-permute-start.9) | collective-permute-done | bytes 73760 | tf_op jit(solution)/shard_map/ppermute | solution.py:52
  40.5 1.8 %collective-permute-start.16 = (bf16[128,1152]{1,0:T(8,128)(2,1)S(1)}, bf16[128,1152]{1,0:T(8,128)(2,1)S(1)}, u32[]{:S(2)}, u32[]{:S(2)}) collective-permute-start(bf16[128,1152]{1,0:T(8,128)(2,1)S(1)} %shard_map.74.refs_0_), channel_id=1, source_target_pairs={{0,128},{4,20},{8,136},{12,28},{16,144},{20,4},{24,152},{28,12},{3... | collective-permute-start | bytes 884744 | tf_op jit(solution)/shard_map/ppermute | solution.py:52
  43.5 3.1 %collective-permute-start.20 = (bf16[288,256]{1,0:T(8,128)(2,1)}, bf16[288,256]{1,0:T(8,128)(2,1)S(1)}, u32[]{:S(2)}, u32[]{:S(2)}) collective-permute-start(bf16[288,256]{1,0:T(8,128)(2,1)} %get-tuple-element.68), channel_id=1, source_target_pairs={{0,2},{1,3},{2,0},{3,1},{4,6},{5,7},{6,4},{7,5},{8,10},{9,11},{10,... | collective-permute-start | bytes 442376 | tf_op jit(solution)/shard_map/ppermute | solution.py:40
  46.7 10.5 %collective-permute-start.13 = (bf16[128,1152]{1,0:T(8,128)(2,1)S(1)}, bf16[128,1152]{1,0:T(8,128)(2,1)S(1)}, u32[]{:S(2)}, u32[]{:S(2)}) collective-permute-start(bf16[128,1152]{1,0:T(8,128)(2,1)S(1)} %shard_map.74.refs_0_), channel_id=1, source_target_pairs={{0,4},{4,0},{1,5},{5,1},{2,6},{6,2},{3,7},{7,3},{8,12},{12,8},{9,1... | collective-permute-start | bytes 884744 | tf_op jit(solution)/shard_map/ppermute | solution.py:40
  59.4 3.0 %shard_map.77 = (f32[16,16,1152]{2,1,0:T(8,128)S(1)}, bf16[16,16,1152]{2,1,0:T(8,128)(2,1)S(1)}, f32[1152,512]{1,0:T(8,128)S(1)}) custom-call(s32[1]{0:T(128)} %bitcast.14.start, f32[1]{0:T(128)} %bitcast.17.multiplier, f32[1]{0:T(128)} %bitcast.19.offset, bf16[128,1152]{1,0:T(8,128)(2,1)S(1)} %shard_map.74.refs_0_, ...), custom_call_target="tpu_custom_call" | custom-call | flops 1811939328 | bytes 8388608 | tf_op jit(solution)/shard_map/pallas_call | solution.py:330
  62.4 2.0 %collective-permute-start.25 = (bf16[16,16,1152]{2,1,0:T(8,128)(2,1)S(1)}, bf16[16,16,1152]{2,1,0:T(8,128)(2,1)S(1)}, u32[]{:S(2)}, u32[]{:S(2)}) collective-permute-start(bf16[16,16,1152]{2,1,0:T(8,128)(2,1)S(1)} %get-tuple-element.83), channel_id=1, source_target_pairs={{0,4},{4,0},{1,5},{5,1},{2,6},{6,2},{3,7},{7,3},{8,12},{12,8},{9,1... | collective-permute-start | bytes 1769480 | tf_op jit(solution)/shard_map/ppermute | solution.py:40
  64.5 2.4 %shard_map.76 = (f32[16,16,1152]{2,1,0:T(8,128)S(1)}, bf16[16,16,1152]{2,1,0:T(8,128)(2,1)S(1)}, bf16[512,512]{1,0:T(8,128)(2,1)S(1)}) custom-call(s32[1]{0:T(128)} %bitcast.13.start, f32[1]{0:T(128)} %bitcast.16.multiplier, f32[1]{0:T(128)} %bitcast.18.offset, bf16[128,1152]{1,0:T(8,128)(2,1)S(1)} %collective-permute-done.13.refs_0_, ...), custom_call_target="tpu_custom_call" | custom-call | flops 1207959552 | bytes 5242880 | tf_op jit(solution)/shard_map/pallas_call | solution.py:338
  71.9 2.6 %collective-permute-start.22 = (bf16[288,512]{1,0:T(8,128)(2,1)S(1)}, bf16[288,512]{1,0:T(8,128)(2,1)S(1)}, u32[]{:S(2)}, u32[]{:S(2)}) collective-permute-start(bf16[288,512]{1,0:T(8,128)(2,1)S(1)} %get-tuple-element.78), channel_id=1, source_target_pairs={{0,1},{1,2},{2,3},{3,0},{4,5},{5,6},{6,7},{7,4},{8,9},{9,10},{10,1... | collective-permute-start | bytes 884744 | tf_op jit(solution)/shard_map/ppermute | solution.py:40
  74.5 1.7 %collective-permute-start.23 = (bf16[288,512]{1,0:T(8,128)(2,1)S(1)}, bf16[288,512]{1,0:T(8,128)(2,1)S(1)}, u32[]{:S(2)}, u32[]{:S(2)}) collective-permute-start(bf16[288,512]{1,0:T(8,128)(2,1)S(1)} %get-tuple-element.79), channel_id=1, source_target_pairs={{0,3},{1,0},{2,1},{3,2},{4,7},{5,4},{6,5},{7,6},{8,11},{9,8},{10,9... | collective-permute-start | bytes 884744 | tf_op jit(solution)/shard_map/ppermute | solution.py:40
  76.2 3.3 %collective-permute-done.26.one = bf16[4,32,1152]{2,1,0:T(8,128)(2,1)S(1)} collective-permute-done((bf16[4,32,1152]{2,1,0:T(8,128)(2,1)S(1)}, bf16[4,32,1152]{2,1,0:T(8,128)(2,1)S(1)}, u32[]{:S(2)}, u32[]{:S(2)}) %collective-permute-start.26) | collective-permute-done | bytes 294944 | tf_op jit(solution)/shard_map/ppermute | solution.py:52
  79.5 6.0 %collective-permute-start.21 = (bf16[288,512]{1,0:T(8,128)(2,1)S(1)}, bf16[288,512]{1,0:T(8,128)(2,1)S(1)}, u32[]{:S(2)}, u32[]{:S(2)}) collective-permute-start(bf16[288,512]{1,0:T(8,128)(2,1)S(1)} %get-tuple-element.76), channel_id=1, source_target_pairs={{0,2},{1,3},{2,0},{3,1},{4,6},{5,7},{6,4},{7,5},{8,10},{9,11},{10,... | collective-permute-start | bytes 884744 | tf_op jit(solution)/shard_map/ppermute | solution.py:40
  88.0 2.5 %collective-permute-done.29.one = bf16[32,1152]{1,0:T(8,128)(2,1)S(1)} collective-permute-done((bf16[32,1152]{1,0:T(8,128)(2,1)S(1)}, bf16[32,1152]{1,0:T(8,128)(2,1)S(1)}, u32[]{:S(2)}, u32[]{:S(2)}) %collective-permute-start.29) | collective-permute-done | bytes 73760 | tf_op jit(solution)/shard_map/ppermute | solution.py:52
  91.5 2.5 %collective-permute-done.31.three = bf16[32,1152]{1,0:T(8,128)(2,1)S(1)} collective-permute-done((bf16[32,1152]{1,0:T(8,128)(2,1)S(1)}, bf16[32,1152]{1,0:T(8,128)(2,1)S(1)}, u32[]{:S(2)}, u32[]{:S(2)}) %collective-permute-start.31) | collective-permute-done | bytes 73760 | tf_op jit(solution)/shard_map/ppermute | solution.py:52
  94.1 7.9 %collective-permute-done.23.three = bf16[288,512]{1,0:T(8,128)(2,1)S(1)} collective-permute-done((bf16[288,512]{1,0:T(8,128)(2,1)S(1)}, bf16[288,512]{1,0:T(8,128)(2,1)S(1)}, u32[]{:S(2)}, u32[]{:S(2)}) %collective-permute-start.23) | collective-permute-done | bytes 294944 | tf_op jit(solution)/shard_map/ppermute | solution.py:40
  (63 shorter events, 23.0 us)
Async XLA Ops:
  3.0 13.6 %collective-permute-start = (bf16[4,32,1152]{2,1,0:T(8,128)(2,1)}, bf16[4,32,1152]{2,1,0:T(8,128)(2,1)S(1)}, u32[]{:S(2)}, u32[]{:S(2)}) collective-permute-start(bf16[4,32,1152]{2,1,0:T(8,128)(2,1)} %get-tuple-element.49), channel_id=1, source_target_pairs={{0,64},{4,12},{8,72},{12,20},{16,80},{20,28},{24,88},{28,4},{32,96... | collective-permute-start | bytes 884744 | tf_op jit(solution)/shard_map/ppermute | solution.py:52
  5.3 11.4 %collective-permute-start.1 = (bf16[4,32,1152]{2,1,0:T(8,128)(2,1)}, bf16[4,32,1152]{2,1,0:T(8,128)(2,1)S(1)}, u32[]{:S(2)}, u32[]{:S(2)}) collective-permute-start(bf16[4,32,1152]{2,1,0:T(8,128)(2,1)} %get-tuple-element.50), channel_id=1, source_target_pairs={{0,128},{4,20},{8,136},{12,28},{16,144},{20,4},{24,152},{28,12},{3... | collective-permute-start | bytes 884744 | tf_op jit(solution)/shard_map/ppermute | solution.py:52
  7.9 8.8 %collective-permute-start.2 = (bf16[4,32,1152]{2,1,0:T(8,128)(2,1)}, bf16[4,32,1152]{2,1,0:T(8,128)(2,1)S(1)}, u32[]{:S(2)}, u32[]{:S(2)}) collective-permute-start(bf16[4,32,1152]{2,1,0:T(8,128)(2,1)} %get-tuple-element.51), channel_id=1, source_target_pairs={{0,192},{4,28},{8,200},{12,4},{16,208},{20,12},{24,216},{28,20},{3... | collective-permute-start | bytes 884744 | tf_op jit(solution)/shard_map/ppermute | solution.py:52
  9.8 21.6 %collective-permute-start.7 = (bf16[288,512]{1,0:T(8,128)(2,1)}, bf16[288,512]{1,0:T(8,128)(2,1)S(1)}, u32[]{:S(2)}, u32[]{:S(2)}) collective-permute-start(bf16[288,512]{1,0:T(8,128)(2,1)} %get-tuple-element.56), channel_id=1, source_target_pairs={{0,1},{1,2},{2,3},{3,0},{4,5},{5,6},{6,7},{7,4},{8,9},{9,10},{10,1... | collective-permute-start | bytes 884744 | tf_op jit(solution)/shard_map/ppermute | solution.py:40
  12.8 18.6 %collective-permute-start.8 = (bf16[288,512]{1,0:T(8,128)(2,1)S(1)}, bf16[288,512]{1,0:T(8,128)(2,1)S(1)}, u32[]{:S(2)}, u32[]{:S(2)}) collective-permute-start(bf16[288,512]{1,0:T(8,128)(2,1)S(1)} %get-tuple-element.57), channel_id=1, source_target_pairs={{0,3},{1,0},{2,1},{3,2},{4,7},{5,4},{6,5},{7,6},{8,11},{9,8},{10,9... | collective-permute-start | bytes 884744 | tf_op jit(solution)/shard_map/ppermute | solution.py:40
  18.0 5.3 %collective-permute-start.4 = (bf16[32,1152]{1,0:T(8,128)(2,1)S(1)}, bf16[32,1152]{1,0:T(8,128)(2,1)S(1)}, u32[]{:S(2)}, u32[]{:S(2)}) collective-permute-start(bf16[32,1152]{1,0:T(8,128)(2,1)S(1)} %get-tuple-element.54), channel_id=1, source_target_pairs={{0,16},{4,132},{8,24},{12,140},{16,0},{20,148},{24,8},{28,156},{32... | collective-permute-start | bytes 221192 | tf_op jit(solution)/shard_map/ppermute | solution.py:52
  24.0 8.4 %collective-permute-start.6 = (bf16[32,1152]{1,0:T(8,128)(2,1)S(1)}, bf16[32,1152]{1,0:T(8,128)(2,1)S(1)}, u32[]{:S(2)}, u32[]{:S(2)}) collective-permute-start(bf16[32,1152]{1,0:T(8,128)(2,1)S(1)} %shard_map.70.here), channel_id=1, source_target_pairs={{0,32},{32,0},{1,33},{33,1},{2,34},{34,2},{3,35},{35,3},{4,36},{36... | collective-permute-start | bytes 221192 | tf_op jit(solution)/shard_map/ppermute | solution.py:40
  25.4 10.4 %collective-permute-start.12 = (bf16[288,256]{1,0:T(8,128)(2,1)S(1)}, bf16[288,256]{1,0:T(8,128)(2,1)S(1)}, u32[]{:S(2)}, u32[]{:S(2)}) collective-permute-start(bf16[288,256]{1,0:T(8,128)(2,1)S(1)} %get-tuple-element.59), channel_id=1, source_target_pairs={{0,2},{1,3},{2,0},{3,1},{4,6},{5,7},{6,4},{7,5},{8,10},{9,11},{10,... | collective-permute-start | bytes 442376 | tf_op jit(solution)/shard_map/ppermute | solution.py:40
  40.2 16.9 %collective-permute-start.14 = (bf16[128,1152]{1,0:T(8,128)(2,1)S(1)}, bf16[128,1152]{1,0:T(8,128)(2,1)S(1)}, u32[]{:S(2)}, u32[]{:S(2)}) collective-permute-start(bf16[128,1152]{1,0:T(8,128)(2,1)S(1)} %shard_map.74.refs_0_), channel_id=1, source_target_pairs={{0,64},{4,12},{8,72},{12,20},{16,80},{20,28},{24,88},{28,4},{32,96... | collective-permute-start | bytes 884744 | tf_op jit(solution)/shard_map/ppermute | solution.py:52
  40.5 16.6 %collective-permute-start.16 = (bf16[128,1152]{1,0:T(8,128)(2,1)S(1)}, bf16[128,1152]{1,0:T(8,128)(2,1)S(1)}, u32[]{:S(2)}, u32[]{:S(2)}) collective-permute-start(bf16[128,1152]{1,0:T(8,128)(2,1)S(1)} %shard_map.74.refs_0_), channel_id=1, source_target_pairs={{0,128},{4,20},{8,136},{12,28},{16,144},{20,4},{24,152},{28,12},{3... | collective-permute-start | bytes 884744 | tf_op jit(solution)/shard_map/ppermute | solution.py:52
  42.3 15.3 %collective-permute-start.18 = (bf16[128,1152]{1,0:T(8,128)(2,1)S(1)}, bf16[128,1152]{1,0:T(8,128)(2,1)S(1)}, u32[]{:S(2)}, u32[]{:S(2)}) collective-permute-start(bf16[128,1152]{1,0:T(8,128)(2,1)S(1)} %shard_map.74.refs_0_), channel_id=1, source_target_pairs={{0,192},{4,28},{8,200},{12,4},{16,208},{20,12},{24,216},{28,20},{3... | collective-permute-start | bytes 884744 | tf_op jit(solution)/shard_map/ppermute | solution.py:52
  43.5 15.6 %collective-permute-start.20 = (bf16[288,256]{1,0:T(8,128)(2,1)}, bf16[288,256]{1,0:T(8,128)(2,1)S(1)}, u32[]{:S(2)}, u32[]{:S(2)}) collective-permute-start(bf16[288,256]{1,0:T(8,128)(2,1)} %get-tuple-element.68), channel_id=1, source_target_pairs={{0,2},{1,3},{2,0},{3,1},{4,6},{5,7},{6,4},{7,5},{8,10},{9,11},{10,... | collective-permute-start | bytes 442376 | tf_op jit(solution)/shard_map/ppermute | solution.py:40
  46.7 17.8 %collective-permute-start.13 = (bf16[128,1152]{1,0:T(8,128)(2,1)S(1)}, bf16[128,1152]{1,0:T(8,128)(2,1)S(1)}, u32[]{:S(2)}, u32[]{:S(2)}) collective-permute-start(bf16[128,1152]{1,0:T(8,128)(2,1)S(1)} %shard_map.74.refs_0_), channel_id=1, source_target_pairs={{0,4},{4,0},{1,5},{5,1},{2,6},{6,2},{3,7},{7,3},{8,12},{12,8},{9,1... | collective-permute-start | bytes 884744 | tf_op jit(solution)/shard_map/ppermute | solution.py:40
  57.2 7.3 %collective-permute-start.15 = (bf16[128,1152]{1,0:T(8,128)(2,1)S(1)}, bf16[128,1152]{1,0:T(8,128)(2,1)S(1)}, u32[]{:S(2)}, u32[]{:S(2)}) collective-permute-start(bf16[128,1152]{1,0:T(8,128)(2,1)S(1)} %collective-permute-done.14.refs_1_), channel_id=1, source_target_pairs={{0,4},{4,0},{1,5},{5,1},{2,6},{6,2},{3,7},{7,3},{8,12},{12,8},{9,1... | collective-permute-start | bytes 884744 | tf_op jit(solution)/shard_map/ppermute | solution.py:40
  57.2 7.3 %collective-permute-start.17 = (bf16[128,1152]{1,0:T(8,128)(2,1)S(1)}, bf16[128,1152]{1,0:T(8,128)(2,1)S(1)}, u32[]{:S(2)}, u32[]{:S(2)}) collective-permute-start(bf16[128,1152]{1,0:T(8,128)(2,1)S(1)} %collective-permute-done.16.refs_2_), channel_id=1, source_target_pairs={{0,4},{4,0},{1,5},{5,1},{2,6},{6,2},{3,7},{7,3},{8,12},{12,8},{9,1... | collective-permute-start | bytes 884744 | tf_op jit(solution)/shard_map/ppermute | solution.py:40
  57.7 6.8 %collective-permute-start.19 = (bf16[128,1152]{1,0:T(8,128)(2,1)S(1)}, bf16[128,1152]{1,0:T(8,128)(2,1)S(1)}, u32[]{:S(2)}, u32[]{:S(2)}) collective-permute-start(bf16[128,1152]{1,0:T(8,128)(2,1)S(1)} %collective-permute-done.18.refs_3_), channel_id=1, source_target_pairs={{0,4},{4,0},{1,5},{5,1},{2,6},{6,2},{3,7},{7,3},{8,12},{12,8},{9,1... | collective-permute-start | bytes 884744 | tf_op jit(solution)/shard_map/ppermute | solution.py:40
  62.4 5.6 %collective-permute-start.25 = (bf16[16,16,1152]{2,1,0:T(8,128)(2,1)S(1)}, bf16[16,16,1152]{2,1,0:T(8,128)(2,1)S(1)}, u32[]{:S(2)}, u32[]{:S(2)}) collective-permute-start(bf16[16,16,1152]{2,1,0:T(8,128)(2,1)S(1)} %get-tuple-element.83), channel_id=1, source_target_pairs={{0,4},{4,0},{1,5},{5,1},{2,6},{6,2},{3,7},{7,3},{8,12},{12,8},{9,1... | collective-permute-start | bytes 1769480 | tf_op jit(solution)/shard_map/ppermute | solution.py:40
  69.1 10.3 %collective-permute-start.26 = (bf16[4,32,1152]{2,1,0:T(8,128)(2,1)S(1)}, bf16[4,32,1152]{2,1,0:T(8,128)(2,1)S(1)}, u32[]{:S(2)}, u32[]{:S(2)}) collective-permute-start(bf16[4,32,1152]{2,1,0:T(8,128)(2,1)S(1)} %get-tuple-element.85), channel_id=1, source_target_pairs={{0,64},{4,12},{8,72},{12,20},{16,80},{20,28},{24,88},{28,4},{32,96... | collective-permute-start | bytes 884744 | tf_op jit(solution)/shard_map/ppermute | solution.py:52
  69.2 16.2 %collective-permute-start.27 = (bf16[4,32,1152]{2,1,0:T(8,128)(2,1)S(1)}, bf16[4,32,1152]{2,1,0:T(8,128)(2,1)S(1)}, u32[]{:S(2)}, u32[]{:S(2)}) collective-permute-start(bf16[4,32,1152]{2,1,0:T(8,128)(2,1)S(1)} %get-tuple-element.86), channel_id=1, source_target_pairs={{0,128},{4,20},{8,136},{12,28},{16,144},{20,4},{24,152},{28,12},{3... | collective-permute-start | bytes 884744 | tf_op jit(solution)/shard_map/ppermute | solution.py:52
  70.4 15.0 %collective-permute-start.28 = (bf16[4,32,1152]{2,1,0:T(8,128)(2,1)S(1)}, bf16[4,32,1152]{2,1,0:T(8,128)(2,1)S(1)}, u32[]{:S(2)}, u32[]{:S(2)}) collective-permute-start(bf16[4,32,1152]{2,1,0:T(8,128)(2,1)S(1)} %get-tuple-element.87), channel_id=1, source_target_pairs={{0,192},{4,28},{8,200},{12,4},{16,208},{20,12},{24,216},{28,20},{3... | collective-permute-start | bytes 884744 | tf_op jit(solution)/shard_map/ppermute | solution.py:52
  71.9 22.2 %collective-permute-start.22 = (bf16[288,512]{1,0:T(8,128)(2,1)S(1)}, bf16[288,512]{1,0:T(8,128)(2,1)S(1)}, u32[]{:S(2)}, u32[]{:S(2)}) collective-permute-start(bf16[288,512]{1,0:T(8,128)(2,1)S(1)} %get-tuple-element.78), channel_id=1, source_target_pairs={{0,1},{1,2},{2,3},{3,0},{4,5},{5,6},{6,7},{7,4},{8,9},{9,10},{10,1... | collective-permute-start | bytes 884744 | tf_op jit(solution)/shard_map/ppermute | solution.py:40
  74.5 27.6 %collective-permute-start.23 = (bf16[288,512]{1,0:T(8,128)(2,1)S(1)}, bf16[288,512]{1,0:T(8,128)(2,1)S(1)}, u32[]{:S(2)}, u32[]{:S(2)}) collective-permute-start(bf16[288,512]{1,0:T(8,128)(2,1)S(1)} %get-tuple-element.79), channel_id=1, source_target_pairs={{0,3},{1,0},{2,1},{3,2},{4,7},{5,4},{6,5},{7,6},{8,11},{9,8},{10,9... | collective-permute-start | bytes 884744 | tf_op jit(solution)/shard_map/ppermute | solution.py:40
  79.5 23.5 %collective-permute-start.21 = (bf16[288,512]{1,0:T(8,128)(2,1)S(1)}, bf16[288,512]{1,0:T(8,128)(2,1)S(1)}, u32[]{:S(2)}, u32[]{:S(2)}) collective-permute-start(bf16[288,512]{1,0:T(8,128)(2,1)S(1)} %get-tuple-element.76), channel_id=1, source_target_pairs={{0,2},{1,3},{2,0},{3,1},{4,6},{5,7},{6,4},{7,5},{8,10},{9,11},{10,... | collective-permute-start | bytes 884744 | tf_op jit(solution)/shard_map/ppermute | solution.py:40
  94.0 9.7 %collective-permute-start.32 = (bf16[2,8,1152]{2,1,0:T(8,128)(2,1)S(1)}, bf16[2,8,1152]{2,1,0:T(8,128)(2,1)S(1)}, u32[]{:S(2)}, u32[]{:S(2)}) collective-permute-start(bf16[2,8,1152]{2,1,0:T(8,128)(2,1)S(1)} %get-tuple-element.93), channel_id=1, source_target_pairs={{0,32},{32,0},{1,33},{33,1},{2,34},{34,2},{3,35},{35,3},{4,36},{36... | collective-permute-start | bytes 110600 | tf_op jit(solution)/shard_map/ppermute | solution.py:40
  (11 other events, 58.8 us)

commit v9 on v8

--- a/solution.py
+++ b/solution.py
@@ -208,25 +208,28 @@
     return lax.dot_general(text[...], weights[...], (((0,), (0,)), ((), ())), preferred_element_type=F32)
 
 
-def own_kernel(start, multiplier, offset, *refs):
-    chunks, (images, keep, send, grad, text, weights) = refs[:4], refs[4:]
-    slab_weights(0, start, multiplier, offset, chunks, images, text, weights)
-    slab_terms(0, images, weights, keep, send)
+def terms_kernel(other, start, multiplier, offset, *refs):
+    chunks, (images, keep, send, weights, text) = refs[:4], refs[4:]
+    slab_weights(other, start, multiplier, offset, chunks, images, text, weights)
+    slab_terms(other, images, weights, keep, send)
+
+
+def own_kernel(*refs):
+    terms_kernel(0, *refs)
+
+
+def other_kernel(*refs):
+    terms_kernel(1, *refs)
+
+
+def pieces_kernel(*refs):
+    chunks, square, pieces, (text, weights, grad) = refs[:8], refs[8:10], refs[10:14], refs[14:]
+    for d, chunk in enumerate(chunks):
+        text[CHUNK * d : CHUNK * d + CHUNK, :] = chunk[...]
+    for slab in range(2):
+        weights[ROWS * slab : ROWS * slab + ROWS, :] = square[slab][...]
+    mine = lax.axis_index("t")
     grad[...] = turned_product(text, weights)
-
-
-def other_kernel(start, multiplier, offset, *refs):
-    chunks, (images, keep, send, weights, text) = refs[:4], refs[4:]
-    slab_weights(1, start, multiplier, offset, chunks, images, text, weights)
-    slab_terms(1, images, weights, keep, send)
-
-
-def pieces_kernel(*refs):
-    chunks, (weights, before), pieces, (text, grad) = refs[:4], refs[4:6], refs[6:10], refs[10:]
-    for d in range(4):
-        text[CHUNK * d : CHUNK * d + CHUNK, :] = chunks[d][...]
-    mine = lax.axis_index("t")
-    grad[...] = before[...] + turned_product(text, weights)
     for d, piece in enumerate(pieces):
         piece[...] = grad[window(ahead(mine, d), PART), :].astype(BF16)
 
@@ -327,30 +330,20 @@
 
     text_scratch = pltpu.VMEM((ROWS, D), BF16)
     kept, sent, square = like(*OWNED, dtype=F32), like(*OWNED), like(ROWS, ROWS)
-    keep_own, send_own, grad = call(
-        own_kernel,
-        [kept, sent, like(D, ROWS, dtype=F32)],
-        scalar_specs + [VMEM] * 5,
-        [text_scratch, pltpu.VMEM((ROWS, ROWS), BF16)],
-        products=3,
-        moved=8,
+    keep_own, send_own, own_weights = call(
+        own_kernel, [kept, sent, square], scalar_specs + [VMEM] * 5, [text_scratch], products=3, moved=8
     )(*scalars, *own, images)
     keep_other, send_other, weights = call(
-        other_kernel,
-        [kept, sent, square],
-        scalar_specs + [VMEM] * 5,
-        [text_scratch],
-        products=2,
-        moved=5,
+        other_kernel, [kept, sent, square], scalar_specs + [VMEM] * 5, [text_scratch], products=2, moved=5
     )(*scalars, *theirs, images)
     pieces = call(
         pieces_kernel,
         [like(PART, ROWS)] * PEERS,
-        [VMEM] * 6,
-        [text_scratch, pltpu.VMEM((D, ROWS), F32)],
+        [VMEM] * 10,
+        [pltpu.VMEM((2 * ROWS, D), BF16), pltpu.VMEM((2 * ROWS, ROWS), BF16), pltpu.VMEM((D, ROWS), F32)],
         products=1,
         moved=5,
-    )(*theirs, weights, grad)
+    )(*own, *theirs, own_weights, weights)
     *pieces, keep_own = lax.optimization_barrier((*pieces, keep_own))
     returned = [pieces[0]] + [shift(pieces[d], "t", d, PEERS) for d in (1, 2, 3)]
 

time: 106 us -> 106 us (level)
  starting transfers between devices: 62.1 us -> 63.9 us
  waiting for transfers between devices: 25.8 us -> 24.3 us
    ppermute x18, waiting for transfers between devices: 15.9 us -> 14.5 us  [along(): return lax.ppermute(value, DP, pairs)]
    ppermute x15, starting transfers between devices: 39.6 us -> 41 us  [shift(): lax.ppermute(value, axis, [(i, (i + by) % size) for i in range(size)])]
  transfers between devices with their start and end apart: 33 -> 33, of which waited for: 12 -> 10; matrix products, arithmetic and copies ran while one was open for 0% -> 0% of each run, Pallas kernels for 10% -> 10%
where the time goes in v9:
time: 106 us; the launch traced here: 105 us
  starting transfers between devices  63.9 us (60%)
  waiting for transfers between devices  24.3 us (23%)
  Pallas kernels  13.1 us (12%)
  between operations  2.85 us (3%)
    ppermute x15, starting transfers between devices, shift(): lax.ppermute(value, axis, [(i, (i + by) % size) for i in range(size)])  41 us
    ppermute x18, starting transfers between devices, along(): return lax.ppermute(value, DP, pairs)  22.9 us
    ppermute x18, waiting for transfers between devices, along(): return lax.ppermute(value, DP, pairs)  14.5 us
    ppermute x15, waiting for transfers between devices, shift(): lax.ppermute(value, axis, [(i, (i + by) % size) for i in range(size)])  9.88 us
    pallas_call x1, Pallas kernels, per_device(): call(cut_text_kernel, [like(4, PIECE, D)] * 4, [HBM], [DMA((4,))], moved=...  2.39 us
    pallas_call x1, Pallas kernels, per_device(): call(other_kernel, [kept, sent, square], scalar_specs + [VMEM] * 5, [text...  2.37 us
    pallas_call x1, Pallas kernels, per_device(): call(own_kernel, [kept, sent, square], scalar_specs + [VMEM] * 5, [text_s...  2.36 us
  transfers between devices with their start and end apart: 33, of which 10 were waited for; matrix products, arithmetic and copies ran while one was open for 0% of the time, Pallas kernels for 10%

profile of v9, /device:TPU:1, one launch (start us, length us, event | category | flops | bytes accessed | tf_op | source)
XLA Modules:
  0.0 104.9 jit_solution(15705723226290615912)
XLA Ops:
  0.6 2.4 %shard_map.68 = (bf16[4,32,1152]{2,1,0:T(8,128)(2,1)}, bf16[4,32,1152]{2,1,0:T(8,128)(2,1)}, bf16[4,32,1152]{2,1,0:T(8,128)(2,1)}, bf16[4,32,1152]{2,1,0:T(8,128)(2,1)}) custom-call(bf16[4,4,32,1152]{3,2,1,0:T(8,128)(2,1)} %bitcast.23), custom_call_target="tpu_custom_call" | custom-call | bytes 2097152 | tf_op jit(solution)/shard_map/pallas_call | solution.py:310
  3.0 2.2 %collective-permute-start = (bf16[4,32,1152]{2,1,0:T(8,128)(2,1)}, bf16[4,32,1152]{2,1,0:T(8,128)(2,1)S(1)}, u32[]{:S(2)}, u32[]{:S(2)}) collective-permute-start(bf16[4,32,1152]{2,1,0:T(8,128)(2,1)} %get-tuple-element.49), channel_id=1, source_target_pairs={{0,64},{4,12},{8,72},{12,20},{16,80},{20,28},{24,88},{28,4},{32,96... | collective-permute-start | bytes 884744 | tf_op jit(solution)/shard_map/ppermute | solution.py:52
  5.3 2.6 %collective-permute-start.1 = (bf16[4,32,1152]{2,1,0:T(8,128)(2,1)}, bf16[4,32,1152]{2,1,0:T(8,128)(2,1)S(1)}, u32[]{:S(2)}, u32[]{:S(2)}) collective-permute-start(bf16[4,32,1152]{2,1,0:T(8,128)(2,1)} %get-tuple-element.50), channel_id=1, source_target_pairs={{0,128},{4,20},{8,136},{12,28},{16,144},{20,4},{24,152},{28,12},{3... | collective-permute-start | bytes 884744 | tf_op jit(solution)/shard_map/ppermute | solution.py:52
  9.9 3.1 %collective-permute-start.7 = (bf16[288,512]{1,0:T(8,128)(2,1)}, bf16[288,512]{1,0:T(8,128)(2,1)S(1)}, u32[]{:S(2)}, u32[]{:S(2)}) collective-permute-start(bf16[288,512]{1,0:T(8,128)(2,1)} %get-tuple-element.56), channel_id=1, source_target_pairs={{0,1},{1,2},{2,3},{3,0},{4,5},{5,6},{6,7},{7,4},{8,9},{9,10},{10,1... | collective-permute-start | bytes 884744 | tf_op jit(solution)/shard_map/ppermute | solution.py:40
  13.0 3.1 %collective-permute-start.8 = (bf16[288,512]{1,0:T(8,128)(2,1)}, bf16[288,512]{1,0:T(8,128)(2,1)S(1)}, u32[]{:S(2)}, u32[]{:S(2)}) collective-permute-start(bf16[288,512]{1,0:T(8,128)(2,1)} %get-tuple-element.57), channel_id=1, source_target_pairs={{0,3},{1,0},{2,1},{3,2},{4,7},{5,4},{6,5},{7,6},{8,11},{9,8},{10,9... | collective-permute-start | bytes 884744 | tf_op jit(solution)/shard_map/ppermute | solution.py:40
  18.1 2.5 %collective-permute-start.4 = (bf16[32,1152]{1,0:T(8,128)(2,1)S(1)}, bf16[32,1152]{1,0:T(8,128)(2,1)S(1)}, u32[]{:S(2)}, u32[]{:S(2)}) collective-permute-start(bf16[32,1152]{1,0:T(8,128)(2,1)S(1)} %get-tuple-element.54), channel_id=1, source_target_pairs={{0,16},{4,132},{8,24},{12,140},{16,0},{20,148},{24,8},{28,156},{32... | collective-permute-start | bytes 221192 | tf_op jit(solution)/shard_map/ppermute | solution.py:52
  21.7 1.7 %collective-permute-done.4.refs_2_ = bf16[32,1152]{1,0:T(8,128)(2,1)S(1)} collective-permute-done((bf16[32,1152]{1,0:T(8,128)(2,1)S(1)}, bf16[32,1152]{1,0:T(8,128)(2,1)S(1)}, u32[]{:S(2)}, u32[]{:S(2)}) %collective-permute-start.4) | collective-permute-done | bytes 73760 | tf_op jit(solution)/shard_map/ppermute | solution.py:52
  25.6 5.8 %collective-permute-start.12 = (bf16[288,256]{1,0:T(8,128)(2,1)S(1)}, bf16[288,256]{1,0:T(8,128)(2,1)S(1)}, u32[]{:S(2)}, u32[]{:S(2)}) collective-permute-start(bf16[288,256]{1,0:T(8,128)(2,1)S(1)} %get-tuple-element.59), channel_id=1, source_target_pairs={{0,2},{1,3},{2,0},{3,1},{4,6},{5,7},{6,4},{7,5},{8,10},{9,11},{10,... | collective-permute-start | bytes 442376 | tf_op jit(solution)/shard_map/ppermute | solution.py:40
  36.6 2.7 %collective-permute-done.10.refs_2_ = bf16[32,1152]{1,0:T(8,128)(2,1)S(1)} collective-permute-done((bf16[32,1152]{1,0:T(8,128)(2,1)S(1)}, bf16[32,1152]{1,0:T(8,128)(2,1)S(1)}, u32[]{:S(2)}, u32[]{:S(2)}) %collective-permute-start.10) | collective-permute-done | bytes 73760 | tf_op jit(solution)/shard_map/ppermute | solution.py:52
  42.8 3.3 %collective-permute-start.20 = (bf16[288,256]{1,0:T(8,128)(2,1)}, bf16[288,256]{1,0:T(8,128)(2,1)S(1)}, u32[]{:S(2)}, u32[]{:S(2)}) collective-permute-start(bf16[288,256]{1,0:T(8,128)(2,1)} %get-tuple-element.68), channel_id=1, source_target_pairs={{0,2},{1,3},{2,0},{3,1},{4,6},{5,7},{6,4},{7,5},{8,10},{9,11},{10,... | collective-permute-start | bytes 442376 | tf_op jit(solution)/shard_map/ppermute | solution.py:40
  46.0 9.4 %collective-permute-start.16 = (bf16[128,1152]{1,0:T(8,128)(2,1)S(1)}, bf16[128,1152]{1,0:T(8,128)(2,1)S(1)}, u32[]{:S(2)}, u32[]{:S(2)}) collective-permute-start(bf16[128,1152]{1,0:T(8,128)(2,1)S(1)} %shard_map.74.refs_3_.refs_0_), channel_id=1, source_target_pairs={{0,4},{4,0},{1,5},{5,1},{2,6},{6,2},{3,7},{7,3},{8,12},{12,8},{9,1... | collective-permute-start | bytes 884744 | tf_op jit(solution)/shard_map/ppermute | solution.py:40
  55.9 2.2 %collective-permute-start.17 = (bf16[128,1152]{1,0:T(8,128)(2,1)S(1)}, bf16[128,1152]{1,0:T(8,128)(2,1)S(1)}, u32[]{:S(2)}, u32[]{:S(2)}) collective-permute-start(bf16[128,1152]{1,0:T(8,128)(2,1)S(1)} %collective-permute-done.13.refs_4_.refs_1_), channel_id=1, source_target_pairs={{0,4},{4,0},{1,5},{5,1},{2,6},{6,2},{3,7},{7,3},{8,12},{12,8},{9,1... | collective-permute-start | bytes 884744 | tf_op jit(solution)/shard_map/ppermute | solution.py:40
  59.7 2.4 %shard_map.76 = (f32[16,16,1152]{2,1,0:T(8,128)S(1)}, bf16[16,16,1152]{2,1,0:T(8,128)(2,1)S(1)}, bf16[512,512]{1,0:T(8,128)(2,1)S(1)}) custom-call(s32[1]{0:T(128)} %bitcast.13.refs_0_, f32[1]{0:T(128)} %bitcast.16.refs_1_, f32[1]{0:T(128)} %bitcast.18.refs_2_, bf16[128,1152]{1,0:T(8,128)(2,1)S(1)} %shard_map.74.refs_3_.refs_0_, ...), custom_call_target="tpu_custom_call" | custom-call | flops 1811939328 | bytes 8388608 | tf_op jit(solution)/shard_map/pallas_call | solution.py:333
  62.2 2.4 %shard_map.77 = (f32[16,16,1152]{2,1,0:T(8,128)S(1)}, bf16[16,16,1152]{2,1,0:T(8,128)(2,1)S(1)}, bf16[512,512]{1,0:T(8,128)(2,1)S(1)}) custom-call(s32[1]{0:T(128)} %bitcast.14.refs_0_, f32[1]{0:T(128)} %bitcast.17.refs_1_, f32[1]{0:T(128)} %bitcast.19.refs_2_, bf16[128,1152]{1,0:T(8,128)(2,1)S(1)} %collective-permute-done.16.refs_3_.refs_4_, ...), custom_call_target="tpu_custom_call" | custom-call | flops 1207959552 | bytes 5242880 | tf_op jit(solution)/shard_map/pallas_call | solution.py:336
  65.1 1.6 %shard_map.78 = (bf16[288,512]{1,0:T(8,128)(2,1)S(1)}, bf16[288,512]{1,0:T(8,128)(2,1)S(1)}, bf16[288,512]{1,0:T(8,128)(2,1)S(1)}, bf16[288,512]{1,0:T(8,128)(2,1)S(1)}) custom-call(bf16[128,1152]{1,0:T(8,128)(2,1)S(1)} %shard_map.74.refs_3_.refs_0_, bf16[128,1152]{1,0:T(8,128)(2,1)S(1)} %collective-permute-done.13.refs_4_.refs_1_, ...), custom_call_target="tpu_custom_call" | custom-call | flops 603979776 | bytes 5242880 | tf_op jit(solution)/shard_map/pallas_call | solution.py:339
  67.8 2.6 %collective-permute-start.27 = (bf16[4,32,1152]{2,1,0:T(8,128)(2,1)S(1)}, bf16[4,32,1152]{2,1,0:T(8,128)(2,1)S(1)}, u32[]{:S(2)}, u32[]{:S(2)}) collective-permute-start(bf16[4,32,1152]{2,1,0:T(8,128)(2,1)S(1)} %get-tuple-element.86), channel_id=1, source_target_pairs={{0,128},{4,20},{8,136},{12,28},{16,144},{20,4},{24,152},{28,12},{3... | collective-permute-start | bytes 884744 | tf_op jit(solution)/shard_map/ppermute | solution.py:52
  70.4 2.0 %collective-permute-start.28 = (bf16[4,32,1152]{2,1,0:T(8,128)(2,1)S(1)}, bf16[4,32,1152]{2,1,0:T(8,128)(2,1)S(1)}, u32[]{:S(2)}, u32[]{:S(2)}) collective-permute-start(bf16[4,32,1152]{2,1,0:T(8,128)(2,1)S(1)} %get-tuple-element.87), channel_id=1, source_target_pairs={{0,192},{4,28},{8,200},{12,4},{16,208},{20,12},{24,216},{28,20},{3... | collective-permute-start | bytes 884744 | tf_op jit(solution)/shard_map/ppermute | solution.py:52
  73.0 3.9 %collective-permute-start.23 = (bf16[288,512]{1,0:T(8,128)(2,1)S(1)}, bf16[288,512]{1,0:T(8,128)(2,1)S(1)}, u32[]{:S(2)}, u32[]{:S(2)}) collective-permute-start(bf16[288,512]{1,0:T(8,128)(2,1)S(1)} %get-tuple-element.79), channel_id=1, source_target_pairs={{0,3},{1,0},{2,1},{3,2},{4,7},{5,4},{6,5},{7,6},{8,11},{9,8},{10,9... | collective-permute-start | bytes 884744 | tf_op jit(solution)/shard_map/ppermute | solution.py:40
  76.9 7.6 %collective-permute-start.21 = (bf16[288,512]{1,0:T(8,128)(2,1)S(1)}, bf16[288,512]{1,0:T(8,128)(2,1)S(1)}, u32[]{:S(2)}, u32[]{:S(2)}) collective-permute-start(bf16[288,512]{1,0:T(8,128)(2,1)S(1)} %get-tuple-element.76), channel_id=1, source_target_pairs={{0,2},{1,3},{2,0},{3,1},{4,6},{5,7},{6,4},{7,5},{8,10},{9,11},{10,... | collective-permute-start | bytes 884744 | tf_op jit(solution)/shard_map/ppermute | solution.py:40
  84.9 1.7 %collective-permute-start.30 = (bf16[32,1152]{1,0:T(8,128)(2,1)S(1)}, bf16[32,1152]{1,0:T(8,128)(2,1)S(1)}, u32[]{:S(2)}, u32[]{:S(2)}) collective-permute-start(bf16[32,1152]{1,0:T(8,128)(2,1)S(1)} %get-tuple-element.90), channel_id=1, source_target_pairs={{0,16},{4,132},{8,24},{12,140},{16,0},{20,148},{24,8},{28,156},{32... | collective-permute-start | bytes 221192 | tf_op jit(solution)/shard_map/ppermute | solution.py:52
  86.5 3.8 %collective-permute-done.29.one = bf16[32,1152]{1,0:T(8,128)(2,1)S(1)} collective-permute-done((bf16[32,1152]{1,0:T(8,128)(2,1)S(1)}, bf16[32,1152]{1,0:T(8,128)(2,1)S(1)}, u32[]{:S(2)}, u32[]{:S(2)}) %collective-permute-start.29) | collective-permute-done | bytes 73760 | tf_op jit(solution)/shard_map/ppermute | solution.py:52
  90.4 3.5 %collective-permute-done.31.three = bf16[32,1152]{1,0:T(8,128)(2,1)S(1)} collective-permute-done((bf16[32,1152]{1,0:T(8,128)(2,1)S(1)}, bf16[32,1152]{1,0:T(8,128)(2,1)S(1)}, u32[]{:S(2)}, u32[]{:S(2)}) %collective-permute-start.31) | collective-permute-done | bytes 73760 | tf_op jit(solution)/shard_map/ppermute | solution.py:52
  95.0 4.0 %collective-permute-done.21.two = bf16[288,512]{1,0:T(8,128)(2,1)S(1)} collective-permute-done((bf16[288,512]{1,0:T(8,128)(2,1)S(1)}, bf16[288,512]{1,0:T(8,128)(2,1)S(1)}, u32[]{:S(2)}, u32[]{:S(2)}) %collective-permute-start.21) | collective-permute-done | bytes 294944 | tf_op jit(solution)/shard_map/ppermute | solution.py:40
  99.7 4.5 %collective-permute-done.32 = bf16[2,8,1152]{2,1,0:T(8,128)(2,1)S(1)} collective-permute-done((bf16[2,8,1152]{2,1,0:T(8,128)(2,1)S(1)}, bf16[2,8,1152]{2,1,0:T(8,128)(2,1)S(1)}, u32[]{:S(2)}, u32[]{:S(2)}) %collective-permute-start.32) | collective-permute-done | bytes 36896 | tf_op jit(solution)/shard_map/ppermute | solution.py:40
  (63 shorter events, 21.3 us)
Async XLA Ops:
  3.0 13.7 %collective-permute-start = (bf16[4,32,1152]{2,1,0:T(8,128)(2,1)}, bf16[4,32,1152]{2,1,0:T(8,128)(2,1)S(1)}, u32[]{:S(2)}, u32[]{:S(2)}) collective-permute-start(bf16[4,32,1152]{2,1,0:T(8,128)(2,1)} %get-tuple-element.49), channel_id=1, source_target_pairs={{0,64},{4,12},{8,72},{12,20},{16,80},{20,28},{24,88},{28,4},{32,96... | collective-permute-start | bytes 884744 | tf_op jit(solution)/shard_map/ppermute | solution.py:52
  5.3 11.5 %collective-permute-start.1 = (bf16[4,32,1152]{2,1,0:T(8,128)(2,1)}, bf16[4,32,1152]{2,1,0:T(8,128)(2,1)S(1)}, u32[]{:S(2)}, u32[]{:S(2)}) collective-permute-start(bf16[4,32,1152]{2,1,0:T(8,128)(2,1)} %get-tuple-element.50), channel_id=1, source_target_pairs={{0,128},{4,20},{8,136},{12,28},{16,144},{20,4},{24,152},{28,12},{3... | collective-permute-start | bytes 884744 | tf_op jit(solution)/shard_map/ppermute | solution.py:52
  7.9 8.9 %collective-permute-start.2 = (bf16[4,32,1152]{2,1,0:T(8,128)(2,1)}, bf16[4,32,1152]{2,1,0:T(8,128)(2,1)S(1)}, u32[]{:S(2)}, u32[]{:S(2)}) collective-permute-start(bf16[4,32,1152]{2,1,0:T(8,128)(2,1)} %get-tuple-element.51), channel_id=1, source_target_pairs={{0,192},{4,28},{8,200},{12,4},{16,208},{20,12},{24,216},{28,20},{3... | collective-permute-start | bytes 884744 | tf_op jit(solution)/shard_map/ppermute | solution.py:52
  9.9 21.5 %collective-permute-start.7 = (bf16[288,512]{1,0:T(8,128)(2,1)}, bf16[288,512]{1,0:T(8,128)(2,1)S(1)}, u32[]{:S(2)}, u32[]{:S(2)}) collective-permute-start(bf16[288,512]{1,0:T(8,128)(2,1)} %get-tuple-element.56), channel_id=1, source_target_pairs={{0,1},{1,2},{2,3},{3,0},{4,5},{5,6},{6,7},{7,4},{8,9},{9,10},{10,1... | collective-permute-start | bytes 884744 | tf_op jit(solution)/shard_map/ppermute | solution.py:40
  13.0 18.4 %collective-permute-start.8 = (bf16[288,512]{1,0:T(8,128)(2,1)}, bf16[288,512]{1,0:T(8,128)(2,1)S(1)}, u32[]{:S(2)}, u32[]{:S(2)}) collective-permute-start(bf16[288,512]{1,0:T(8,128)(2,1)} %get-tuple-element.57), channel_id=1, source_target_pairs={{0,3},{1,0},{2,1},{3,2},{4,7},{5,4},{6,5},{7,6},{8,11},{9,8},{10,9... | collective-permute-start | bytes 884744 | tf_op jit(solution)/shard_map/ppermute | solution.py:40
  24.1 8.6 %collective-permute-start.6 = (bf16[32,1152]{1,0:T(8,128)(2,1)S(1)}, bf16[32,1152]{1,0:T(8,128)(2,1)S(1)}, u32[]{:S(2)}, u32[]{:S(2)}) collective-permute-start(bf16[32,1152]{1,0:T(8,128)(2,1)S(1)} %shard_map.70.here), channel_id=1, source_target_pairs={{0,32},{32,0},{1,33},{33,1},{2,34},{34,2},{3,35},{35,3},{4,36},{36... | collective-permute-start | bytes 221192 | tf_op jit(solution)/shard_map/ppermute | solution.py:40
  25.6 9.6 %collective-permute-start.12 = (bf16[288,256]{1,0:T(8,128)(2,1)S(1)}, bf16[288,256]{1,0:T(8,128)(2,1)S(1)}, u32[]{:S(2)}, u32[]{:S(2)}) collective-permute-start(bf16[288,256]{1,0:T(8,128)(2,1)S(1)} %get-tuple-element.59), channel_id=1, source_target_pairs={{0,2},{1,3},{2,0},{3,1},{4,6},{5,7},{6,4},{7,5},{8,10},{9,11},{10,... | collective-permute-start | bytes 442376 | tf_op jit(solution)/shard_map/ppermute | solution.py:40
  40.0 15.4 %collective-permute-start.15 = (bf16[128,1152]{1,0:T(8,128)(2,1)S(1)}, bf16[128,1152]{1,0:T(8,128)(2,1)S(1)}, u32[]{:S(2)}, u32[]{:S(2)}) collective-permute-start(bf16[128,1152]{1,0:T(8,128)(2,1)S(1)} %shard_map.74.refs_3_.refs_0_), channel_id=1, source_target_pairs={{0,192},{4,28},{8,200},{12,4},{16,208},{20,12},{24,216},{28,20},{3... | collective-permute-start | bytes 884744 | tf_op jit(solution)/shard_map/ppermute | solution.py:52
  41.3 14.0 %collective-permute-start.14 = (bf16[128,1152]{1,0:T(8,128)(2,1)S(1)}, bf16[128,1152]{1,0:T(8,128)(2,1)S(1)}, u32[]{:S(2)}, u32[]{:S(2)}) collective-permute-start(bf16[128,1152]{1,0:T(8,128)(2,1)S(1)} %shard_map.74.refs_3_.refs_0_), channel_id=1, source_target_pairs={{0,128},{4,20},{8,136},{12,28},{16,144},{20,4},{24,152},{28,12},{3... | collective-permute-start | bytes 884744 | tf_op jit(solution)/shard_map/ppermute | solution.py:52
  42.8 13.1 %collective-permute-start.13 = (bf16[128,1152]{1,0:T(8,128)(2,1)S(1)}, bf16[128,1152]{1,0:T(8,128)(2,1)S(1)}, u32[]{:S(2)}, u32[]{:S(2)}) collective-permute-start(bf16[128,1152]{1,0:T(8,128)(2,1)S(1)} %shard_map.74.refs_3_.refs_0_), channel_id=1, source_target_pairs={{0,64},{4,12},{8,72},{12,20},{16,80},{20,28},{24,88},{28,4},{32,96... | collective-permute-start | bytes 884744 | tf_op jit(solution)/shard_map/ppermute | solution.py:52
  42.8 16.6 %collective-permute-start.20 = (bf16[288,256]{1,0:T(8,128)(2,1)}, bf16[288,256]{1,0:T(8,128)(2,1)S(1)}, u32[]{:S(2)}, u32[]{:S(2)}) collective-permute-start(bf16[288,256]{1,0:T(8,128)(2,1)} %get-tuple-element.68), channel_id=1, source_target_pairs={{0,2},{1,3},{2,0},{3,1},{4,6},{5,7},{6,4},{7,5},{8,10},{9,11},{10,... | collective-permute-start | bytes 442376 | tf_op jit(solution)/shard_map/ppermute | solution.py:40
  46.0 16.2 %collective-permute-start.16 = (bf16[128,1152]{1,0:T(8,128)(2,1)S(1)}, bf16[128,1152]{1,0:T(8,128)(2,1)S(1)}, u32[]{:S(2)}, u32[]{:S(2)}) collective-permute-start(bf16[128,1152]{1,0:T(8,128)(2,1)S(1)} %shard_map.74.refs_3_.refs_0_), channel_id=1, source_target_pairs={{0,4},{4,0},{1,5},{5,1},{2,6},{6,2},{3,7},{7,3},{8,12},{12,8},{9,1... | collective-permute-start | bytes 884744 | tf_op jit(solution)/shard_map/ppermute | solution.py:40
  55.4 6.8 %collective-permute-start.19 = (bf16[128,1152]{1,0:T(8,128)(2,1)S(1)}, bf16[128,1152]{1,0:T(8,128)(2,1)S(1)}, u32[]{:S(2)}, u32[]{:S(2)}) collective-permute-start(bf16[128,1152]{1,0:T(8,128)(2,1)S(1)} %collective-permute-done.15.refs_6_.refs_3_), channel_id=1, source_target_pairs={{0,4},{4,0},{1,5},{5,1},{2,6},{6,2},{3,7},{7,3},{8,12},{12,8},{9,1... | collective-permute-start | bytes 884744 | tf_op jit(solution)/shard_map/ppermute | solution.py:40
  55.4 6.8 %collective-permute-start.18 = (bf16[128,1152]{1,0:T(8,128)(2,1)S(1)}, bf16[128,1152]{1,0:T(8,128)(2,1)S(1)}, u32[]{:S(2)}, u32[]{:S(2)}) collective-permute-start(bf16[128,1152]{1,0:T(8,128)(2,1)S(1)} %collective-permute-done.14.refs_5_.refs_2_), channel_id=1, source_target_pairs={{0,4},{4,0},{1,5},{5,1},{2,6},{6,2},{3,7},{7,3},{8,12},{12,8},{9,1... | collective-permute-start | bytes 884744 | tf_op jit(solution)/shard_map/ppermute | solution.py:40
  55.9 6.3 %collective-permute-start.17 = (bf16[128,1152]{1,0:T(8,128)(2,1)S(1)}, bf16[128,1152]{1,0:T(8,128)(2,1)S(1)}, u32[]{:S(2)}, u32[]{:S(2)}) collective-permute-start(bf16[128,1152]{1,0:T(8,128)(2,1)S(1)} %collective-permute-done.13.refs_4_.refs_1_), channel_id=1, source_target_pairs={{0,4},{4,0},{1,5},{5,1},{2,6},{6,2},{3,7},{7,3},{8,12},{12,8},{9,1... | collective-permute-start | bytes 884744 | tf_op jit(solution)/shard_map/ppermute | solution.py:40
  67.0 9.9 %collective-permute-start.26 = (bf16[4,32,1152]{2,1,0:T(8,128)(2,1)S(1)}, bf16[4,32,1152]{2,1,0:T(8,128)(2,1)S(1)}, u32[]{:S(2)}, u32[]{:S(2)}) collective-permute-start(bf16[4,32,1152]{2,1,0:T(8,128)(2,1)S(1)} %get-tuple-element.85), channel_id=1, source_target_pairs={{0,64},{4,12},{8,72},{12,20},{16,80},{20,28},{24,88},{28,4},{32,96... | collective-permute-start | bytes 884744 | tf_op jit(solution)/shard_map/ppermute | solution.py:52
  67.8 16.7 %collective-permute-start.27 = (bf16[4,32,1152]{2,1,0:T(8,128)(2,1)S(1)}, bf16[4,32,1152]{2,1,0:T(8,128)(2,1)S(1)}, u32[]{:S(2)}, u32[]{:S(2)}) collective-permute-start(bf16[4,32,1152]{2,1,0:T(8,128)(2,1)S(1)} %get-tuple-element.86), channel_id=1, source_target_pairs={{0,128},{4,20},{8,136},{12,28},{16,144},{20,4},{24,152},{28,12},{3... | collective-permute-start | bytes 884744 | tf_op jit(solution)/shard_map/ppermute | solution.py:52
  70.4 14.1 %collective-permute-start.28 = (bf16[4,32,1152]{2,1,0:T(8,128)(2,1)S(1)}, bf16[4,32,1152]{2,1,0:T(8,128)(2,1)S(1)}, u32[]{:S(2)}, u32[]{:S(2)}) collective-permute-start(bf16[4,32,1152]{2,1,0:T(8,128)(2,1)S(1)} %get-tuple-element.87), channel_id=1, source_target_pairs={{0,192},{4,28},{8,200},{12,4},{16,208},{20,12},{24,216},{28,20},{3... | collective-permute-start | bytes 884744 | tf_op jit(solution)/shard_map/ppermute | solution.py:52
  72.4 21.6 %collective-permute-start.22 = (bf16[288,512]{1,0:T(8,128)(2,1)S(1)}, bf16[288,512]{1,0:T(8,128)(2,1)S(1)}, u32[]{:S(2)}, u32[]{:S(2)}) collective-permute-start(bf16[288,512]{1,0:T(8,128)(2,1)S(1)} %get-tuple-element.78), channel_id=1, source_target_pairs={{0,1},{1,2},{2,3},{3,0},{4,5},{5,6},{6,7},{7,4},{8,9},{9,10},{10,1... | collective-permute-start | bytes 884744 | tf_op jit(solution)/shard_map/ppermute | solution.py:40
  73.0 21.0 %collective-permute-start.23 = (bf16[288,512]{1,0:T(8,128)(2,1)S(1)}, bf16[288,512]{1,0:T(8,128)(2,1)S(1)}, u32[]{:S(2)}, u32[]{:S(2)}) collective-permute-start(bf16[288,512]{1,0:T(8,128)(2,1)S(1)} %get-tuple-element.79), channel_id=1, source_target_pairs={{0,3},{1,0},{2,1},{3,2},{4,7},{5,4},{6,5},{7,6},{8,11},{9,8},{10,9... | collective-permute-start | bytes 884744 | tf_op jit(solution)/shard_map/ppermute | solution.py:40
  76.9 22.1 %collective-permute-start.21 = (bf16[288,512]{1,0:T(8,128)(2,1)S(1)}, bf16[288,512]{1,0:T(8,128)(2,1)S(1)}, u32[]{:S(2)}, u32[]{:S(2)}) collective-permute-start(bf16[288,512]{1,0:T(8,128)(2,1)S(1)} %get-tuple-element.76), channel_id=1, source_target_pairs={{0,2},{1,3},{2,0},{3,1},{4,6},{5,7},{6,4},{7,5},{8,10},{9,11},{10,... | collective-permute-start | bytes 884744 | tf_op jit(solution)/shard_map/ppermute | solution.py:40
  84.8 5.6 %collective-permute-start.29 = (bf16[32,1152]{1,0:T(8,128)(2,1)S(1)}, bf16[32,1152]{1,0:T(8,128)(2,1)S(1)}, u32[]{:S(2)}, u32[]{:S(2)}) collective-permute-start(bf16[32,1152]{1,0:T(8,128)(2,1)S(1)} %get-tuple-element.89), channel_id=1, source_target_pairs={{0,8},{4,68},{8,16},{12,76},{16,24},{20,84},{24,0},{28,92},{32,40}... | collective-permute-start | bytes 221192 | tf_op jit(solution)/shard_map/ppermute | solution.py:52
  84.9 5.5 %collective-permute-start.30 = (bf16[32,1152]{1,0:T(8,128)(2,1)S(1)}, bf16[32,1152]{1,0:T(8,128)(2,1)S(1)}, u32[]{:S(2)}, u32[]{:S(2)}) collective-permute-start(bf16[32,1152]{1,0:T(8,128)(2,1)S(1)} %get-tuple-element.90), channel_id=1, source_target_pairs={{0,16},{4,132},{8,24},{12,140},{16,0},{20,148},{24,8},{28,156},{32... | collective-permute-start | bytes 221192 | tf_op jit(solution)/shard_map/ppermute | solution.py:52
  93.9 10.3 %collective-permute-start.32 = (bf16[2,8,1152]{2,1,0:T(8,128)(2,1)S(1)}, bf16[2,8,1152]{2,1,0:T(8,128)(2,1)S(1)}, u32[]{:S(2)}, u32[]{:S(2)}) collective-permute-start(bf16[2,8,1152]{2,1,0:T(8,128)(2,1)S(1)} %get-tuple-element.93), channel_id=1, source_target_pairs={{0,32},{32,0},{1,33},{33,1},{2,34},{34,2},{3,35},{35,3},{4,36},{36... | collective-permute-start | bytes 110600 | tf_op jit(solution)/shard_map/ppermute | solution.py:40
  (11 other events, 59.4 us)
